TPU v7x, 256 devices: a whole 4x4x8 slice. The times are simulated.
256 devices in a mesh: seq: 16 (over x, z_hi, core), fsdp: 16 (over y, z_lo).
Axes of the slice: x: 4, y: 4, z: 8 (z_hi: 2, z_lo: 4; z = z_hi * 4 + z_lo), core: 2. Of those that a mesh axis runs over, the one named last changes fastest.
Arguments:
- queries: bfloat16 [16, 3, 2048, 1536], P('fsdp', None, 'seq'), as said below
- key_rows: bfloat16 [16, 3, 2048, 1536], P('fsdp', None, 'seq'), may hold values from -4 to 4
- value_rows: bfloat16 [16, 3, 2048, 1536], P('fsdp', None, 'seq'), may hold values from -6 to 6
- text_keys: bfloat16 [16, 256, 1536], P('fsdp', 'seq'), may hold values from -6 to 6
- text_values: bfloat16 [16, 256, 1536], P('fsdp', 'seq'), may hold values from -6 to 6
- residual: bfloat16 [16, 3, 2048, 3072], P('fsdp', None, 'seq'), may hold values from -4 to 4
- out_gate: float32 [3072], replicated, may hold values from -6 to 6
- out_weight: bfloat16 [1536, 3072], P(None, 'fsdp'), may hold values from -0.15625 to 0.15625
- out_bias: float32 [3072], replicated, may hold values from -2 to 2
- tile_lists: int32 [16, 3, 16, 27], P('fsdp', None, 'seq'), may hold values from -1 to 47, as said below
Outputs:
- mixed: bfloat16 [16, 3, 2048, 3072], P('fsdp', None, 'seq')
Inputs may be any that keep to these rules, and one draw needn't show every extreme that they name: `tile_lists`: tile s of a clip lies at grid position (t, h, w) with s = (t * 8 + h) * 2 + w, 0 <= t < 3, 0 <= h < 8, 0 <= w < 2. The list of tile s names s itself and some of the other tiles of the same clip whose three grid coordinates each differ from those of s by at most one, each tile at most once, in any order, the remaining entries being -1. `queries`: entries lie within 8 or 240 / sqrt(128) in magnitude, whichever is larger.
All inputs are finite; a program needn't handle non-finite values.
Results may differ from a plain program's by a relative error of at most 0.0053.
Values may be sent and summed in bfloat16 or wider, within the bound.
No kernel may reach another device: no remote copies, remote signals or barrier semaphores. Data moves between devices by JAX's collectives and lax.ppermute only.
A program may use at most 192 MiB of HBM per device.

v0:
```python
import functools

import jax
import jax.numpy as jnp
from jax import lax
from jax.experimental import pallas as pl
from jax.experimental.pallas import tpu as pltpu
from jax.sharding import PartitionSpec as P

HEADS = 12
HD = 128
TILE = 128
GT = 3
ROWS = GT * TILE
HID = HEADS * HD
QUARTER = HID // 4
PANEL = 192
D = 3072
TEXT = 256
GROUPS = (5, 4, 2, 1)
NEG = -1e30
SCALE = HD**-0.5 * 1.4426950408889634
AXES = ("seq", "fsdp")


def place(x, y, z, c):
    return (((x % 4) * 2 + z % 8 // 4) * 2 + c % 2) * 16 + (y % 4) * 4 + z % 4


def shift(value, dx=0, dy=0, dz=0, dc=0):
    pairs = [
        (place(x, y, z, c), place(x + dx, y + dy, z + dz, c + dc))
        for x in range(4)
        for y in range(4)
        for z in range(8)
        for c in range(2)
    ]
    return lax.ppermute(value, AXES, pairs)


def forward(value, flip=0):
    pairs = [(s, ((s + 4) % 16 if s % 4 < 2 else (s - 4) % 16) ^ flip) for s in range(16)]
    return lax.ppermute(value, "seq", pairs)


def swap(value, bit):
    return lax.ppermute(value, "seq", [(s, s ^ bit) for s in range(16)])


def across(value):
    pairs = [(s, (s - 4) % 16 if s % 4 < 2 else (s + 4) % 16) for s in range(16)]
    return lax.ppermute(value, "seq", pairs)


def join_kernel(*refs):
    first = 0
    for ref in refs[:-1]:
        refs[-1][:, first : first + ref.shape[1], :] = ref[...]
        first += ref.shape[1]


def join(*pieces):
    rows = sum(p.shape[1] for p in pieces)
    return pl.pallas_call(
        join_kernel,
        out_shape=jax.ShapeDtypeStruct((2, rows, HID), jnp.bfloat16),
        compiler_params=pltpu.CompilerParams(vmem_limit_bytes=16 * 1024 * 1024),
        cost_estimate=pl.CostEstimate(
            flops=0, bytes_accessed=8 * rows * HID, transcendentals=0
        ),
        name="join",
    )(*pieces)


def merge_kernel(near, far, out):
    out[:2] = near[...]
    out[2:] = far[...]


def merge(near, far):
    return pl.pallas_call(
        merge_kernel,
        grid=(near.shape[2] // HD,),
        out_shape=jax.ShapeDtypeStruct((4,) + near.shape[1:], jnp.bfloat16),
        in_specs=[pl.BlockSpec((2, ROWS, HD), lambda i: (0, 0, i))] * 2,
        out_specs=pl.BlockSpec((4, ROWS, HD), lambda i: (0, 0, i)),
        cost_estimate=pl.CostEstimate(flops=0, bytes_accessed=8 * near.size, transcendentals=0),
        name="merge",
    )(near, far)


def pair_kernel(k, v, out):
    out[0] = k[...]
    out[1] = v[...]


def pair(k, v, first, count, width=HD):
    rows = k.shape[0]
    return pl.pallas_call(
        pair_kernel,
        grid=(count,),
        out_shape=jax.ShapeDtypeStruct((2, rows, count * width), jnp.bfloat16),
        in_specs=[pl.BlockSpec((rows, width), lambda i: (0, first + i))] * 2,
        out_specs=pl.BlockSpec((2, rows, width), lambda i: (0, 0, i)),
        compiler_params=pltpu.CompilerParams(vmem_limit_bytes=16 * 1024 * 1024),
        cost_estimate=pl.CostEstimate(
            flops=0, bytes_accessed=8 * rows * count * width, transcendentals=0
        ),
        name="pair",
    )(k, v)


def place_kernel(where, *refs):
    for n, ref in enumerate(refs[:-1]):
        refs[-1][where[n]] = ref[...]


def place_all(where, *pieces):
    shape = (4,) + pieces[0].shape
    size = 4 * pieces[0].size
    return pl.pallas_call(
        place_kernel,
        out_shape=jax.ShapeDtypeStruct(shape, jnp.bfloat16),
        in_specs=[pl.BlockSpec(memory_space=pltpu.SMEM)]
        + [pl.BlockSpec(memory_space=pltpu.VMEM)] * 4,
        compiler_params=pltpu.CompilerParams(vmem_limit_bytes=16 * 1024 * 1024),
        cost_estimate=pl.CostEstimate(flops=0, bytes_accessed=4 * size, transcendentals=0),
        name="place",
    )(where, *pieces)


def attend_kernel(bias, q, k0, v0, a1, b0, b1, c0, c1, words, out):
    contract = (((1,), (1,)), ((), ()))
    sources = [(k0, v0)] + [(r.at[0], r.at[1]) for r in (a1, b0, b1, c0, c1)]
    for t in range(GT):
        low, high = max(0, t - 1), min(GT, t + 2)
        qt = q[t * TILE : (t + 1) * TILE, :]
        pieces = []
        peak = None
        for n, (k, _) in enumerate(sources):
            s = lax.dot_general(
                qt, k[low * TILE : high * TILE, :], contract, preferred_element_type=jnp.float32
            )
            for j in range(low, high):
                part = s[:, (j - low) * TILE : (j - low + 1) * TILE] * SCALE + bias[t, n * GT + j]
                pieces.append(part)
                peak = part if peak is None else jnp.maximum(peak, part)
        s = lax.dot_general(qt, words[0], contract, preferred_element_type=jnp.float32) * SCALE
        for j in range(TEXT // TILE):
            part = s[:, j * TILE : (j + 1) * TILE]
            pieces.append(part)
            peak = jnp.maximum(peak, part)
        top = jnp.max(peak, axis=1, keepdims=True)
        total = jnp.zeros((TILE, TILE), jnp.float32)
        acc = jnp.zeros((TILE, HD), jnp.float32)
        at = 0
        for n in range(len(sources) + 1):
            if n < len(sources):
                count = high - low
                values = sources[n][1][low * TILE : high * TILE, :]
            else:
                count = TEXT // TILE
                values = words[1]
            weights = []
            for j in range(count):
                e = jnp.exp2(pieces[at + j] - top)
                total = total + e
                weights.append(e.astype(jnp.bfloat16))
            at += count
            acc = acc + jnp.dot(
                jnp.concatenate(weights, axis=1), values, preferred_element_type=jnp.float32
            )
        row = jnp.sum(total, axis=1, keepdims=True)
        out[t * TILE : (t + 1) * TILE, :] = (acc / row).astype(jnp.bfloat16)


def attend(bias, q, k0, v0, beside, near, far, text, first, count, merged=False):
    wide = pl.BlockSpec((ROWS, HD), lambda i: (0, first + i))
    words = pl.BlockSpec((2, TEXT, HD), lambda i: (0, 0, first + i))
    pack = pl.BlockSpec((2, ROWS, HD), lambda i: (0, 0, i))
    upper = pl.BlockSpec((2, ROWS, HD), lambda i: (1, 0, i))
    whole = pl.BlockSpec((2, ROWS, HD), lambda i: (0, 0, first + i))
    units = 48 * count
    return pl.pallas_call(
        attend_kernel,
        grid=(count,),
        out_shape=jax.ShapeDtypeStruct((ROWS, count * HD), jnp.bfloat16),
        in_specs=[pl.BlockSpec(memory_space=pltpu.SMEM)]
        + [wide] * 3
        + [whole]
        + [pack] * 3
        + [upper if merged else pack]
        + [words],
        out_specs=pl.BlockSpec((ROWS, HD), lambda i: (0, i)),
        compiler_params=pltpu.CompilerParams(vmem_limit_bytes=14 * 1024 * 1024),
        cost_estimate=pl.CostEstimate(
            flops=units * TILE * TILE * HD * 16,
            bytes_accessed=count * 2 * HD * (ROWS * 14 + TEXT * 2),
            transcendentals=units * TILE * TILE,
        ),
        name="attend",
    )(bias, q, k0, v0, beside, *near, *far, text)


def project_kernel(*refs):
    parts = refs[: len(GROUPS)]
    order, wa, wb, wc, wd, bias, gate, residual, out, att, mine = refs[
        len(GROUPS) :
    ]
    step = pl.program_id(0)

    @pl.when(step == 0)
    def _():
        head = 0
        for part in parts:
            for n in range(part.shape[1] // HD):
                column = head % 3 * HD
                att[head // 3, :, column : column + HD] = part[:, n * HD : (n + 1) * HD]
                head += 1
        for n in range(4):
            mine[:, n * QUARTER : (n + 1) * QUARTER] = att[order[n]]

    wt = jnp.concatenate([wa[...], wb[...], wc[...], wd[...]], axis=1)
    projected = lax.dot_general(
        mine[...], wt, (((1,), (1,)), ((), ())), preferred_element_type=jnp.float32
    )
    projected = (projected + bias[...]).astype(jnp.bfloat16).astype(jnp.float32)
    out[...] = (residual[...].astype(jnp.float32) + gate[...] * projected).astype(jnp.bfloat16)


def project(parts, order, weights, bias, gate, residual):
    step = 512
    panel = pl.BlockSpec((step, QUARTER), lambda i: (i, 0))
    return pl.pallas_call(
        project_kernel,
        grid=(D // step,),
        out_shape=jax.ShapeDtypeStruct((ROWS, D), jnp.bfloat16),
        in_specs=[pl.BlockSpec(part.shape, lambda i: (0, 0)) for part in parts]
        + [pl.BlockSpec(memory_space=pltpu.SMEM)]
        + [panel] * 4
        + [
            pl.BlockSpec((1, step), lambda i: (0, i)),
            pl.BlockSpec((1, step), lambda i: (0, i)),
            pl.BlockSpec((ROWS, step), lambda i: (0, i)),
        ],
        out_specs=pl.BlockSpec((ROWS, step), lambda i: (0, i)),
        scratch_shapes=[
            pltpu.VMEM((4, ROWS, QUARTER), jnp.bfloat16),
            pltpu.VMEM((ROWS, HID), jnp.bfloat16),
        ],
        compiler_params=pltpu.CompilerParams(vmem_limit_bytes=14 * 1024 * 1024),
        cost_estimate=pl.CostEstimate(
            flops=2 * ROWS * HID * D,
            bytes_accessed=2 * D * HID + 4 * ROWS * D,
            transcendentals=0,
        ),
        name="project",
    )(*parts, order, *weights, bias, gate, residual)


def stage(ready, work, *operands):
    shapes = jax.eval_shape(work, *operands)
    return lax.cond(
        ready,
        work,
        lambda *_: tuple(jnp.zeros(s.shape, s.dtype) for s in shapes),
        *operands,
    )


def local(
    queries,
    key_rows,
    value_rows,
    text_keys,
    text_values,
    residual,
    out_gate,
    out_weight,
    out_bias,
    tile_lists,
):
    seq, fsdp = lax.axis_index("seq"), lax.axis_index("fsdp")
    x, zh, c = seq // 4, seq // 2 % 2, seq % 2
    y, zl = fsdp // 4, fsdp % 4
    q = queries.reshape(ROWS, HID)
    k0, v0 = key_rows.reshape(ROWS, HID), value_rows.reshape(ROWS, HID)

    far_spot = jnp.where(zh == 0, seq - 2, seq + 2)
    spots = jnp.stack(
        [seq, seq ^ 1, seq ^ 2, seq ^ 3, far_spot, far_spot ^ 1]
    )
    inside = (spots >= 0) & (spots < 16)
    candidates = spots[:, None] + 16 * jnp.arange(GT, dtype=jnp.int32)[None, :]
    listed = tile_lists[0, :, 0, :]
    present = jnp.any(listed[:, None, None, :] == candidates[None, :, :, None], axis=3)
    present = present & inside[None, :, None]
    bias = jnp.where(present, 0.0, NEG).astype(jnp.float32).reshape(GT, 6 * GT)

    steps = jnp.array([0, 1, -1, 2], jnp.int32)
    firsts = [sum(GROUPS[:g]) for g in range(len(GROUPS))]
    packs = [pair(k0, v0, first, count) for first, count in zip(firsts, GROUPS)]

    def attend_group(g, near, others, far, text, far_other=None):
        return attend(
            bias,
            q,
            k0,
            v0,
            beside,
            (near, others),
            (far, others if far_other is None else far_other),
            text,
            firsts[g],
            GROUPS[g],
            far_other is None,
        )

    text = pair(text_keys[0], text_values[0], 0, 1, HID)
    piece = lax.dynamic_slice(
        out_weight.T, (0, (x % 2 * 2 + c) * QUARTER), (PANEL, QUARTER)
    )
    text_z = swap(text, 2)
    pack0, keys, values, wz1, wz2, wz3, text_z = lax.optimization_barrier(
        (
            packs[0],
            k0,
            v0,
            shift(piece, dz=1),
            shift(piece, dz=-1),
            shift(piece, dz=2),
            text_z,
        )
    )
    text = join(text, text_z)
    packs, bias, beside, wz1, wz2, wz3, text_x = lax.optimization_barrier(
        (
            packs[1:],
            bias,
            shift(pair(keys, values, 0, HEADS), dc=1),
            wz1,
            wz2,
            wz3,
            swap(text, 4),
        )
    )
    near0 = shift(pack0, dz=4)
    packs = (pack0,) + tuple(packs)
    ready = tile_lists[0, 0, 0, 0] > -2

    def weight_stage(piece, wz1, wz2, wz3, text, text_x):
        text = join(text, text_x)
        text = join(text, swap(text, 8))
        text = join(text, swap(text, 1))
        wz = place_all((zl - steps) % 4, piece, wz1, wz2, wz3)
        wy = place_all(
            (y - steps) % 4, wz, shift(wz, dy=1), shift(wz, dy=-1), shift(wz, dy=2)
        )
        return wy.reshape(D, QUARTER), text

    wy, text = stage(ready, weight_stage, piece, wz1, wz2, wz3, text, text_x)
    pack1, wy = lax.optimization_barrier((packs[1], wy))
    near1 = shift(pack1, dz=4)
    near0, wy = lax.optimization_barrier((near0, wy))
    wx = across(wy)

    def first_stage(near0):
        far0 = forward(near0)
        return far0, shift(near0, dc=1), shift(far0, dc=1)

    far0, near0_other, far0_other = stage(ready, first_stage, near0)

    def second_stage(near1, near0, near0_other, far0, far0_other, text):
        part0 = attend_group(0, near0, near0_other, far0, text, far0_other)
        near1_other = shift(near1, dc=1)
        far1, part0 = lax.optimization_barrier((forward(near1), part0))
        return part0, far1, near1_other, shift(far1, dc=1)

    pack2, near1, far0_other = lax.optimization_barrier((packs[2], near1, far0_other))
    near2 = shift(pack2, dz=4)
    part0, far1, near1_other, far1_other = stage(
        ready, second_stage, near1, near0, near0_other, far0, far0_other, text
    )

    def third_stage(near2, near1, near1_other, far1, far1_other, text, wy, wx):
        part1 = attend_group(1, near1, near1_other, far1, text, far1_other)
        wb, wd = shift(wy, dc=1), shift(wx, dc=1)
        far2, part1 = lax.optimization_barrier((forward(near2), part1))
        return part1, far2, shift(merge(near2, far2), dc=1), wb, wd

    pack3, near2, part0, wx = lax.optimization_barrier((packs[3], near2, part0, wx))
    near3 = shift(pack3, dz=4)
    part1, far2, others2, wb, wd = stage(
        ready,
        third_stage,
        near2,
        near1,
        near1_other,
        far1,
        far1_other,
        text,
        wy,
        wx,
    )
    near3, others2 = lax.optimization_barrier((near3, others2))
    part2 = attend_group(2, near2, others2, far2, text)
    far3, far3_other, near3_other, part2 = lax.optimization_barrier(
        (forward(near3), forward(near3, flip=1), shift(near3, dc=1), part2)
    )
    part3 = attend_group(3, near3, near3_other, far3, text, far3_other)
    parts = [part0, part1, part2, part3]
    own = x % 2 * 2 + c
    order = jnp.stack([own, own ^ 1, own ^ 2, own ^ 3]).astype(jnp.int32)
    weights = [w.reshape(-1, QUARTER) for w in (wy, wb, wx, wd)]
    mixed = project(
        parts,
        order,
        weights,
        out_bias.reshape(1, D),
        out_gate.reshape(1, D),
        residual.reshape(ROWS, D),
    )
    return mixed.reshape(residual.shape)


def solution(mesh):
    placed = (
        P("fsdp", None, "seq", None),
        P("fsdp", None, "seq", None),
        P("fsdp", None, "seq", None),
        P("fsdp", "seq", None),
        P("fsdp", "seq", None),
        P("fsdp", None, "seq", None),
        P(),
        P(None, "fsdp"),
        P(),
        P("fsdp", None, "seq", None),
    )
    return jax.shard_map(
        local, mesh=mesh, in_specs=placed, out_specs=P("fsdp", None, "seq", None), check_vma=False
    )
```

profile of v0, /device:TPU:72, one launch (start us, length us, event | category | flops | bytes accessed | tf_op | source)
XLA Modules:
  0.0 196.6 jit_solution(16864151444240009487)
XLA Ops:
  1.1 4.6 %collective-permute-start.17 = (bf16[192,384]{1,0:T(8,128)(2,1)S(1)}, bf16[192,384]{1,0:T(8,128)(2,1)S(1)}, u32[]{:S(2)}, u32[]{:S(2)}) collective-permute-start(bf16[192,384]{1,0:T(8,128)(2,1)S(1)} %dynamic-slice_bitcast_fusion), channel_id=1, source_target_pairs={{0,2},{16,18},{1,3},{17,19},{2,32},{18,48},{3,33},{19,49},{32,34},... | collective-permute-start | bytes 442376 | tf_op jit(solution)/shard_map/ppermute | solution.py:38
  10.8 3.9 %pair.9 = bf16[2,384,640]{2,1,0:T(8,128)(2,1)} custom-call(bf16[384,1536]{1,0:T(8,128)(2,1)} %bitcast.31, bf16[384,1536]{1,0:T(8,128)(2,1)} %bitcast.40), custom_call_target="tpu_custom_call" | custom-call | bytes 1966080 | tf_op jit(solution)/shard_map/pair/pallas_call | solution.py:99
  14.6 5.3 %collective-permute-done.18.refs_1_ = bf16[2,16,1536]{2,1,0:T(8,128)(2,1)S(1)} collective-permute-done((bf16[2,16,1536]{2,1,0:T(8,128)(2,1)S(1)}, bf16[2,16,1536]{2,1,0:T(8,128)(2,1)S(1)}, u32[]{:S(2)}, u32[]{:S(2)}) %collective-permute-start.18) | collective-permute-done | bytes 98336 | tf_op jit(solution)/shard_map/ppermute | solution.py:47
  21.4 5.8 %collective-permute-start.22 = (bf16[2,384,640]{2,1,0:T(8,128)(2,1)}, bf16[2,384,640]{2,1,0:T(8,128)(2,1)}, u32[]{:S(2)}, u32[]{:S(2)}) collective-permute-start(bf16[2,384,640]{2,1,0:T(8,128)(2,1)} %pair.9), channel_id=1, source_target_pairs={{0,32},{16,48},{1,33},{17,49},{2,34},{18,50},{3,35},{19,51},{32,0}... | collective-permute-start | bytes 2949128 | tf_op jit(solution)/shard_map/ppermute | solution.py:38
  34.2 5.5 %collective-permute-done.20 = bf16[2,32,1536]{2,1,0:T(8,128)(2,1)S(1)} collective-permute-done((bf16[2,32,1536]{2,1,0:T(8,128)(2,1)S(1)}, bf16[2,32,1536]{2,1,0:T(8,128)(2,1)S(1)}, u32[]{:S(2)}, u32[]{:S(2)}) %collective-permute-start.20) | collective-permute-done | bytes 196640 | tf_op jit(solution)/shard_map/ppermute | solution.py:47
  39.7 45.3 %conditional.4 = (bf16[3072,384]{1,0:T(8,128)(2,1)}, bf16[2,256,1536]{2,1,0:T(8,128)(2,1)S(1)}) conditional(s32[]{:T(128)} %bitcast.12, () %tuple.55, (s32[]{:T(128)}, s32[]{:T(128)}, (), bf16[192,384]{1,0:T(8,128)(2,1)}, bf16[192,384]{1,0:T(8,128)(2,1)}, /*index=5*/bf16[192,384]{1,0:T(8,128)(2,1)}, bf16[192,384]{1,0:T(8,128)(2,1)}, ...), branch_computations={%region_1.2_spmd, %region_2.3_spmd} | conditional | flops 115 | bytes 25559704 | solution.py:263
  39.8 3.1 %collective-permute-start.13 = (bf16[2,64,1536]{2,1,0:T(8,128)(2,1)S(1)}, bf16[2,64,1536]{2,1,0:T(8,128)(2,1)S(1)}, u32[]{:S(2)}, u32[]{:S(2)}) collective-permute-start(bf16[2,64,1536]{2,1,0:T(8,128)(2,1)S(1)} %join.4.refs_0_), channel_id=1, source_target_pairs={{0,128},{16,144},{32,160},{48,176},{64,192},{80,208},{96,224},{112... | collective-permute-start | bytes 1179656 | tf_op jit(solution)/shard_map/cond/branch_1_fun/ppermute | solution.py:47
  42.9 8.9 %collective-permute-done.13.refs_1_ = bf16[2,64,1536]{2,1,0:T(8,128)(2,1)S(1)} collective-permute-done((bf16[2,64,1536]{2,1,0:T(8,128)(2,1)S(1)}, bf16[2,64,1536]{2,1,0:T(8,128)(2,1)S(1)}, u32[]{:S(2)}, u32[]{:S(2)}) %collective-permute-start.13) | collective-permute-done | bytes 393248 | tf_op jit(solution)/shard_map/cond/branch_1_fun/ppermute | solution.py:47
  57.1 13.3 %collective-permute-done.12.refs_3_ = bf16[4,192,384]{2,1,0:T(8,128)(2,1)S(1)} collective-permute-done((bf16[4,192,384]{2,1,0:T(8,128)(2,1)S(1)}, bf16[4,192,384]{2,1,0:T(8,128)(2,1)S(1)}, u32[]{:S(2)}, u32[]{:S(2)}) %collective-permute-start.12) | collective-permute-done | bytes 589856 | tf_op jit(solution)/shard_map/cond/branch_1_fun/ppermute | solution.py:38
  70.4 12.2 %collective-permute-done.11.refs_2_ = bf16[4,192,384]{2,1,0:T(8,128)(2,1)S(1)} collective-permute-done((bf16[4,192,384]{2,1,0:T(8,128)(2,1)S(1)}, bf16[4,192,384]{2,1,0:T(8,128)(2,1)S(1)}, u32[]{:S(2)}, u32[]{:S(2)}) %collective-permute-start.11) | collective-permute-done | bytes 589856 | tf_op jit(solution)/shard_map/cond/branch_1_fun/ppermute | solution.py:38
  87.9 27.8 %conditional.5 = (bf16[2,384,640]{2,1,0:T(8,128)(2,1)}, bf16[2,384,640]{2,1,0:T(8,128)(2,1)}, bf16[2,384,640]{2,1,0:T(8,128)(2,1)}) conditional(s32[]{:T(128)} %bitcast.12, () %tuple.58, bf16[2,384,640]{2,1,0:T(8,128)(2,1)} %collective-permute-done.22), branch_computations={%region_3.4_spmd, %region_4.5_spmd} | conditional | bytes 11796624 | solution.py:263
  88.4 24.4 %collective-permute-done = bf16[2,384,640]{2,1,0:T(8,128)(2,1)} collective-permute-done((bf16[2,384,640]{2,1,0:T(8,128)(2,1)}, bf16[2,384,640]{2,1,0:T(8,128)(2,1)}, u32[]{:S(2)}, u32[]{:S(2)}) %collective-permute-start) | collective-permute-done | bytes 983072 | tf_op jit(solution)/shard_map/cond/branch_1_fun/ppermute | solution.py:43
  112.8 2.9 %collective-permute-done.2 = bf16[2,384,640]{2,1,0:T(8,128)(2,1)} collective-permute-done((bf16[2,384,640]{2,1,0:T(8,128)(2,1)}, bf16[2,384,640]{2,1,0:T(8,128)(2,1)}, u32[]{:S(2)}, u32[]{:S(2)}) %collective-permute-start.2) | collective-permute-done | bytes 983072 | tf_op jit(solution)/shard_map/cond/branch_1_fun/ppermute | solution.py:38
  115.7 9.9 %collective-permute-done.21 = bf16[2,384,512]{2,1,0:T(8,128)(2,1)} collective-permute-done((bf16[2,384,512]{2,1,0:T(8,128)(2,1)S(1)}, bf16[2,384,512]{2,1,0:T(8,128)(2,1)}, u32[]{:S(2)}, u32[]{:S(2)}) %collective-permute-start.21) | collective-permute-done | bytes 786464 | tf_op jit(solution)/shard_map/ppermute | solution.py:38
  127.9 23.3 %conditional.6 = (bf16[384,640]{1,0:T(8,128)(2,1)S(1)}, bf16[2,384,512]{2,1,0:T(8,128)(2,1)}, bf16[2,384,512]{2,1,0:T(8,128)(2,1)}, bf16[2,384,512]{2,1,0:T(8,128)(2,1)}) conditional(s32[]{:T(128)} %bitcast.12, () %tuple.61, (bf16[2,384,512]{2,1,0:T(8,128)(2,1)}, f32[3,18]{1,0:T(4,128)S(1)}, bf16[384,1536]{1,0:T(8,128)(2,1)}, ...), branch_computations={%region_5.6_spmd, %region_6.7_spmd} | conditional | flops 8053063680 | bytes 16973976 | solution.py:263
  128.4 10.9 %attend.4 = bf16[384,640]{1,0:T(8,128)(2,1)S(1)} custom-call(f32[3,18]{1,0:T(4,128)S(1)} %get-tuple-element.125.bias, bf16[384,1536]{1,0:T(8,128)(2,1)} %get-tuple-element.126.q, bf16[384,1536]{1,0:T(8,128)(2,1)S(1)} %get-tuple-element.127.k0, bf16[384,1536]{1,0:T(8,128)(2,1)} %get-tuple-element.128.v0, bf16[2,384,1536]{2,1,0:T(8,128)(2,1)} %get-tuple-element.129.a1, ...), custom_call_target="tpu_custom_call" | custom-call | flops 8053063680 | bytes 7536640 | tf_op jit(solution)/shard_map/cond/branch_1_fun/attend/pallas_call | solution.py:184
  139.4 9.3 %collective-permute-done.3 = bf16[2,384,512]{2,1,0:T(8,128)(2,1)} collective-permute-done((bf16[2,384,512]{2,1,0:T(8,128)(2,1)}, bf16[2,384,512]{2,1,0:T(8,128)(2,1)}, u32[]{:S(2)}, u32[]{:S(2)}) %collective-permute-start.3) | collective-permute-done | bytes 786464 | tf_op jit(solution)/shard_map/cond/branch_1_fun/ppermute | solution.py:43
  153.8 17.9 %conditional.7 = (bf16[384,512]{1,0:T(8,128)(2,1)S(1)}, bf16[2,384,256]{2,1,0:T(8,128)(2,1)}, bf16[4,384,256]{2,1,0:T(8,128)(2,1)}, bf16[3072,384]{1,0:T(8,128)(2,1)}, bf16[3072,384]{1,0:T(8,128)(2,1)}) conditional(s32[]{:T(128)} %bitcast.12, () %tuple.64, (bf16[2,384,256]{2,1,0:T(8,128)(2,1)}, f32[3,18]{1,0:T(4,128)S(1)}, ...), branch_computations={%region_7.8_spmd, %region_8.9_spmd} | conditional | flops 6442450944 | bytes 31195336 | solution.py:263
  154.3 9.1 %attend.5 = bf16[384,512]{1,0:T(8,128)(2,1)S(1)} custom-call(f32[3,18]{1,0:T(4,128)S(1)} %get-tuple-element.138.bias, bf16[384,1536]{1,0:T(8,128)(2,1)} %get-tuple-element.139.q, bf16[384,1536]{1,0:T(8,128)(2,1)S(1)} %get-tuple-element.140.k0, bf16[384,1536]{1,0:T(8,128)(2,1)} %get-tuple-element.141.v0, bf16[2,384,1536]{2,1,0:T(8,128)(2,1)} %get-tuple-element.142.a1, ...), custom_call_target="tpu_custom_call" | custom-call | flops 6442450944 | bytes 6029312 | tf_op jit(solution)/shard_map/cond/branch_1_fun/attend/pallas_call | solution.py:184
  163.4 3.6 %collective-permute-done.6.far = bf16[2,384,256]{2,1,0:T(8,128)(2,1)} collective-permute-done((bf16[2,384,256]{2,1,0:T(8,128)(2,1)}, bf16[2,384,256]{2,1,0:T(8,128)(2,1)}, u32[]{:S(2)}, u32[]{:S(2)}) %collective-permute-start.6) | collective-permute-done | bytes 393248 | tf_op jit(solution)/shard_map/cond/branch_1_fun/ppermute | solution.py:43
  172.2 5.3 %attend.6.refs_2_ = bf16[384,256]{1,0:T(8,128)(2,1)S(1)} custom-call(f32[3,18]{1,0:T(4,128)S(1)} %and_select_fusion.2.bias, bf16[384,1536]{1,0:T(8,128)(2,1)} %bitcast.51, bf16[384,1536]{1,0:T(8,128)(2,1)S(1)} %bitcast.38, bf16[384,1536]{1,0:T(8,128)(2,1)} %bitcast.44, bf16[2,384,1536]{2,1,0:T(8,128)(2,1)} %collective-permute-done.19.a1, ...), custom_call_target="tpu_custom_call" | custom-call | flops 3221225472 | bytes 3014656 | tf_op jit(solution)/shard_map/attend/pallas_call | solution.py:184
  179.8 4.7 %collective-permute-done.26.c0 = bf16[2,384,128]{2,1,0:T(8,128)(2,1)S(1)} collective-permute-done((bf16[2,384,128]{2,1,0:T(8,128)(2,1)S(1)}, bf16[2,384,128]{2,1,0:T(8,128)(2,1)S(1)}, u32[]{:S(2)}, u32[]{:S(2)}) %collective-permute-start.26) | collective-permute-done | bytes 196640 | tf_op jit(solution)/shard_map/ppermute | solution.py:43
  184.5 2.9 %attend.7.refs_3_ = bf16[384,128]{1,0:T(8,128)(2,1)S(1)} custom-call(f32[3,18]{1,0:T(4,128)S(1)} %and_select_fusion.2.bias, bf16[384,1536]{1,0:T(8,128)(2,1)S(1)} %bitcast.52, bf16[384,1536]{1,0:T(8,128)(2,1)S(1)} %bitcast.39, bf16[384,1536]{1,0:T(8,128)(2,1)S(1)} %bitcast.48, bf16[2,384,1536]{2,1,0:T(8,128)(2,1)} %collective-permute-done.19.a1, ...), custom_call_target="tpu_custom_call" | custom-call | flops 1610612736 | bytes 1507328 | tf_op jit(solution)/shard_map/attend/pallas_call | solution.py:184
  187.4 9.2 %project.1 = bf16[384,3072]{1,0:T(8,128)(2,1)} custom-call(bf16[384,640]{1,0:T(8,128)(2,1)S(1)} %get-tuple-element.228.refs_0_, bf16[384,512]{1,0:T(8,128)(2,1)S(1)} %get-tuple-element.234.refs_1_, bf16[384,256]{1,0:T(8,128)(2,1)S(1)} %attend.6.refs_2_, bf16[384,128]{1,0:T(8,128)(2,1)S(1)} %attend.7.refs_3_, s32[4]{0:T(128)S(1)} %pad_add_fusion.refs_4_, ...), custom_call_target="tpu_custom_call" | custom-call | flops 3623878656 | bytes 14155776 | tf_op jit(solution)/shard_map/project/pallas_call | solution.py:234
  (129 shorter events, 40.8 us)
Async XLA Ops:
  1.1 18.9 %collective-permute-start.17 = (bf16[192,384]{1,0:T(8,128)(2,1)S(1)}, bf16[192,384]{1,0:T(8,128)(2,1)S(1)}, u32[]{:S(2)}, u32[]{:S(2)}) collective-permute-start(bf16[192,384]{1,0:T(8,128)(2,1)S(1)} %dynamic-slice_bitcast_fusion), channel_id=1, source_target_pairs={{0,2},{16,18},{1,3},{17,19},{2,32},{18,48},{3,33},{19,49},{32,34},... | collective-permute-start | bytes 442376 | tf_op jit(solution)/shard_map/ppermute | solution.py:38
  5.7 14.3 %collective-permute-start.16 = (bf16[192,384]{1,0:T(8,128)(2,1)S(1)}, bf16[192,384]{1,0:T(8,128)(2,1)S(1)}, u32[]{:S(2)}, u32[]{:S(2)}) collective-permute-start(bf16[192,384]{1,0:T(8,128)(2,1)S(1)} %dynamic-slice_bitcast_fusion), channel_id=1, source_target_pairs={{0,35},{16,51},{1,0},{17,16},{2,1},{18,17},{3,2},{19,18},{32,3},{4... | collective-permute-start | bytes 442376 | tf_op jit(solution)/shard_map/ppermute | solution.py:38
  5.7 14.3 %collective-permute-start.15 = (bf16[192,384]{1,0:T(8,128)(2,1)S(1)}, bf16[192,384]{1,0:T(8,128)(2,1)S(1)}, u32[]{:S(2)}, u32[]{:S(2)}) collective-permute-start(bf16[192,384]{1,0:T(8,128)(2,1)S(1)} %dynamic-slice_bitcast_fusion), channel_id=1, source_target_pairs={{0,1},{16,17},{1,2},{17,18},{2,3},{18,19},{3,32},{19,48},{32,33},{... | collective-permute-start | bytes 442376 | tf_op jit(solution)/shard_map/ppermute | solution.py:38
  9.3 10.7 %collective-permute-start.18 = (bf16[2,16,1536]{2,1,0:T(8,128)(2,1)S(1)}, bf16[2,16,1536]{2,1,0:T(8,128)(2,1)S(1)}, u32[]{:S(2)}, u32[]{:S(2)}) collective-permute-start(bf16[2,16,1536]{2,1,0:T(8,128)(2,1)S(1)} %pair.10.refs_0_), channel_id=1, source_target_pairs={{0,32},{16,48},{32,0},{48,16},{64,96},{80,112},{96,64},{112,80},{1... | collective-permute-start | bytes 294920 | tf_op jit(solution)/shard_map/ppermute | solution.py:47
  21.3 18.4 %collective-permute-start.19 = (bf16[2,384,1536]{2,1,0:T(8,128)(2,1)S(1)}, bf16[2,384,1536]{2,1,0:T(8,128)(2,1)}, u32[]{:S(2)}, u32[]{:S(2)}) collective-permute-start(bf16[2,384,1536]{2,1,0:T(8,128)(2,1)S(1)} %pair.11), channel_id=1, source_target_pairs={{0,16},{16,0},{1,17},{17,1},{2,18},{18,2},{3,19},{19,3},{32,48},{4... | collective-permute-start | bytes 7077896 | tf_op jit(solution)/shard_map/ppermute | solution.py:38
  21.4 63.7 %collective-permute-start.22 = (bf16[2,384,640]{2,1,0:T(8,128)(2,1)}, bf16[2,384,640]{2,1,0:T(8,128)(2,1)}, u32[]{:S(2)}, u32[]{:S(2)}) collective-permute-start(bf16[2,384,640]{2,1,0:T(8,128)(2,1)} %pair.9), channel_id=1, source_target_pairs={{0,32},{16,48},{1,33},{17,49},{2,34},{18,50},{3,35},{19,51},{32,0}... | collective-permute-start | bytes 2949128 | tf_op jit(solution)/shard_map/ppermute | solution.py:38
  39.8 12.0 %collective-permute-start.13 = (bf16[2,64,1536]{2,1,0:T(8,128)(2,1)S(1)}, bf16[2,64,1536]{2,1,0:T(8,128)(2,1)S(1)}, u32[]{:S(2)}, u32[]{:S(2)}) collective-permute-start(bf16[2,64,1536]{2,1,0:T(8,128)(2,1)S(1)} %join.4.refs_0_), channel_id=1, source_target_pairs={{0,128},{16,144},{32,160},{48,176},{64,192},{80,208},{96,224},{112... | collective-permute-start | bytes 1179656 | tf_op jit(solution)/shard_map/cond/branch_1_fun/ppermute | solution.py:47
  51.9 33.0 %collective-permute-start.14 = (bf16[2,128,1536]{2,1,0:T(8,128)(2,1)S(1)}, bf16[2,128,1536]{2,1,0:T(8,128)(2,1)S(1)}, u32[]{:S(2)}, u32[]{:S(2)}) collective-permute-start(bf16[2,128,1536]{2,1,0:T(8,128)(2,1)S(1)} %join.5.refs_0_), channel_id=1, source_target_pairs={{0,16},{16,0},{32,48},{48,32},{64,80},{80,64},{96,112},{112,96},{1... | collective-permute-start | bytes 2359304 | tf_op jit(solution)/shard_map/cond/branch_1_fun/ppermute | solution.py:47
  52.6 17.8 %collective-permute-start.12 = (bf16[4,192,384]{2,1,0:T(8,128)(2,1)S(1)}, bf16[4,192,384]{2,1,0:T(8,128)(2,1)S(1)}, u32[]{:S(2)}, u32[]{:S(2)}) collective-permute-start(bf16[4,192,384]{2,1,0:T(8,128)(2,1)S(1)} %place.2.refs_0_), channel_id=1, source_target_pairs={{0,8},{16,24},{1,9},{17,25},{2,10},{18,26},{3,11},{19,27},{32,40},... | collective-permute-start | bytes 1769480 | tf_op jit(solution)/shard_map/cond/branch_1_fun/ppermute | solution.py:38
  55.0 27.6 %collective-permute-start.11 = (bf16[4,192,384]{2,1,0:T(8,128)(2,1)S(1)}, bf16[4,192,384]{2,1,0:T(8,128)(2,1)S(1)}, u32[]{:S(2)}, u32[]{:S(2)}) collective-permute-start(bf16[4,192,384]{2,1,0:T(8,128)(2,1)S(1)} %place.2.refs_0_), channel_id=1, source_target_pairs={{0,12},{16,28},{1,13},{17,29},{2,14},{18,30},{3,15},{19,31},{32,44... | collective-permute-start | bytes 1769480 | tf_op jit(solution)/shard_map/cond/branch_1_fun/ppermute | solution.py:38
  56.4 26.4 %collective-permute-start.10 = (bf16[4,192,384]{2,1,0:T(8,128)(2,1)S(1)}, bf16[4,192,384]{2,1,0:T(8,128)(2,1)S(1)}, u32[]{:S(2)}, u32[]{:S(2)}) collective-permute-start(bf16[4,192,384]{2,1,0:T(8,128)(2,1)S(1)} %place.2.refs_0_), channel_id=1, source_target_pairs={{0,4},{16,20},{1,5},{17,21},{2,6},{18,22},{3,7},{19,23},{32,36},{4... | collective-permute-start | bytes 1769480 | tf_op jit(solution)/shard_map/cond/branch_1_fun/ppermute | solution.py:38
  85.0 66.2 %collective-permute-start.24 = (bf16[3072,384]{1,0:T(8,128)(2,1)}, bf16[3072,384]{1,0:T(8,128)(2,1)}, u32[]{:S(2)}, u32[]{:S(2)}) collective-permute-start(bf16[3072,384]{1,0:T(8,128)(2,1)} %get-tuple-element.227.refs_5_), channel_id=1, source_target_pairs={{0,192},{16,208},{32,96},{48,112},{64,0},{80,16},{96,160},{112,176... | collective-permute-start | bytes 7077896 | tf_op jit(solution)/shard_map/ppermute | solution.py:52
  87.9 37.7 %collective-permute-start.21 = (bf16[2,384,512]{2,1,0:T(8,128)(2,1)S(1)}, bf16[2,384,512]{2,1,0:T(8,128)(2,1)}, u32[]{:S(2)}, u32[]{:S(2)}) collective-permute-start(bf16[2,384,512]{2,1,0:T(8,128)(2,1)S(1)} %copy-done.3), channel_id=1, source_target_pairs={{0,32},{16,48},{1,33},{17,49},{2,34},{18,50},{3,35},{19,51},{32,0}... | collective-permute-start | bytes 2359304 | tf_op jit(solution)/shard_map/ppermute | solution.py:38
  87.9 24.9 %collective-permute-start = (bf16[2,384,640]{2,1,0:T(8,128)(2,1)}, bf16[2,384,640]{2,1,0:T(8,128)(2,1)}, u32[]{:S(2)}, u32[]{:S(2)}) collective-permute-start(bf16[2,384,640]{2,1,0:T(8,128)(2,1)} %param.3), channel_id=1, source_target_pairs={{0,64},{16,80},{32,224},{48,240},{64,128},{80,144},{96,32},{112,48... | collective-permute-start | bytes 2949128 | tf_op jit(solution)/shard_map/cond/branch_1_fun/ppermute | solution.py:43
  88.4 24.4 %collective-permute-start.1 = (bf16[2,384,640]{2,1,0:T(8,128)(2,1)}, bf16[2,384,640]{2,1,0:T(8,128)(2,1)}, u32[]{:S(2)}, u32[]{:S(2)}) collective-permute-start(bf16[2,384,640]{2,1,0:T(8,128)(2,1)} %param.3), channel_id=1, source_target_pairs={{0,16},{16,0},{1,17},{17,1},{2,18},{18,2},{3,19},{19,3},{32,48},{4... | collective-permute-start | bytes 2949128 | tf_op jit(solution)/shard_map/cond/branch_1_fun/ppermute | solution.py:38
  125.6 25.7 %collective-permute-start.23 = (bf16[2,384,256]{2,1,0:T(8,128)(2,1)S(1)}, bf16[2,384,256]{2,1,0:T(8,128)(2,1)}, u32[]{:S(2)}, u32[]{:S(2)}) collective-permute-start(bf16[2,384,256]{2,1,0:T(8,128)(2,1)S(1)} %pair.7), channel_id=1, source_target_pairs={{0,32},{16,48},{1,33},{17,49},{2,34},{18,50},{3,35},{19,51},{32,0}... | collective-permute-start | bytes 1179656 | tf_op jit(solution)/shard_map/ppermute | solution.py:38
  127.9 20.7 %collective-permute-start.3 = (bf16[2,384,512]{2,1,0:T(8,128)(2,1)}, bf16[2,384,512]{2,1,0:T(8,128)(2,1)}, u32[]{:S(2)}, u32[]{:S(2)}) collective-permute-start(bf16[2,384,512]{2,1,0:T(8,128)(2,1)} %get-tuple-element.124), channel_id=1, source_target_pairs={{0,64},{16,80},{32,224},{48,240},{64,128},{80,144},{96,32},{112,48... | collective-permute-start | bytes 2359304 | tf_op jit(solution)/shard_map/cond/branch_1_fun/ppermute | solution.py:43
  128.4 20.2 %collective-permute-start.4 = (bf16[2,384,512]{2,1,0:T(8,128)(2,1)}, bf16[2,384,512]{2,1,0:T(8,128)(2,1)}, u32[]{:S(2)}, u32[]{:S(2)}) collective-permute-start(bf16[2,384,512]{2,1,0:T(8,128)(2,1)} %get-tuple-element.124), channel_id=1, source_target_pairs={{0,16},{16,0},{1,17},{17,1},{2,18},{18,2},{3,19},{19,3},{32,48},{4... | collective-permute-start | bytes 2359304 | tf_op jit(solution)/shard_map/cond/branch_1_fun/ppermute | solution.py:38
  151.3 20.4 %collective-permute-start.25 = (bf16[2,384,128]{2,1,0:T(8,128)(2,1)S(1)}, bf16[2,384,128]{2,1,0:T(8,128)(2,1)S(1)}, u32[]{:S(2)}, u32[]{:S(2)}) collective-permute-start(bf16[2,384,128]{2,1,0:T(8,128)(2,1)S(1)} %copy-done.5), channel_id=1, source_target_pairs={{0,32},{16,48},{1,33},{17,49},{2,34},{18,50},{3,35},{19,51},{32,0}... | collective-permute-start | bytes 589832 | tf_op jit(solution)/shard_map/ppermute | solution.py:38
  153.8 17.9 %collective-permute-start.8 = (bf16[3072,384]{1,0:T(8,128)(2,1)}, bf16[3072,384]{1,0:T(8,128)(2,1)}, u32[]{:S(2)}, u32[]{:S(2)}) collective-permute-start(bf16[3072,384]{1,0:T(8,128)(2,1)} %get-tuple-element.150), channel_id=1, source_target_pairs={{0,16},{16,0},{1,17},{17,1},{2,18},{18,2},{3,19},{19,3},{32,48},{4... | collective-permute-start | bytes 7077896 | tf_op jit(solution)/shard_map/cond/branch_1_fun/ppermute | solution.py:38
  153.8 17.8 %collective-permute-start.9 = (bf16[3072,384]{1,0:T(8,128)(2,1)}, bf16[3072,384]{1,0:T(8,128)(2,1)}, u32[]{:S(2)}, u32[]{:S(2)}) collective-permute-start(bf16[3072,384]{1,0:T(8,128)(2,1)} %get-tuple-element.151), channel_id=1, source_target_pairs={{0,16},{16,0},{1,17},{17,1},{2,18},{18,2},{3,19},{19,3},{32,48},{4... | collective-permute-start | bytes 7077896 | tf_op jit(solution)/shard_map/cond/branch_1_fun/ppermute | solution.py:38
  154.3 12.6 %collective-permute-start.6 = (bf16[2,384,256]{2,1,0:T(8,128)(2,1)}, bf16[2,384,256]{2,1,0:T(8,128)(2,1)}, u32[]{:S(2)}, u32[]{:S(2)}) collective-permute-start(bf16[2,384,256]{2,1,0:T(8,128)(2,1)} %get-tuple-element.137.near), channel_id=1, source_target_pairs={{0,64},{16,80},{32,224},{48,240},{64,128},{80,144},{96,32},{112,48... | collective-permute-start | bytes 1179656 | tf_op jit(solution)/shard_map/cond/branch_1_fun/ppermute | solution.py:43
  171.9 7.9 %collective-permute-start.27 = (bf16[2,384,128]{2,1,0:T(8,128)(2,1)S(1)}, bf16[2,384,128]{2,1,0:T(8,128)(2,1)S(1)}, u32[]{:S(2)}, u32[]{:S(2)}) collective-permute-start(bf16[2,384,128]{2,1,0:T(8,128)(2,1)S(1)} %collective-permute-done.25.b0), channel_id=1, source_target_pairs={{0,80},{16,64},{32,240},{48,224},{64,144},{80,128},{96,48},{112,32... | collective-permute-start | bytes 589832 | tf_op jit(solution)/shard_map/ppermute | solution.py:43
  171.9 12.6 %collective-permute-start.26 = (bf16[2,384,128]{2,1,0:T(8,128)(2,1)S(1)}, bf16[2,384,128]{2,1,0:T(8,128)(2,1)S(1)}, u32[]{:S(2)}, u32[]{:S(2)}) collective-permute-start(bf16[2,384,128]{2,1,0:T(8,128)(2,1)S(1)} %collective-permute-done.25.b0), channel_id=1, source_target_pairs={{0,64},{16,80},{32,224},{48,240},{64,128},{80,144},{96,32},{112,48... | collective-permute-start | bytes 589832 | tf_op jit(solution)/shard_map/ppermute | solution.py:43
  (34 other events, 333.5 us)
where the time goes:
time: 197 us
  waiting for transfers between devices  108 us (55%)
  Pallas kernels  49.2 us (25%)
  starting transfers between devices  32.7 us (17%)
  local copies, waits for them, and re-layouts  5.35 us (3%)
    ppermute x5, waiting for transfers between devices, forward(): return lax.ppermute(value, 'seq', pairs)  44.2 us
    ppermute x19, waiting for transfers between devices, shift(): return lax.ppermute(value, AXES, pairs)  43.7 us
    pallas_call x4, Pallas kernels, attend(): pl.pallas_call(attend_kernel, grid=(count,), out_shape=jax.ShapeDtypeStru...  28.2 us
    ppermute x19, starting transfers between devices, shift(): return lax.ppermute(value, AXES, pairs)  22.4 us
    ppermute x4, waiting for transfers between devices, swap(): return lax.ppermute(value, 'seq', [(s, s ^ bit) for s in range(16)])  19.7 us
    pallas_call x1, Pallas kernels, project(): pl.pallas_call(project_kernel, grid=(D // step,), out_shape=jax.ShapeDtyp...  9.15 us
    pallas_call x6, Pallas kernels, pair(): pl.pallas_call(pair_kernel, grid=(count,), out_shape=jax.ShapeDtypeStruct...  6.89 us
    ppermute x4, starting transfers between devices, swap(): return lax.ppermute(value, 'seq', [(s, s ^ bit) for s in range(16)])  6.23 us
  transfers between devices with their start and end apart: 29, of which 15 were waited for; matrix products, arithmetic and copies ran while one was open for 1% of the time, Pallas kernels for 18%

commit v1 on v0

--- a/solution.py
+++ b/solution.py
@@ -17,7 +17,7 @@
 PANEL = 192
 D = 3072
 TEXT = 256
-GROUPS = (5, 4, 2, 1)
+GROUPS = (4, 4, 3, 1)
 NEG = -1e30
 SCALE = HD**-0.5 * 1.4426950408889634
 AXES = ("seq", "fsdp")
@@ -204,7 +204,7 @@
 
 def project_kernel(*refs):
     parts = refs[: len(GROUPS)]
-    order, wa, wb, wc, wd, bias, gate, residual, out, att, mine = refs[
+    order, wa, wb, wc, wd, bias, gate, residual, out, mine = refs[
         len(GROUPS) :
     ]
     step = pl.program_id(0)
@@ -214,11 +214,9 @@
         head = 0
         for part in parts:
             for n in range(part.shape[1] // HD):
-                column = head % 3 * HD
-                att[head // 3, :, column : column + HD] = part[:, n * HD : (n + 1) * HD]
+                column = pl.multiple_of(order[head // 3] * QUARTER + head % 3 * HD, HD)
+                mine[:, pl.ds(column, HD)] = part[:, n * HD : (n + 1) * HD]
                 head += 1
-        for n in range(4):
-            mine[:, n * QUARTER : (n + 1) * QUARTER] = att[order[n]]
 
     wt = jnp.concatenate([wa[...], wb[...], wc[...], wd[...]], axis=1)
     projected = lax.dot_general(
@@ -245,7 +243,6 @@
         ],
         out_specs=pl.BlockSpec((ROWS, step), lambda i: (0, i)),
         scratch_shapes=[
-            pltpu.VMEM((4, ROWS, QUARTER), jnp.bfloat16),
             pltpu.VMEM((ROWS, HID), jnp.bfloat16),
         ],
         compiler_params=pltpu.CompilerParams(vmem_limit_bytes=14 * 1024 * 1024),
@@ -332,8 +329,7 @@
             text_z,
         )
     )
-    text = join(text, text_z)
-    packs, bias, beside, wz1, wz2, wz3, text_x = lax.optimization_barrier(
+    packs, bias, beside, wz1, wz2, wz3 = lax.optimization_barrier(
         (
             packs[1:],
             bias,
@@ -341,34 +337,32 @@
             wz1,
             wz2,
             wz3,
-            swap(text, 4),
         )
     )
     near0 = shift(pack0, dz=4)
     packs = (pack0,) + tuple(packs)
     ready = tile_lists[0, 0, 0, 0] > -2
 
-    def weight_stage(piece, wz1, wz2, wz3, text, text_x):
-        text = join(text, text_x)
+    def weight_stage(piece, wz1, wz2, wz3, text, text_z):
+        wz = place_all((zl - steps) % 4, piece, wz1, wz2, wz3)
+        wy1, text = lax.optimization_barrier((shift(wz, dy=1), join(text, text_z)))
+        wy = place_all((y - steps) % 4, wz, wy1, shift(wz, dy=-1), shift(wz, dy=2))
+        text = join(text, swap(text, 4))
         text = join(text, swap(text, 8))
-        text = join(text, swap(text, 1))
-        wz = place_all((zl - steps) % 4, piece, wz1, wz2, wz3)
-        wy = place_all(
-            (y - steps) % 4, wz, shift(wz, dy=1), shift(wz, dy=-1), shift(wz, dy=2)
-        )
         return wy.reshape(D, QUARTER), text
 
-    wy, text = stage(ready, weight_stage, piece, wz1, wz2, wz3, text, text_x)
+    wy, text = stage(ready, weight_stage, piece, wz1, wz2, wz3, text, text_z)
     pack1, wy = lax.optimization_barrier((packs[1], wy))
     near1 = shift(pack1, dz=4)
     near0, wy = lax.optimization_barrier((near0, wy))
     wx = across(wy)
 
-    def first_stage(near0):
+    def first_stage(near0, text):
         far0 = forward(near0)
-        return far0, shift(near0, dc=1), shift(far0, dc=1)
-
-    far0, near0_other, far0_other = stage(ready, first_stage, near0)
+        text = join(text, swap(text, 1))
+        return far0, shift(near0, dc=1), shift(far0, dc=1), text
+
+    far0, near0_other, far0_other, text = stage(ready, first_stage, near0, text)
 
     def second_stage(near1, near0, near0_other, far0, far0_other, text):
         part0 = attend_group(0, near0, near0_other, far0, text, far0_other)

time: 197 us -> 190 us (0.964); the launches traced: 197 us -> 187 us
  waiting for transfers between devices: 108 us -> 91.4 us
  Pallas kernels: 49.2 us -> 53.5 us
  starting transfers between devices: 32.7 us -> 34.8 us
    ppermute x4, waiting for transfers between devices: 19.7 us -> 11.4 us  [swap(): return lax.ppermute(value, 'seq', [(s, s ^ bit) for s in range(16)])]
    ppermute x19, waiting for transfers between devices: 43.7 us -> 37.3 us  [shift(): return lax.ppermute(value, AXES, pairs)]
    pallas_call x4, Pallas kernels: 0.2 us -> 4.31 us  [join(): pl.pallas_call(join_kernel, out_shape=jax.ShapeDtypeStruct((2, rows, HID)...]
    ppermute x19, starting transfers between devices: 22.4 us -> 24.6 us  [shift(): return lax.ppermute(value, AXES, pairs)]
    unnamed x49 -> x51, local copies, waits for them, and re-layouts: 4.31 us -> 4.31 us
  transfers between devices with their start and end apart: 29 -> 29, of which waited for: 15 -> 15; matrix products, arithmetic and copies ran while one was open for 1% -> 1% of each run, Pallas kernels for 18% -> 21%
where the time goes in v1:
time: 190 us; the launch traced here: 187 us
  waiting for transfers between devices  91.4 us (48%)
  Pallas kernels  53.5 us (28%)
  starting transfers between devices  34.8 us (18%)
  local copies, waits for them, and re-layouts  5.32 us (3%)
    ppermute x5, waiting for transfers between devices, forward(): return lax.ppermute(value, 'seq', pairs)  42.7 us
    ppermute x19, waiting for transfers between devices, shift(): return lax.ppermute(value, AXES, pairs)  37.3 us
    pallas_call x4, Pallas kernels, attend(): pl.pallas_call(attend_kernel, grid=(count,), out_shape=jax.ShapeDtypeStru...  28.3 us
    ppermute x19, starting transfers between devices, shift(): return lax.ppermute(value, AXES, pairs)  24.6 us
    ppermute x4, waiting for transfers between devices, swap(): return lax.ppermute(value, 'seq', [(s, s ^ bit) for s in range(16)])  11.4 us
    pallas_call x1, Pallas kernels, project(): pl.pallas_call(project_kernel, grid=(D // step,), out_shape=jax.ShapeDtyp...  9.16 us
    ppermute x4, starting transfers between devices, swap(): return lax.ppermute(value, 'seq', [(s, s ^ bit) for s in range(16)])  6.06 us
    pallas_call x6, Pallas kernels, pair(): pl.pallas_call(pair_kernel, grid=(count,), out_shape=jax.ShapeDtypeStruct...  5.25 us
  transfers between devices with their start and end apart: 29, of which 15 were waited for; matrix products, arithmetic and copies ran while one was open for 1% of the time, Pallas kernels for 21%

profile of v1, /device:TPU:72, one launch (start us, length us, event | category | flops | bytes accessed | tf_op | source)
XLA Modules:
  0.0 187.5 jit_solution(13394894520566727133)
XLA Ops:
  1.1 4.6 %collective-permute-start.18 = (bf16[192,384]{1,0:T(8,128)(2,1)S(1)}, bf16[192,384]{1,0:T(8,128)(2,1)S(1)}, u32[]{:S(2)}, u32[]{:S(2)}) collective-permute-start(bf16[192,384]{1,0:T(8,128)(2,1)S(1)} %dynamic-slice_bitcast_fusion), channel_id=1, source_target_pairs={{0,2},{16,18},{1,3},{17,19},{2,32},{18,48},{3,33},{19,49},{32,34},... | collective-permute-start | bytes 442376 | tf_op jit(solution)/shard_map/ppermute | solution.py:38
  12.9 7.0 %collective-permute-done.19 = bf16[2,16,1536]{2,1,0:T(8,128)(2,1)S(1)} collective-permute-done((bf16[2,16,1536]{2,1,0:T(8,128)(2,1)S(1)}, bf16[2,16,1536]{2,1,0:T(8,128)(2,1)S(1)}, u32[]{:S(2)}, u32[]{:S(2)}) %collective-permute-start.19) | collective-permute-done | bytes 98336 | tf_op jit(solution)/shard_map/ppermute | solution.py:47
  21.5 5.7 %collective-permute-start.22 = (bf16[2,384,512]{2,1,0:T(8,128)(2,1)}, bf16[2,384,512]{2,1,0:T(8,128)(2,1)}, u32[]{:S(2)}, u32[]{:S(2)}) collective-permute-start(bf16[2,384,512]{2,1,0:T(8,128)(2,1)} %copy-done.2), channel_id=1, source_target_pairs={{0,32},{16,48},{1,33},{17,49},{2,34},{18,50},{3,35},{19,51},{32,0}... | collective-permute-start | bytes 2359304 | tf_op jit(solution)/shard_map/ppermute | solution.py:38
  32.7 35.5 %conditional.4 = (bf16[3072,384]{1,0:T(8,128)(2,1)}, bf16[2,128,1536]{2,1,0:T(8,128)(2,1)}) conditional(s32[]{:T(128)} %bitcast.12, () %tuple.56, (s32[]{:T(128)}, s32[]{:T(128)}, (), bf16[192,384]{1,0:T(8,128)(2,1)}, bf16[192,384]{1,0:T(8,128)(2,1)}, /*index=5*/bf16[192,384]{1,0:T(8,128)(2,1)}, bf16[192,384]{1,0:T(8,128)(2,1)}, ...), branch_computations={%region_1.2_spmd, %region_2.3_spmd} | conditional | flops 115 | bytes 18088396 | solution.py:260
  40.7 10.3 %collective-permute-done.11.refs_1_ = bf16[4,192,384]{2,1,0:T(8,128)(2,1)S(1)} collective-permute-done((bf16[4,192,384]{2,1,0:T(8,128)(2,1)S(1)}, bf16[4,192,384]{2,1,0:T(8,128)(2,1)S(1)}, u32[]{:S(2)}, u32[]{:S(2)}) %collective-permute-start.11) | collective-permute-done | bytes 589856 | tf_op jit(solution)/shard_map/cond/branch_1_fun/ppermute | solution.py:38
  52.5 4.2 %collective-permute-done.14.refs_1_ = bf16[2,32,1536]{2,1,0:T(8,128)(2,1)S(1)} collective-permute-done((bf16[2,32,1536]{2,1,0:T(8,128)(2,1)S(1)}, bf16[2,32,1536]{2,1,0:T(8,128)(2,1)S(1)}, u32[]{:S(2)}, u32[]{:S(2)}) %collective-permute-start.14) | collective-permute-done | bytes 196640 | tf_op jit(solution)/shard_map/cond/branch_1_fun/ppermute | solution.py:47
  56.7 3.1 %collective-permute-start.15 = (bf16[2,64,1536]{2,1,0:T(8,128)(2,1)S(1)}, bf16[2,64,1536]{2,1,0:T(8,128)(2,1)S(1)}, u32[]{:S(2)}, u32[]{:S(2)}) collective-permute-start(bf16[2,64,1536]{2,1,0:T(8,128)(2,1)S(1)} %join.5.refs_0_), channel_id=1, source_target_pairs={{0,128},{16,144},{32,160},{48,176},{64,192},{80,208},{96,224},{112... | collective-permute-start | bytes 1179656 | tf_op jit(solution)/shard_map/cond/branch_1_fun/ppermute | solution.py:47
  59.8 5.2 %collective-permute-done.12.refs_2_ = bf16[4,192,384]{2,1,0:T(8,128)(2,1)S(1)} collective-permute-done((bf16[4,192,384]{2,1,0:T(8,128)(2,1)S(1)}, bf16[4,192,384]{2,1,0:T(8,128)(2,1)S(1)}, u32[]{:S(2)}, u32[]{:S(2)}) %collective-permute-start.12) | collective-permute-done | bytes 589856 | tf_op jit(solution)/shard_map/cond/branch_1_fun/ppermute | solution.py:38
  71.0 22.6 %conditional.5 = (bf16[2,384,512]{2,1,0:T(8,128)(2,1)}, bf16[2,384,512]{2,1,0:T(8,128)(2,1)}, bf16[2,384,512]{2,1,0:T(8,128)(2,1)}, bf16[2,256,1536]{2,1,0:T(8,128)(2,1)}) conditional(s32[]{:T(128)} %bitcast.12, () %tuple.59, (bf16[2,384,512]{2,1,0:T(8,128)(2,1)}, bf16[2,128,1536]{2,1,0:T(8,128)(2,1)}) %tuple.61), branch_computations={%region_3.4_spmd, %region_4.5_spmd} | conditional | bytes 15728832 | solution.py:260
  72.1 18.9 %collective-permute-done = bf16[2,384,512]{2,1,0:T(8,128)(2,1)} collective-permute-done((bf16[2,384,512]{2,1,0:T(8,128)(2,1)}, bf16[2,384,512]{2,1,0:T(8,128)(2,1)}, u32[]{:S(2)}, u32[]{:S(2)}) %collective-permute-start) | collective-permute-done | bytes 786464 | tf_op jit(solution)/shard_map/cond/branch_1_fun/ppermute | solution.py:43
  93.6 14.4 %collective-permute-done.21 = bf16[2,384,512]{2,1,0:T(8,128)(2,1)} collective-permute-done((bf16[2,384,512]{2,1,0:T(8,128)(2,1)S(1)}, bf16[2,384,512]{2,1,0:T(8,128)(2,1)}, u32[]{:S(2)}, u32[]{:S(2)}) %collective-permute-start.21) | collective-permute-done | bytes 786464 | tf_op jit(solution)/shard_map/ppermute | solution.py:38
  110.4 23.3 %conditional.6 = (bf16[384,512]{1,0:T(8,128)(2,1)S(1)}, bf16[2,384,512]{2,1,0:T(8,128)(2,1)}, bf16[2,384,512]{2,1,0:T(8,128)(2,1)}, bf16[2,384,512]{2,1,0:T(8,128)(2,1)}) conditional(s32[]{:T(128)} %bitcast.12, () %tuple.63, (bf16[2,384,512]{2,1,0:T(8,128)(2,1)}, f32[3,18]{1,0:T(4,128)S(1)}, bf16[384,1536]{1,0:T(8,128)(2,1)}, ...), branch_computations={%region_5.6_spmd, %region_6.7_spmd} | conditional | flops 6442450944 | bytes 15466648 | solution.py:260
  111.0 9.0 %attend.4 = bf16[384,512]{1,0:T(8,128)(2,1)S(1)} custom-call(f32[3,18]{1,0:T(4,128)S(1)} %get-tuple-element.132.bias, bf16[384,1536]{1,0:T(8,128)(2,1)} %get-tuple-element.133.q, bf16[384,1536]{1,0:T(8,128)(2,1)S(1)} %get-tuple-element.134.k0, bf16[384,1536]{1,0:T(8,128)(2,1)} %get-tuple-element.135.v0, bf16[2,384,1536]{2,1,0:T(8,128)(2,1)} %get-tuple-element.136.a1, ...), custom_call_target="tpu_custom_call" | custom-call | flops 6442450944 | bytes 6029312 | tf_op jit(solution)/shard_map/cond/branch_1_fun/attend/pallas_call | solution.py:184
  120.0 11.1 %collective-permute-done.4 = bf16[2,384,512]{2,1,0:T(8,128)(2,1)} collective-permute-done((bf16[2,384,512]{2,1,0:T(8,128)(2,1)}, bf16[2,384,512]{2,1,0:T(8,128)(2,1)}, u32[]{:S(2)}, u32[]{:S(2)}) %collective-permute-start.4) | collective-permute-done | bytes 786464 | tf_op jit(solution)/shard_map/cond/branch_1_fun/ppermute | solution.py:43
  135.1 3.5 %collective-permute-start.25 = (bf16[2,384,128]{2,1,0:T(8,128)(2,1)S(1)}, bf16[2,384,128]{2,1,0:T(8,128)(2,1)S(1)}, u32[]{:S(2)}, u32[]{:S(2)}) collective-permute-start(bf16[2,384,128]{2,1,0:T(8,128)(2,1)S(1)} %copy-done.6), channel_id=1, source_target_pairs={{0,32},{16,48},{1,33},{17,49},{2,34},{18,50},{3,35},{19,51},{32,0}... | collective-permute-start | bytes 589832 | tf_op jit(solution)/shard_map/ppermute | solution.py:38
  138.7 23.8 %conditional.7 = (bf16[384,512]{1,0:T(8,128)(2,1)S(1)}, bf16[2,384,384]{2,1,0:T(8,128)(2,1)}, bf16[4,384,384]{2,1,0:T(8,128)(2,1)}, bf16[3072,384]{1,0:T(8,128)(2,1)}, bf16[3072,384]{1,0:T(8,128)(2,1)}) conditional(s32[]{:T(128)} %bitcast.12, () %tuple.66, (bf16[2,384,384]{2,1,0:T(8,128)(2,1)}, f32[3,18]{1,0:T(4,128)S(1)}, ...), branch_computations={%region_7.8_spmd, %region_8.9_spmd} | conditional | flops 6442450944 | bytes 34341064 | solution.py:260
  139.2 9.1 %attend.5 = bf16[384,512]{1,0:T(8,128)(2,1)S(1)} custom-call(f32[3,18]{1,0:T(4,128)S(1)} %get-tuple-element.145.bias, bf16[384,1536]{1,0:T(8,128)(2,1)} %get-tuple-element.146.q, bf16[384,1536]{1,0:T(8,128)(2,1)S(1)} %get-tuple-element.147.k0, bf16[384,1536]{1,0:T(8,128)(2,1)} %get-tuple-element.148.v0, bf16[2,384,1536]{2,1,0:T(8,128)(2,1)} %get-tuple-element.149.a1, ...), custom_call_target="tpu_custom_call" | custom-call | flops 6442450944 | bytes 6029312 | tf_op jit(solution)/shard_map/cond/branch_1_fun/attend/pallas_call | solution.py:184
  148.3 7.8 %collective-permute-done.7.far = bf16[2,384,384]{2,1,0:T(8,128)(2,1)} collective-permute-done((bf16[2,384,384]{2,1,0:T(8,128)(2,1)}, bf16[2,384,384]{2,1,0:T(8,128)(2,1)}, u32[]{:S(2)}, u32[]{:S(2)}) %collective-permute-start.7) | collective-permute-done | bytes 589856 | tf_op jit(solution)/shard_map/cond/branch_1_fun/ppermute | solution.py:43
  156.1 3.2 %merge.1 = bf16[4,384,384]{2,1,0:T(8,128)(2,1)} custom-call(bf16[2,384,384]{2,1,0:T(8,128)(2,1)} %get-tuple-element.144.near, bf16[2,384,384]{2,1,0:T(8,128)(2,1)} %collective-permute-done.7.far), custom_call_target="tpu_custom_call" | custom-call | bytes 2359296 | tf_op jit(solution)/shard_map/cond/branch_1_fun/merge/pallas_call | solution.py:81
  159.3 3.2 %collective-permute-done.8 = bf16[4,384,384]{2,1,0:T(8,128)(2,1)} collective-permute-done((bf16[4,384,384]{2,1,0:T(8,128)(2,1)}, bf16[4,384,384]{2,1,0:T(8,128)(2,1)}, u32[]{:S(2)}, u32[]{:S(2)}) %collective-permute-start.8) | collective-permute-done | bytes 1179680 | tf_op jit(solution)/shard_map/cond/branch_1_fun/ppermute | solution.py:38
  163.0 7.3 %attend.6.refs_2_ = bf16[384,384]{1,0:T(8,128)(2,1)S(1)} custom-call(f32[3,18]{1,0:T(4,128)S(1)} %and_select_fusion.2.bias, bf16[384,1536]{1,0:T(8,128)(2,1)} %bitcast.51, bf16[384,1536]{1,0:T(8,128)(2,1)S(1)} %bitcast.38, bf16[384,1536]{1,0:T(8,128)(2,1)} %bitcast.44, bf16[2,384,1536]{2,1,0:T(8,128)(2,1)} %collective-permute-done.20.a1, ...), custom_call_target="tpu_custom_call" | custom-call | flops 4831838208 | bytes 4521984 | tf_op jit(solution)/shard_map/attend/pallas_call | solution.py:184
  170.7 4.7 %collective-permute-done.26.c0 = bf16[2,384,128]{2,1,0:T(8,128)(2,1)S(1)} collective-permute-done((bf16[2,384,128]{2,1,0:T(8,128)(2,1)S(1)}, bf16[2,384,128]{2,1,0:T(8,128)(2,1)S(1)}, u32[]{:S(2)}, u32[]{:S(2)}) %collective-permute-start.26) | collective-permute-done | bytes 196640 | tf_op jit(solution)/shard_map/ppermute | solution.py:43
  175.4 2.9 %attend.7.refs_3_ = bf16[384,128]{1,0:T(8,128)(2,1)S(1)} custom-call(f32[3,18]{1,0:T(4,128)S(1)} %and_select_fusion.2.bias, bf16[384,1536]{1,0:T(8,128)(2,1)S(1)} %bitcast.52, bf16[384,1536]{1,0:T(8,128)(2,1)S(1)} %bitcast.39, bf16[384,1536]{1,0:T(8,128)(2,1)S(1)} %bitcast.48, bf16[2,384,1536]{2,1,0:T(8,128)(2,1)} %collective-permute-done.20.a1, ...), custom_call_target="tpu_custom_call" | custom-call | flops 1610612736 | bytes 1507328 | tf_op jit(solution)/shard_map/attend/pallas_call | solution.py:184
  178.3 9.2 %project.1 = bf16[384,3072]{1,0:T(8,128)(2,1)} custom-call(bf16[384,512]{1,0:T(8,128)(2,1)S(1)} %get-tuple-element.235.refs_0_, bf16[384,512]{1,0:T(8,128)(2,1)S(1)} %get-tuple-element.241.refs_1_, bf16[384,384]{1,0:T(8,128)(2,1)S(1)} %attend.6.refs_2_, bf16[384,128]{1,0:T(8,128)(2,1)S(1)} %attend.7.refs_3_, s32[4]{0:T(128)S(1)} %pad_add_fusion.refs_4_, ...), custom_call_target="tpu_custom_call" | custom-call | flops 3623878656 | bytes 14155776 | tf_op jit(solution)/shard_map/project/pallas_call | solution.py:232
  (121 shorter events, 42.1 us)
Async XLA Ops:
  1.1 18.9 %collective-permute-start.18 = (bf16[192,384]{1,0:T(8,128)(2,1)S(1)}, bf16[192,384]{1,0:T(8,128)(2,1)S(1)}, u32[]{:S(2)}, u32[]{:S(2)}) collective-permute-start(bf16[192,384]{1,0:T(8,128)(2,1)S(1)} %dynamic-slice_bitcast_fusion), channel_id=1, source_target_pairs={{0,2},{16,18},{1,3},{17,19},{2,32},{18,48},{3,33},{19,49},{32,34},... | collective-permute-start | bytes 442376 | tf_op jit(solution)/shard_map/ppermute | solution.py:38
  5.7 14.3 %collective-permute-start.17 = (bf16[192,384]{1,0:T(8,128)(2,1)S(1)}, bf16[192,384]{1,0:T(8,128)(2,1)S(1)}, u32[]{:S(2)}, u32[]{:S(2)}) collective-permute-start(bf16[192,384]{1,0:T(8,128)(2,1)S(1)} %dynamic-slice_bitcast_fusion), channel_id=1, source_target_pairs={{0,35},{16,51},{1,0},{17,16},{2,1},{18,17},{3,2},{19,18},{32,3},{4... | collective-permute-start | bytes 442376 | tf_op jit(solution)/shard_map/ppermute | solution.py:38
  5.7 14.3 %collective-permute-start.16 = (bf16[192,384]{1,0:T(8,128)(2,1)S(1)}, bf16[192,384]{1,0:T(8,128)(2,1)S(1)}, u32[]{:S(2)}, u32[]{:S(2)}) collective-permute-start(bf16[192,384]{1,0:T(8,128)(2,1)S(1)} %dynamic-slice_bitcast_fusion), channel_id=1, source_target_pairs={{0,1},{16,17},{1,2},{17,18},{2,3},{18,19},{3,32},{19,48},{32,33},{... | collective-permute-start | bytes 442376 | tf_op jit(solution)/shard_map/ppermute | solution.py:38
  9.3 10.6 %collective-permute-start.19 = (bf16[2,16,1536]{2,1,0:T(8,128)(2,1)S(1)}, bf16[2,16,1536]{2,1,0:T(8,128)(2,1)S(1)}, u32[]{:S(2)}, u32[]{:S(2)}) collective-permute-start(bf16[2,16,1536]{2,1,0:T(8,128)(2,1)S(1)} %pair.10), channel_id=1, source_target_pairs={{0,32},{16,48},{32,0},{48,16},{64,96},{80,112},{96,64},{112,80},{1... | collective-permute-start | bytes 294920 | tf_op jit(solution)/shard_map/ppermute | solution.py:47
  21.3 11.4 %collective-permute-start.20 = (bf16[2,384,1536]{2,1,0:T(8,128)(2,1)S(1)}, bf16[2,384,1536]{2,1,0:T(8,128)(2,1)}, u32[]{:S(2)}, u32[]{:S(2)}) collective-permute-start(bf16[2,384,1536]{2,1,0:T(8,128)(2,1)S(1)} %pair.11), channel_id=1, source_target_pairs={{0,16},{16,0},{1,17},{17,1},{2,18},{18,2},{3,19},{19,3},{32,48},{4... | collective-permute-start | bytes 7077896 | tf_op jit(solution)/shard_map/ppermute | solution.py:38
  21.5 46.7 %collective-permute-start.22 = (bf16[2,384,512]{2,1,0:T(8,128)(2,1)}, bf16[2,384,512]{2,1,0:T(8,128)(2,1)}, u32[]{:S(2)}, u32[]{:S(2)}) collective-permute-start(bf16[2,384,512]{2,1,0:T(8,128)(2,1)} %copy-done.2), channel_id=1, source_target_pairs={{0,32},{16,48},{1,33},{17,49},{2,34},{18,50},{3,35},{19,51},{32,0}... | collective-permute-start | bytes 2359304 | tf_op jit(solution)/shard_map/ppermute | solution.py:38
  34.7 16.2 %collective-permute-start.11 = (bf16[4,192,384]{2,1,0:T(8,128)(2,1)S(1)}, bf16[4,192,384]{2,1,0:T(8,128)(2,1)S(1)}, u32[]{:S(2)}, u32[]{:S(2)}) collective-permute-start(bf16[4,192,384]{2,1,0:T(8,128)(2,1)S(1)} %place.2.refs_0_), channel_id=1, source_target_pairs={{0,4},{16,20},{1,5},{17,21},{2,6},{18,22},{3,7},{19,23},{32,36},{4... | collective-permute-start | bytes 1769480 | tf_op jit(solution)/shard_map/cond/branch_1_fun/ppermute | solution.py:38
  36.4 23.4 %collective-permute-start.13 = (bf16[4,192,384]{2,1,0:T(8,128)(2,1)S(1)}, bf16[4,192,384]{2,1,0:T(8,128)(2,1)S(1)}, u32[]{:S(2)}, u32[]{:S(2)}) collective-permute-start(bf16[4,192,384]{2,1,0:T(8,128)(2,1)S(1)} %place.2.refs_0_), channel_id=1, source_target_pairs={{0,8},{16,24},{1,9},{17,25},{2,10},{18,26},{3,11},{19,27},{32,40},... | collective-permute-start | bytes 1769480 | tf_op jit(solution)/shard_map/cond/branch_1_fun/ppermute | solution.py:38
  37.3 27.6 %collective-permute-start.12 = (bf16[4,192,384]{2,1,0:T(8,128)(2,1)S(1)}, bf16[4,192,384]{2,1,0:T(8,128)(2,1)S(1)}, u32[]{:S(2)}, u32[]{:S(2)}) collective-permute-start(bf16[4,192,384]{2,1,0:T(8,128)(2,1)S(1)} %place.2.refs_0_), channel_id=1, source_target_pairs={{0,12},{16,28},{1,13},{17,29},{2,14},{18,30},{3,15},{19,31},{32,44... | collective-permute-start | bytes 1769480 | tf_op jit(solution)/shard_map/cond/branch_1_fun/ppermute | solution.py:38
  56.7 10.6 %collective-permute-start.15 = (bf16[2,64,1536]{2,1,0:T(8,128)(2,1)S(1)}, bf16[2,64,1536]{2,1,0:T(8,128)(2,1)S(1)}, u32[]{:S(2)}, u32[]{:S(2)}) collective-permute-start(bf16[2,64,1536]{2,1,0:T(8,128)(2,1)S(1)} %join.5.refs_0_), channel_id=1, source_target_pairs={{0,128},{16,144},{32,160},{48,176},{64,192},{80,208},{96,224},{112... | collective-permute-start | bytes 1179656 | tf_op jit(solution)/shard_map/cond/branch_1_fun/ppermute | solution.py:47
  68.2 66.8 %collective-permute-start.24 = (bf16[3072,384]{1,0:T(8,128)(2,1)}, bf16[3072,384]{1,0:T(8,128)(2,1)}, u32[]{:S(2)}, u32[]{:S(2)}) collective-permute-start(bf16[3072,384]{1,0:T(8,128)(2,1)} %get-tuple-element.234.refs_5_), channel_id=1, source_target_pairs={{0,192},{16,208},{32,96},{48,112},{64,0},{80,16},{96,160},{112,176... | collective-permute-start | bytes 7077896 | tf_op jit(solution)/shard_map/ppermute | solution.py:52
  70.9 37.0 %collective-permute-start.21 = (bf16[2,384,512]{2,1,0:T(8,128)(2,1)S(1)}, bf16[2,384,512]{2,1,0:T(8,128)(2,1)}, u32[]{:S(2)}, u32[]{:S(2)}) collective-permute-start(bf16[2,384,512]{2,1,0:T(8,128)(2,1)S(1)} %copy-done.4), channel_id=1, source_target_pairs={{0,32},{16,48},{1,33},{17,49},{2,34},{18,50},{3,35},{19,51},{32,0}... | collective-permute-start | bytes 2359304 | tf_op jit(solution)/shard_map/ppermute | solution.py:38
  71.0 20.0 %collective-permute-start = (bf16[2,384,512]{2,1,0:T(8,128)(2,1)}, bf16[2,384,512]{2,1,0:T(8,128)(2,1)}, u32[]{:S(2)}, u32[]{:S(2)}) collective-permute-start(bf16[2,384,512]{2,1,0:T(8,128)(2,1)} %get-tuple-element.129), channel_id=1, source_target_pairs={{0,64},{16,80},{32,224},{48,240},{64,128},{80,144},{96,32},{112,48... | collective-permute-start | bytes 2359304 | tf_op jit(solution)/shard_map/cond/branch_1_fun/ppermute | solution.py:43
  71.6 19.4 %collective-permute-start.3 = (bf16[2,128,1536]{2,1,0:T(8,128)(2,1)}, bf16[2,128,1536]{2,1,0:T(8,128)(2,1)S(1)}, u32[]{:S(2)}, u32[]{:S(2)}) collective-permute-start(bf16[2,128,1536]{2,1,0:T(8,128)(2,1)} %get-tuple-element.130.refs_0_), channel_id=1, source_target_pairs={{0,16},{16,0},{32,48},{48,32},{64,80},{80,64},{96,112},{112,96},{1... | collective-permute-start | bytes 2359304 | tf_op jit(solution)/shard_map/cond/branch_1_fun/ppermute | solution.py:47
  71.6 21.8 %collective-permute-start.1 = (bf16[2,384,512]{2,1,0:T(8,128)(2,1)}, bf16[2,384,512]{2,1,0:T(8,128)(2,1)}, u32[]{:S(2)}, u32[]{:S(2)}) collective-permute-start(bf16[2,384,512]{2,1,0:T(8,128)(2,1)} %get-tuple-element.129), channel_id=1, source_target_pairs={{0,16},{16,0},{1,17},{17,1},{2,18},{18,2},{3,19},{19,3},{32,48},{4... | collective-permute-start | bytes 2359304 | tf_op jit(solution)/shard_map/cond/branch_1_fun/ppermute | solution.py:38
  108.0 27.1 %collective-permute-start.23 = (bf16[2,384,384]{2,1,0:T(8,128)(2,1)S(1)}, bf16[2,384,384]{2,1,0:T(8,128)(2,1)}, u32[]{:S(2)}, u32[]{:S(2)}) collective-permute-start(bf16[2,384,384]{2,1,0:T(8,128)(2,1)S(1)} %pair.7), channel_id=1, source_target_pairs={{0,32},{16,48},{1,33},{17,49},{2,34},{18,50},{3,35},{19,51},{32,0}... | collective-permute-start | bytes 1769480 | tf_op jit(solution)/shard_map/ppermute | solution.py:38
  110.4 20.7 %collective-permute-start.4 = (bf16[2,384,512]{2,1,0:T(8,128)(2,1)}, bf16[2,384,512]{2,1,0:T(8,128)(2,1)}, u32[]{:S(2)}, u32[]{:S(2)}) collective-permute-start(bf16[2,384,512]{2,1,0:T(8,128)(2,1)} %get-tuple-element.131), channel_id=1, source_target_pairs={{0,64},{16,80},{32,224},{48,240},{64,128},{80,144},{96,32},{112,48... | collective-permute-start | bytes 2359304 | tf_op jit(solution)/shard_map/cond/branch_1_fun/ppermute | solution.py:43
  111.0 20.1 %collective-permute-start.5 = (bf16[2,384,512]{2,1,0:T(8,128)(2,1)}, bf16[2,384,512]{2,1,0:T(8,128)(2,1)}, u32[]{:S(2)}, u32[]{:S(2)}) collective-permute-start(bf16[2,384,512]{2,1,0:T(8,128)(2,1)} %get-tuple-element.131), channel_id=1, source_target_pairs={{0,16},{16,0},{1,17},{17,1},{2,18},{18,2},{3,19},{19,3},{32,48},{4... | collective-permute-start | bytes 2359304 | tf_op jit(solution)/shard_map/cond/branch_1_fun/ppermute | solution.py:38
  135.1 27.4 %collective-permute-start.25 = (bf16[2,384,128]{2,1,0:T(8,128)(2,1)S(1)}, bf16[2,384,128]{2,1,0:T(8,128)(2,1)S(1)}, u32[]{:S(2)}, u32[]{:S(2)}) collective-permute-start(bf16[2,384,128]{2,1,0:T(8,128)(2,1)S(1)} %copy-done.6), channel_id=1, source_target_pairs={{0,32},{16,48},{1,33},{17,49},{2,34},{18,50},{3,35},{19,51},{32,0}... | collective-permute-start | bytes 589832 | tf_op jit(solution)/shard_map/ppermute | solution.py:38
  138.7 23.8 %collective-permute-start.9 = (bf16[3072,384]{1,0:T(8,128)(2,1)}, bf16[3072,384]{1,0:T(8,128)(2,1)}, u32[]{:S(2)}, u32[]{:S(2)}) collective-permute-start(bf16[3072,384]{1,0:T(8,128)(2,1)} %get-tuple-element.157), channel_id=1, source_target_pairs={{0,16},{16,0},{1,17},{17,1},{2,18},{18,2},{3,19},{19,3},{32,48},{4... | collective-permute-start | bytes 7077896 | tf_op jit(solution)/shard_map/cond/branch_1_fun/ppermute | solution.py:38
  138.7 23.7 %collective-permute-start.10 = (bf16[3072,384]{1,0:T(8,128)(2,1)}, bf16[3072,384]{1,0:T(8,128)(2,1)}, u32[]{:S(2)}, u32[]{:S(2)}) collective-permute-start(bf16[3072,384]{1,0:T(8,128)(2,1)} %get-tuple-element.158), channel_id=1, source_target_pairs={{0,16},{16,0},{1,17},{17,1},{2,18},{18,2},{3,19},{19,3},{32,48},{4... | collective-permute-start | bytes 7077896 | tf_op jit(solution)/shard_map/cond/branch_1_fun/ppermute | solution.py:38
  139.2 16.9 %collective-permute-start.7 = (bf16[2,384,384]{2,1,0:T(8,128)(2,1)}, bf16[2,384,384]{2,1,0:T(8,128)(2,1)}, u32[]{:S(2)}, u32[]{:S(2)}) collective-permute-start(bf16[2,384,384]{2,1,0:T(8,128)(2,1)} %get-tuple-element.144.near), channel_id=1, source_target_pairs={{0,64},{16,80},{32,224},{48,240},{64,128},{80,144},{96,32},{112,48... | collective-permute-start | bytes 1769480 | tf_op jit(solution)/shard_map/cond/branch_1_fun/ppermute | solution.py:43
  162.7 7.9 %collective-permute-start.27 = (bf16[2,384,128]{2,1,0:T(8,128)(2,1)S(1)}, bf16[2,384,128]{2,1,0:T(8,128)(2,1)S(1)}, u32[]{:S(2)}, u32[]{:S(2)}) collective-permute-start(bf16[2,384,128]{2,1,0:T(8,128)(2,1)S(1)} %collective-permute-done.25.b0), channel_id=1, source_target_pairs={{0,80},{16,64},{32,240},{48,224},{64,144},{80,128},{96,48},{112,32... | collective-permute-start | bytes 589832 | tf_op jit(solution)/shard_map/ppermute | solution.py:43
  162.7 12.6 %collective-permute-start.26 = (bf16[2,384,128]{2,1,0:T(8,128)(2,1)S(1)}, bf16[2,384,128]{2,1,0:T(8,128)(2,1)S(1)}, u32[]{:S(2)}, u32[]{:S(2)}) collective-permute-start(bf16[2,384,128]{2,1,0:T(8,128)(2,1)S(1)} %collective-permute-done.25.b0), channel_id=1, source_target_pairs={{0,64},{16,80},{32,224},{48,240},{64,128},{80,144},{96,32},{112,48... | collective-permute-start | bytes 589832 | tf_op jit(solution)/shard_map/ppermute | solution.py:43
  (30 other events, 263.5 us)

commit v2 on v1

--- a/solution.py
+++ b/solution.py
@@ -17,7 +17,7 @@
 PANEL = 192
 D = 3072
 TEXT = 256
-GROUPS = (4, 4, 3, 1)
+GROUPS = (6, 3, 2, 1)
 NEG = -1e30
 SCALE = HD**-0.5 * 1.4426950408889634
 AXES = ("seq", "fsdp")
@@ -70,23 +70,6 @@
         ),
         name="join",
     )(*pieces)
-
-
-def merge_kernel(near, far, out):
-    out[:2] = near[...]
-    out[2:] = far[...]
-
-
-def merge(near, far):
-    return pl.pallas_call(
-        merge_kernel,
-        grid=(near.shape[2] // HD,),
-        out_shape=jax.ShapeDtypeStruct((4,) + near.shape[1:], jnp.bfloat16),
-        in_specs=[pl.BlockSpec((2, ROWS, HD), lambda i: (0, 0, i))] * 2,
-        out_specs=pl.BlockSpec((4, ROWS, HD), lambda i: (0, 0, i)),
-        cost_estimate=pl.CostEstimate(flops=0, bytes_accessed=8 * near.size, transcendentals=0),
-        name="merge",
-    )(near, far)
 
 
 def pair_kernel(k, v, out):
@@ -174,11 +157,10 @@
         out[t * TILE : (t + 1) * TILE, :] = (acc / row).astype(jnp.bfloat16)
 
 
-def attend(bias, q, k0, v0, beside, near, far, text, first, count, merged=False):
+def attend(bias, q, k0, v0, beside, near, far, text, first, count):
     wide = pl.BlockSpec((ROWS, HD), lambda i: (0, first + i))
     words = pl.BlockSpec((2, TEXT, HD), lambda i: (0, 0, first + i))
     pack = pl.BlockSpec((2, ROWS, HD), lambda i: (0, 0, i))
-    upper = pl.BlockSpec((2, ROWS, HD), lambda i: (1, 0, i))
     whole = pl.BlockSpec((2, ROWS, HD), lambda i: (0, 0, first + i))
     units = 48 * count
     return pl.pallas_call(
@@ -188,8 +170,7 @@
         in_specs=[pl.BlockSpec(memory_space=pltpu.SMEM)]
         + [wide] * 3
         + [whole]
-        + [pack] * 3
-        + [upper if merged else pack]
+        + [pack] * 4
         + [words],
         out_specs=pl.BlockSpec((ROWS, HD), lambda i: (0, i)),
         compiler_params=pltpu.CompilerParams(vmem_limit_bytes=14 * 1024 * 1024),
@@ -298,19 +279,18 @@
     firsts = [sum(GROUPS[:g]) for g in range(len(GROUPS))]
     packs = [pair(k0, v0, first, count) for first, count in zip(firsts, GROUPS)]
 
-    def attend_group(g, near, others, far, text, far_other=None):
+    def attend_group(g, near, near_other, far, text, far_other):
         return attend(
             bias,
             q,
             k0,
             v0,
             beside,
-            (near, others),
-            (far, others if far_other is None else far_other),
+            (near, near_other),
+            (far, far_other),
             text,
             firsts[g],
             GROUPS[g],
-            far_other is None,
         )
 
     text = pair(text_keys[0], text_values[0], 0, 1, HID)
@@ -376,15 +356,15 @@
         ready, second_stage, near1, near0, near0_other, far0, far0_other, text
     )
 
-    def third_stage(near2, near1, near1_other, far1, far1_other, text, wy, wx):
+    def third_stage(near2, near1, near1_other, far1, far1_other, text, wy):
         part1 = attend_group(1, near1, near1_other, far1, text, far1_other)
-        wb, wd = shift(wy, dc=1), shift(wx, dc=1)
+        near2_other, wb = shift(near2, dc=1), shift(wy, dc=1)
         far2, part1 = lax.optimization_barrier((forward(near2), part1))
-        return part1, far2, shift(merge(near2, far2), dc=1), wb, wd
-
-    pack3, near2, part0, wx = lax.optimization_barrier((packs[3], near2, part0, wx))
+        return part1, near2_other, far2, shift(far2, dc=1), wb
+
+    pack3, near2, part0 = lax.optimization_barrier((packs[3], near2, part0))
     near3 = shift(pack3, dz=4)
-    part1, far2, others2, wb, wd = stage(
+    part1, near2_other, far2, far2_other, wb = stage(
         ready,
         third_stage,
         near2,
@@ -394,10 +374,10 @@
         far1_other,
         text,
         wy,
-        wx,
-    )
-    near3, others2 = lax.optimization_barrier((near3, others2))
-    part2 = attend_group(2, near2, others2, far2, text)
+    )
+    near3, near2_other, wx = lax.optimization_barrier((near3, near2_other, wx))
+    wd = shift(wx, dc=1)
+    part2 = attend_group(2, near2, near2_other, far2, text, far2_other)
     far3, far3_other, near3_other, part2 = lax.optimization_barrier(
         (forward(near3), forward(near3, flip=1), shift(near3, dc=1), part2)
     )

time: 190 us -> 186 us (0.979)
  Pallas kernels: 53.5 us -> 49.6 us
  local copies, waits for them, and re-layouts: 5.32 us -> 8.11 us
  waiting for transfers between devices: 91.4 us -> 89.4 us
    ppermute x19 -> x20, waiting for transfers between devices: 37.3 us -> 32.7 us  [shift(): return lax.ppermute(value, AXES, pairs)]
    pallas_call x1 -> x0, Pallas kernels: 3.18 us -> none  [merge(): pl.pallas_call(merge_kernel, grid=(near.shape[2] // HD,), out_shape=jax.S...]
    ppermute x4, waiting for transfers between devices: 11.4 us -> 14.1 us  [swap(): return lax.ppermute(value, 'seq', [(s, s ^ bit) for s in range(16)])]
    unnamed x51 -> x57, local copies, waits for them, and re-layouts: 4.31 us -> 7.06 us
    ppermute x19 -> x20, starting transfers between devices: 24.6 us -> 24 us  [shift(): return lax.ppermute(value, AXES, pairs)]
  transfers between devices with their start and end apart: 29 -> 30, of which waited for: 15 -> 14; matrix products, arithmetic and copies ran while one was open for 1% -> 1% of each run, Pallas kernels for 21% -> 22%
where the time goes in v2:
time: 186 us; the launch traced here: 184 us
  waiting for transfers between devices  89.4 us (48%)
  Pallas kernels  49.6 us (27%)
  starting transfers between devices  35.2 us (19%)
  local copies, waits for them, and re-layouts  8.11 us (4%)
    ppermute x5, waiting for transfers between devices, forward(): return lax.ppermute(value, 'seq', pairs)  42.5 us
    ppermute x20, waiting for transfers between devices, shift(): return lax.ppermute(value, AXES, pairs)  32.7 us
    pallas_call x4, Pallas kernels, attend(): pl.pallas_call(attend_kernel, grid=(count,), out_shape=jax.ShapeDtypeStru...  28.5 us
    ppermute x20, starting transfers between devices, shift(): return lax.ppermute(value, AXES, pairs)  24 us
    ppermute x4, waiting for transfers between devices, swap(): return lax.ppermute(value, 'seq', [(s, s ^ bit) for s in range(16)])  14.1 us
    pallas_call x1, Pallas kernels, project(): pl.pallas_call(project_kernel, grid=(D // step,), out_shape=jax.ShapeDtyp...  8.32 us
    unnamed x57, local copies, waits for them, and re-layouts  7.06 us
    ppermute x4, starting transfers between devices, swap(): return lax.ppermute(value, 'seq', [(s, s ^ bit) for s in range(16)])  6.65 us
  transfers between devices with their start and end apart: 30, of which 14 were waited for; matrix products, arithmetic and copies ran while one was open for 1% of the time, Pallas kernels for 22%

profile of v2, /device:TPU:72, one launch (start us, length us, event | category | flops | bytes accessed | tf_op | source)
XLA Modules:
  0.0 184.5 jit_solution(16952146429827449085)
XLA Ops:
  3.2 5.7 %collective-permute-start.18 = (bf16[192,384]{1,0:T(8,128)(2,1)S(1)}, bf16[192,384]{1,0:T(8,128)(2,1)S(1)}, u32[]{:S(2)}, u32[]{:S(2)}) collective-permute-start(bf16[192,384]{1,0:T(8,128)(2,1)S(1)} %dynamic-slice_bitcast_fusion), channel_id=1, source_target_pairs={{0,2},{16,18},{1,3},{17,19},{2,32},{18,48},{3,33},{19,49},{32,34},... | collective-permute-start | bytes 442376 | tf_op jit(solution)/shard_map/ppermute | solution.py:38
  12.0 4.7 %pair.9 = bf16[2,384,768]{2,1,0:T(8,128)(2,1)} custom-call(bf16[384,1536]{1,0:T(8,128)(2,1)} %bitcast.31, bf16[384,1536]{1,0:T(8,128)(2,1)} %bitcast.40), custom_call_target="tpu_custom_call" | custom-call | bytes 2359296 | tf_op jit(solution)/shard_map/pair/pallas_call | solution.py:82
  16.7 5.0 %collective-permute-done.19 = bf16[2,16,1536]{2,1,0:T(8,128)(2,1)S(1)} collective-permute-done((bf16[2,16,1536]{2,1,0:T(8,128)(2,1)S(1)}, bf16[2,16,1536]{2,1,0:T(8,128)(2,1)S(1)}, u32[]{:S(2)}, u32[]{:S(2)}) %collective-permute-start.19) | collective-permute-done | bytes 98336 | tf_op jit(solution)/shard_map/ppermute | solution.py:47
  23.1 3.5 %collective-permute-start.22 = (bf16[2,384,768]{2,1,0:T(8,128)(2,1)}, bf16[2,384,768]{2,1,0:T(8,128)(2,1)}, u32[]{:S(2)}, u32[]{:S(2)}) collective-permute-start(bf16[2,384,768]{2,1,0:T(8,128)(2,1)} %pair.9), channel_id=1, source_target_pairs={{0,32},{16,48},{1,33},{17,49},{2,34},{18,50},{3,35},{19,51},{32,0}... | collective-permute-start | bytes 3538952 | tf_op jit(solution)/shard_map/ppermute | solution.py:38
  30.8 35.4 %conditional.4 = (bf16[3072,384]{1,0:T(8,128)(2,1)S(1)}, bf16[2,128,1536]{2,1,0:T(8,128)(2,1)}) conditional(s32[]{:T(128)} %bitcast.12, () %tuple.56, (s32[]{:T(128)}, s32[]{:T(128)}, (), bf16[192,384]{1,0:T(8,128)(2,1)}, bf16[192,384]{1,0:T(8,128)(2,1)}, /*index=5*/bf16[192,384]{1,0:T(8,128)(2,1)}, bf16[192,384]{1,0:T(8,128)(2,1)}, ...), branch_computations={%region_1.2_spmd, %region_2.3_spmd} | conditional | flops 115 | bytes 18088396 | solution.py:241
  38.1 10.9 %collective-permute-done.11.refs_1_ = bf16[4,192,384]{2,1,0:T(8,128)(2,1)S(1)} collective-permute-done((bf16[4,192,384]{2,1,0:T(8,128)(2,1)S(1)}, bf16[4,192,384]{2,1,0:T(8,128)(2,1)S(1)}, u32[]{:S(2)}, u32[]{:S(2)}) %collective-permute-start.11) | collective-permute-done | bytes 589856 | tf_op jit(solution)/shard_map/cond/branch_1_fun/ppermute | solution.py:38
  50.5 4.2 %collective-permute-done.14.refs_1_ = bf16[2,32,1536]{2,1,0:T(8,128)(2,1)S(1)} collective-permute-done((bf16[2,32,1536]{2,1,0:T(8,128)(2,1)S(1)}, bf16[2,32,1536]{2,1,0:T(8,128)(2,1)S(1)}, u32[]{:S(2)}, u32[]{:S(2)}) %collective-permute-start.14) | collective-permute-done | bytes 196640 | tf_op jit(solution)/shard_map/cond/branch_1_fun/ppermute | solution.py:47
  54.7 3.1 %collective-permute-start.15 = (bf16[2,64,1536]{2,1,0:T(8,128)(2,1)S(1)}, bf16[2,64,1536]{2,1,0:T(8,128)(2,1)S(1)}, u32[]{:S(2)}, u32[]{:S(2)}) collective-permute-start(bf16[2,64,1536]{2,1,0:T(8,128)(2,1)S(1)} %join.5.refs_0_), channel_id=1, source_target_pairs={{0,128},{16,144},{32,160},{48,176},{64,192},{80,208},{96,224},{112... | collective-permute-start | bytes 1179656 | tf_op jit(solution)/shard_map/cond/branch_1_fun/ppermute | solution.py:47
  57.8 5.0 %collective-permute-done.13.refs_3_ = bf16[4,192,384]{2,1,0:T(8,128)(2,1)S(1)} collective-permute-done((bf16[4,192,384]{2,1,0:T(8,128)(2,1)S(1)}, bf16[4,192,384]{2,1,0:T(8,128)(2,1)S(1)}, u32[]{:S(2)}, u32[]{:S(2)}) %collective-permute-start.13) | collective-permute-done | bytes 589856 | tf_op jit(solution)/shard_map/cond/branch_1_fun/ppermute | solution.py:38
  67.6 12.4 %collective-permute-done.22 = bf16[2,384,768]{2,1,0:T(8,128)(2,1)} collective-permute-done((bf16[2,384,768]{2,1,0:T(8,128)(2,1)}, bf16[2,384,768]{2,1,0:T(8,128)(2,1)}, u32[]{:S(2)}, u32[]{:S(2)}) %collective-permute-start.22) | collective-permute-done | bytes 1179680 | tf_op jit(solution)/shard_map/ppermute | solution.py:38
  80.0 2.8 %collective-permute-start.25 = (bf16[3072,384]{1,0:T(8,128)(2,1)}, bf16[3072,384]{1,0:T(8,128)(2,1)S(1)}, u32[]{:S(2)}, u32[]{:S(2)}) collective-permute-start(bf16[3072,384]{1,0:T(8,128)(2,1)} %copy-done.13), channel_id=1, source_target_pairs={{0,192},{16,208},{32,96},{48,112},{64,0},{80,16},{96,160},{112,176... | collective-permute-start | bytes 7077896 | tf_op jit(solution)/shard_map/ppermute | solution.py:52
  84.9 35.1 %conditional.5 = (bf16[2,384,768]{2,1,0:T(8,128)(2,1)}, bf16[2,384,768]{2,1,0:T(8,128)(2,1)}, bf16[2,384,768]{2,1,0:T(8,128)(2,1)}, bf16[2,256,1536]{2,1,0:T(8,128)(2,1)}) conditional(s32[]{:T(128)} %bitcast.12, () %tuple.59, (bf16[2,384,768]{2,1,0:T(8,128)(2,1)}, bf16[2,128,1536]{2,1,0:T(8,128)(2,1)}) %tuple.61), branch_computations={%region_3.4_spmd, %region_4.5_spmd} | conditional | bytes 20447424 | solution.py:241
  86.4 27.4 %collective-permute-done = bf16[2,384,768]{2,1,0:T(8,128)(2,1)} collective-permute-done((bf16[2,384,768]{2,1,0:T(8,128)(2,1)}, bf16[2,384,768]{2,1,0:T(8,128)(2,1)}, u32[]{:S(2)}, u32[]{:S(2)}) %collective-permute-start) | collective-permute-done | bytes 1179680 | tf_op jit(solution)/shard_map/cond/branch_1_fun/ppermute | solution.py:43
  114.3 3.3 %collective-permute-done.3.refs_1_ = bf16[2,128,1536]{2,1,0:T(8,128)(2,1)S(1)} collective-permute-done((bf16[2,128,1536]{2,1,0:T(8,128)(2,1)}, bf16[2,128,1536]{2,1,0:T(8,128)(2,1)S(1)}, u32[]{:S(2)}, u32[]{:S(2)}) %collective-permute-start.3) | collective-permute-done | bytes 786464 | tf_op jit(solution)/shard_map/cond/branch_1_fun/ppermute | solution.py:47
  122.7 19.2 %conditional.6 = (bf16[384,768]{1,0:T(8,128)(2,1)S(1)}, bf16[2,384,384]{2,1,0:T(8,128)(2,1)}, bf16[2,384,384]{2,1,0:T(8,128)(2,1)}, bf16[2,384,384]{2,1,0:T(8,128)(2,1)}) conditional(s32[]{:T(128)} %bitcast.12, () %tuple.63, (bf16[2,384,384]{2,1,0:T(8,128)(2,1)}, f32[3,18]{1,0:T(4,128)S(1)}, bf16[384,1536]{1,0:T(8,128)(2,1)}, ...), branch_computations={%region_5.6_spmd, %region_6.7_spmd} | conditional | flops 9663676416 | bytes 16122008 | solution.py:241
  122.7 12.9 %attend.4 = bf16[384,768]{1,0:T(8,128)(2,1)S(1)} custom-call(f32[3,18]{1,0:T(4,128)S(1)} %get-tuple-element.130.bias, bf16[384,1536]{1,0:T(8,128)(2,1)} %get-tuple-element.131.q, bf16[384,1536]{1,0:T(8,128)(2,1)} %get-tuple-element.132.k0, bf16[384,1536]{1,0:T(8,128)(2,1)} %get-tuple-element.133.v0, bf16[2,384,1536]{2,1,0:T(8,128)(2,1)} %get-tuple-element.134.a1, ...), custom_call_target="tpu_custom_call" | custom-call | flops 9663676416 | bytes 9043968 | tf_op jit(solution)/shard_map/cond/branch_1_fun/attend/pallas_call | solution.py:166
  135.6 3.9 %collective-permute-done.4 = bf16[2,384,384]{2,1,0:T(8,128)(2,1)} collective-permute-done((bf16[2,384,384]{2,1,0:T(8,128)(2,1)}, bf16[2,384,384]{2,1,0:T(8,128)(2,1)}, u32[]{:S(2)}, u32[]{:S(2)}) %collective-permute-start.4) | collective-permute-done | bytes 589856 | tf_op jit(solution)/shard_map/cond/branch_1_fun/ppermute | solution.py:43
  144.8 15.1 %conditional.7 = (bf16[384,384]{1,0:T(8,128)(2,1)S(1)}, bf16[2,384,256]{2,1,0:T(8,128)(2,1)}, bf16[2,384,256]{2,1,0:T(8,128)(2,1)}, bf16[2,384,256]{2,1,0:T(8,128)(2,1)}, bf16[3072,384]{1,0:T(8,128)(2,1)}) conditional(s32[]{:T(128)} %bitcast.12, () %tuple.66, (bf16[2,384,256]{2,1,0:T(8,128)(2,1)}, f32[3,18]{1,0:T(4,128)S(1)}, ...), branch_computations={%region_7.8_spmd, %region_8.9_spmd} | conditional | flops 4831838208 | bytes 18677960 | solution.py:241
  145.3 7.2 %attend.5 = bf16[384,384]{1,0:T(8,128)(2,1)S(1)} custom-call(f32[3,18]{1,0:T(4,128)S(1)} %get-tuple-element.143.bias, bf16[384,1536]{1,0:T(8,128)(2,1)} %get-tuple-element.144.q, bf16[384,1536]{1,0:T(8,128)(2,1)} %get-tuple-element.145.k0, bf16[384,1536]{1,0:T(8,128)(2,1)} %get-tuple-element.146.v0, bf16[2,384,1536]{2,1,0:T(8,128)(2,1)} %get-tuple-element.147.a1, ...), custom_call_target="tpu_custom_call" | custom-call | flops 4831838208 | bytes 4521984 | tf_op jit(solution)/shard_map/cond/branch_1_fun/attend/pallas_call | solution.py:166
  152.5 5.4 %collective-permute-done.7 = bf16[2,384,256]{2,1,0:T(8,128)(2,1)} collective-permute-done((bf16[2,384,256]{2,1,0:T(8,128)(2,1)}, bf16[2,384,256]{2,1,0:T(8,128)(2,1)}, u32[]{:S(2)}, u32[]{:S(2)}) %collective-permute-start.7) | collective-permute-done | bytes 393248 | tf_op jit(solution)/shard_map/cond/branch_1_fun/ppermute | solution.py:43
  161.7 5.4 %attend.6.refs_2_ = bf16[384,256]{1,0:T(8,128)(2,1)S(1)} custom-call(f32[3,18]{1,0:T(4,128)S(1)} %and_select_fusion.2.bias, bf16[384,1536]{1,0:T(8,128)(2,1)} %bitcast.52, bf16[384,1536]{1,0:T(8,128)(2,1)} %bitcast.34, bf16[384,1536]{1,0:T(8,128)(2,1)} %bitcast.43, bf16[2,384,1536]{2,1,0:T(8,128)(2,1)} %collective-permute-done.20.a1, ...), custom_call_target="tpu_custom_call" | custom-call | flops 3221225472 | bytes 3014656 | tf_op jit(solution)/shard_map/attend/pallas_call | solution.py:166
  169.9 3.1 %collective-permute-done.27.c1 = bf16[2,384,128]{2,1,0:T(8,128)(2,1)S(1)} collective-permute-done((bf16[2,384,128]{2,1,0:T(8,128)(2,1)S(1)}, bf16[2,384,128]{2,1,0:T(8,128)(2,1)S(1)}, u32[]{:S(2)}, u32[]{:S(2)}) %collective-permute-start.27) | collective-permute-done | bytes 196640 | tf_op jit(solution)/shard_map/ppermute | solution.py:43
  173.0 3.1 %attend.7.refs_3_ = bf16[384,128]{1,0:T(8,128)(2,1)S(1)} custom-call(f32[3,18]{1,0:T(4,128)S(1)} %and_select_fusion.2.bias, bf16[384,1536]{1,0:T(8,128)(2,1)S(1)} %bitcast.53, bf16[384,1536]{1,0:T(8,128)(2,1)S(1)} %bitcast.39, bf16[384,1536]{1,0:T(8,128)(2,1)S(1)} %bitcast.48, bf16[2,384,1536]{2,1,0:T(8,128)(2,1)} %collective-permute-done.20.a1, ...), custom_call_target="tpu_custom_call" | custom-call | flops 1610612736 | bytes 1507328 | tf_op jit(solution)/shard_map/attend/pallas_call | solution.py:166
  176.2 8.3 %project.1 = bf16[384,3072]{1,0:T(8,128)(2,1)} custom-call(bf16[384,768]{1,0:T(8,128)(2,1)S(1)} %copy-done.16, bf16[384,384]{1,0:T(8,128)(2,1)S(1)} %copy-done.19, bf16[384,256]{1,0:T(8,128)(2,1)S(1)} %attend.6.refs_2_, bf16[384,128]{1,0:T(8,128)(2,1)S(1)} %attend.7.refs_3_, s32[4]{0:T(128)S(1)} %pad_add_fusion.refs_4_, bf16[3072,384]{1,0:T(8,128)(2,1)S(1)} %copy-done.14, ...), custom_call_target="tpu_custom_call" | custom-call | flops 3623878656 | bytes 14155776 | tf_op jit(solution)/shard_map/project/pallas_call | solution.py:213
  (128 shorter events, 46.3 us)
Async XLA Ops:
  1.1 20.6 %collective-permute-start.16 = (bf16[192,384]{1,0:T(8,128)(2,1)S(1)}, bf16[192,384]{1,0:T(8,128)(2,1)S(1)}, u32[]{:S(2)}, u32[]{:S(2)}) collective-permute-start(bf16[192,384]{1,0:T(8,128)(2,1)S(1)} %dynamic-slice_bitcast_fusion), channel_id=1, source_target_pairs={{0,1},{16,17},{1,2},{17,18},{2,3},{18,19},{3,32},{19,48},{32,33},{... | collective-permute-start | bytes 442376 | tf_op jit(solution)/shard_map/ppermute | solution.py:38
  3.1 18.6 %collective-permute-start.17 = (bf16[192,384]{1,0:T(8,128)(2,1)S(1)}, bf16[192,384]{1,0:T(8,128)(2,1)S(1)}, u32[]{:S(2)}, u32[]{:S(2)}) collective-permute-start(bf16[192,384]{1,0:T(8,128)(2,1)S(1)} %dynamic-slice_bitcast_fusion), channel_id=1, source_target_pairs={{0,35},{16,51},{1,0},{17,16},{2,1},{18,17},{3,2},{19,18},{32,3},{4... | collective-permute-start | bytes 442376 | tf_op jit(solution)/shard_map/ppermute | solution.py:38
  3.2 18.5 %collective-permute-start.18 = (bf16[192,384]{1,0:T(8,128)(2,1)S(1)}, bf16[192,384]{1,0:T(8,128)(2,1)S(1)}, u32[]{:S(2)}, u32[]{:S(2)}) collective-permute-start(bf16[192,384]{1,0:T(8,128)(2,1)S(1)} %dynamic-slice_bitcast_fusion), channel_id=1, source_target_pairs={{0,2},{16,18},{1,3},{17,19},{2,32},{18,48},{3,33},{19,49},{32,34},... | collective-permute-start | bytes 442376 | tf_op jit(solution)/shard_map/ppermute | solution.py:38
  10.5 11.2 %collective-permute-start.19 = (bf16[2,16,1536]{2,1,0:T(8,128)(2,1)S(1)}, bf16[2,16,1536]{2,1,0:T(8,128)(2,1)S(1)}, u32[]{:S(2)}, u32[]{:S(2)}) collective-permute-start(bf16[2,16,1536]{2,1,0:T(8,128)(2,1)S(1)} %pair.10), channel_id=1, source_target_pairs={{0,32},{16,48},{32,0},{48,16},{64,96},{80,112},{96,64},{112,80},{1... | collective-permute-start | bytes 294920 | tf_op jit(solution)/shard_map/ppermute | solution.py:47
  23.1 56.9 %collective-permute-start.22 = (bf16[2,384,768]{2,1,0:T(8,128)(2,1)}, bf16[2,384,768]{2,1,0:T(8,128)(2,1)}, u32[]{:S(2)}, u32[]{:S(2)}) collective-permute-start(bf16[2,384,768]{2,1,0:T(8,128)(2,1)} %pair.9), channel_id=1, source_target_pairs={{0,32},{16,48},{1,33},{17,49},{2,34},{18,50},{3,35},{19,51},{32,0}... | collective-permute-start | bytes 3538952 | tf_op jit(solution)/shard_map/ppermute | solution.py:38
  32.7 16.2 %collective-permute-start.11 = (bf16[4,192,384]{2,1,0:T(8,128)(2,1)S(1)}, bf16[4,192,384]{2,1,0:T(8,128)(2,1)S(1)}, u32[]{:S(2)}, u32[]{:S(2)}) collective-permute-start(bf16[4,192,384]{2,1,0:T(8,128)(2,1)S(1)} %place.2.refs_0_), channel_id=1, source_target_pairs={{0,4},{16,20},{1,5},{17,21},{2,6},{18,22},{3,7},{19,23},{32,36},{4... | collective-permute-start | bytes 1769480 | tf_op jit(solution)/shard_map/cond/branch_1_fun/ppermute | solution.py:38
  34.4 23.4 %collective-permute-start.12 = (bf16[4,192,384]{2,1,0:T(8,128)(2,1)S(1)}, bf16[4,192,384]{2,1,0:T(8,128)(2,1)S(1)}, u32[]{:S(2)}, u32[]{:S(2)}) collective-permute-start(bf16[4,192,384]{2,1,0:T(8,128)(2,1)S(1)} %place.2.refs_0_), channel_id=1, source_target_pairs={{0,12},{16,28},{1,13},{17,29},{2,14},{18,30},{3,15},{19,31},{32,44... | collective-permute-start | bytes 1769480 | tf_op jit(solution)/shard_map/cond/branch_1_fun/ppermute | solution.py:38
  34.8 28.0 %collective-permute-start.13 = (bf16[4,192,384]{2,1,0:T(8,128)(2,1)S(1)}, bf16[4,192,384]{2,1,0:T(8,128)(2,1)S(1)}, u32[]{:S(2)}, u32[]{:S(2)}) collective-permute-start(bf16[4,192,384]{2,1,0:T(8,128)(2,1)S(1)} %place.2.refs_0_), channel_id=1, source_target_pairs={{0,8},{16,24},{1,9},{17,25},{2,10},{18,26},{3,11},{19,27},{32,40},... | collective-permute-start | bytes 1769480 | tf_op jit(solution)/shard_map/cond/branch_1_fun/ppermute | solution.py:38
  54.7 10.6 %collective-permute-start.15 = (bf16[2,64,1536]{2,1,0:T(8,128)(2,1)S(1)}, bf16[2,64,1536]{2,1,0:T(8,128)(2,1)S(1)}, u32[]{:S(2)}, u32[]{:S(2)}) collective-permute-start(bf16[2,64,1536]{2,1,0:T(8,128)(2,1)S(1)} %join.5.refs_0_), channel_id=1, source_target_pairs={{0,128},{16,144},{32,160},{48,176},{64,192},{80,208},{96,224},{112... | collective-permute-start | bytes 1179656 | tf_op jit(solution)/shard_map/cond/branch_1_fun/ppermute | solution.py:47
  80.0 80.0 %collective-permute-start.25 = (bf16[3072,384]{1,0:T(8,128)(2,1)}, bf16[3072,384]{1,0:T(8,128)(2,1)S(1)}, u32[]{:S(2)}, u32[]{:S(2)}) collective-permute-start(bf16[3072,384]{1,0:T(8,128)(2,1)} %copy-done.13), channel_id=1, source_target_pairs={{0,192},{16,208},{32,96},{48,112},{64,0},{80,16},{96,160},{112,176... | collective-permute-start | bytes 7077896 | tf_op jit(solution)/shard_map/ppermute | solution.py:52
  82.7 37.3 %collective-permute-start.21 = (bf16[2,384,384]{2,1,0:T(8,128)(2,1)S(1)}, bf16[2,384,384]{2,1,0:T(8,128)(2,1)}, u32[]{:S(2)}, u32[]{:S(2)}) collective-permute-start(bf16[2,384,384]{2,1,0:T(8,128)(2,1)S(1)} %pair.6), channel_id=1, source_target_pairs={{0,32},{16,48},{1,33},{17,49},{2,34},{18,50},{3,35},{19,51},{32,0}... | collective-permute-start | bytes 1769480 | tf_op jit(solution)/shard_map/ppermute | solution.py:38
  84.9 28.9 %collective-permute-start = (bf16[2,384,768]{2,1,0:T(8,128)(2,1)}, bf16[2,384,768]{2,1,0:T(8,128)(2,1)}, u32[]{:S(2)}, u32[]{:S(2)}) collective-permute-start(bf16[2,384,768]{2,1,0:T(8,128)(2,1)} %get-tuple-element.127), channel_id=1, source_target_pairs={{0,64},{16,80},{32,224},{48,240},{64,128},{80,144},{96,32},{112,48... | collective-permute-start | bytes 3538952 | tf_op jit(solution)/shard_map/cond/branch_1_fun/ppermute | solution.py:43
  86.4 33.6 %collective-permute-start.1 = (bf16[2,384,768]{2,1,0:T(8,128)(2,1)}, bf16[2,384,768]{2,1,0:T(8,128)(2,1)}, u32[]{:S(2)}, u32[]{:S(2)}) collective-permute-start(bf16[2,384,768]{2,1,0:T(8,128)(2,1)} %get-tuple-element.127), channel_id=1, source_target_pairs={{0,16},{16,0},{1,17},{17,1},{2,18},{18,2},{3,19},{19,3},{32,48},{4... | collective-permute-start | bytes 3538952 | tf_op jit(solution)/shard_map/cond/branch_1_fun/ppermute | solution.py:38
  120.0 21.8 %collective-permute-start.23 = (bf16[2,384,256]{2,1,0:T(8,128)(2,1)}, bf16[2,384,256]{2,1,0:T(8,128)(2,1)S(1)}, u32[]{:S(2)}, u32[]{:S(2)}) collective-permute-start(bf16[2,384,256]{2,1,0:T(8,128)(2,1)} %copy-done.2), channel_id=1, source_target_pairs={{0,32},{16,48},{1,33},{17,49},{2,34},{18,50},{3,35},{19,51},{32,0}... | collective-permute-start | bytes 1179656 | tf_op jit(solution)/shard_map/ppermute | solution.py:38
  122.7 16.8 %collective-permute-start.4 = (bf16[2,384,384]{2,1,0:T(8,128)(2,1)}, bf16[2,384,384]{2,1,0:T(8,128)(2,1)}, u32[]{:S(2)}, u32[]{:S(2)}) collective-permute-start(bf16[2,384,384]{2,1,0:T(8,128)(2,1)} %get-tuple-element.129), channel_id=1, source_target_pairs={{0,64},{16,80},{32,224},{48,240},{64,128},{80,144},{96,32},{112,48... | collective-permute-start | bytes 1769480 | tf_op jit(solution)/shard_map/cond/branch_1_fun/ppermute | solution.py:43
  122.7 16.8 %collective-permute-start.5 = (bf16[2,384,384]{2,1,0:T(8,128)(2,1)}, bf16[2,384,384]{2,1,0:T(8,128)(2,1)}, u32[]{:S(2)}, u32[]{:S(2)}) collective-permute-start(bf16[2,384,384]{2,1,0:T(8,128)(2,1)} %get-tuple-element.129), channel_id=1, source_target_pairs={{0,16},{16,0},{1,17},{17,1},{2,18},{18,2},{3,19},{19,3},{32,48},{4... | collective-permute-start | bytes 1769480 | tf_op jit(solution)/shard_map/cond/branch_1_fun/ppermute | solution.py:38
  142.6 17.3 %collective-permute-start.24 = (bf16[2,384,128]{2,1,0:T(8,128)(2,1)S(1)}, bf16[2,384,128]{2,1,0:T(8,128)(2,1)S(1)}, u32[]{:S(2)}, u32[]{:S(2)}) collective-permute-start(bf16[2,384,128]{2,1,0:T(8,128)(2,1)S(1)} %copy-done.4), channel_id=1, source_target_pairs={{0,32},{16,48},{1,33},{17,49},{2,34},{18,50},{3,35},{19,51},{32,0}... | collective-permute-start | bytes 589832 | tf_op jit(solution)/shard_map/ppermute | solution.py:38
  144.8 15.1 %collective-permute-start.10 = (bf16[3072,384]{1,0:T(8,128)(2,1)}, bf16[3072,384]{1,0:T(8,128)(2,1)}, u32[]{:S(2)}, u32[]{:S(2)}) collective-permute-start(bf16[3072,384]{1,0:T(8,128)(2,1)} %get-tuple-element.155), channel_id=1, source_target_pairs={{0,16},{16,0},{1,17},{17,1},{2,18},{18,2},{3,19},{19,3},{32,48},{4... | collective-permute-start | bytes 7077896 | tf_op jit(solution)/shard_map/cond/branch_1_fun/ppermute | solution.py:38
  144.8 13.1 %collective-permute-start.7 = (bf16[2,384,256]{2,1,0:T(8,128)(2,1)}, bf16[2,384,256]{2,1,0:T(8,128)(2,1)}, u32[]{:S(2)}, u32[]{:S(2)}) collective-permute-start(bf16[2,384,256]{2,1,0:T(8,128)(2,1)} %get-tuple-element.142), channel_id=1, source_target_pairs={{0,64},{16,80},{32,224},{48,240},{64,128},{80,144},{96,32},{112,48... | collective-permute-start | bytes 1179656 | tf_op jit(solution)/shard_map/cond/branch_1_fun/ppermute | solution.py:43
  145.1 12.8 %collective-permute-start.8 = (bf16[2,384,256]{2,1,0:T(8,128)(2,1)}, bf16[2,384,256]{2,1,0:T(8,128)(2,1)}, u32[]{:S(2)}, u32[]{:S(2)}) collective-permute-start(bf16[2,384,256]{2,1,0:T(8,128)(2,1)} %get-tuple-element.142), channel_id=1, source_target_pairs={{0,16},{16,0},{1,17},{17,1},{2,18},{18,2},{3,19},{19,3},{32,48},{4... | collective-permute-start | bytes 1179656 | tf_op jit(solution)/shard_map/cond/branch_1_fun/ppermute | solution.py:38
  160.7 15.4 %collective-permute-start.29 = (bf16[3072,384]{1,0:T(8,128)(2,1)S(1)}, bf16[3072,384]{1,0:T(8,128)(2,1)}, u32[]{:S(2)}, u32[]{:S(2)}) collective-permute-start(bf16[3072,384]{1,0:T(8,128)(2,1)S(1)} %collective-permute-done.25.refs_7_), channel_id=1, source_target_pairs={{0,16},{16,0},{1,17},{17,1},{2,18},{18,2},{3,19},{19,3},{32,48},{4... | collective-permute-start | bytes 7077896 | tf_op jit(solution)/shard_map/ppermute | solution.py:38
  160.9 9.0 %collective-permute-start.26 = (bf16[2,384,128]{2,1,0:T(8,128)(2,1)S(1)}, bf16[2,384,128]{2,1,0:T(8,128)(2,1)S(1)}, u32[]{:S(2)}, u32[]{:S(2)}) collective-permute-start(bf16[2,384,128]{2,1,0:T(8,128)(2,1)S(1)} %collective-permute-done.24.b0), channel_id=1, source_target_pairs={{0,64},{16,80},{32,224},{48,240},{64,128},{80,144},{96,32},{112,48... | collective-permute-start | bytes 589832 | tf_op jit(solution)/shard_map/ppermute | solution.py:43
  160.9 12.0 %collective-permute-start.27 = (bf16[2,384,128]{2,1,0:T(8,128)(2,1)S(1)}, bf16[2,384,128]{2,1,0:T(8,128)(2,1)S(1)}, u32[]{:S(2)}, u32[]{:S(2)}) collective-permute-start(bf16[2,384,128]{2,1,0:T(8,128)(2,1)S(1)} %collective-permute-done.24.b0), channel_id=1, source_target_pairs={{0,80},{16,64},{32,240},{48,224},{64,144},{80,128},{96,48},{112,32... | collective-permute-start | bytes 589832 | tf_op jit(solution)/shard_map/ppermute | solution.py:43
  161.0 11.9 %collective-permute-start.28 = (bf16[2,384,128]{2,1,0:T(8,128)(2,1)S(1)}, bf16[2,384,128]{2,1,0:T(8,128)(2,1)S(1)}, u32[]{:S(2)}, u32[]{:S(2)}) collective-permute-start(bf16[2,384,128]{2,1,0:T(8,128)(2,1)S(1)} %collective-permute-done.24.b0), channel_id=1, source_target_pairs={{0,16},{16,0},{1,17},{17,1},{2,18},{18,2},{3,19},{19,3},{32,48},{4... | collective-permute-start | bytes 589832 | tf_op jit(solution)/shard_map/ppermute | solution.py:38
  (34 other events, 181.0 us)

commit v3 on v2

--- a/solution.py
+++ b/solution.py
@@ -112,7 +112,7 @@
     )(where, *pieces)
 
 
-def attend_kernel(bias, q, k0, v0, a1, b0, b1, c0, c1, words, out):
+def attend_kernel(bias, q, k0, v0, a1, b0, b1, c0, c1, t0, t1, out):
     contract = (((1,), (1,)), ((), ()))
     sources = [(k0, v0)] + [(r.at[0], r.at[1]) for r in (a1, b0, b1, c0, c1)]
     for t in range(GT):
@@ -128,7 +128,8 @@
                 part = s[:, (j - low) * TILE : (j - low + 1) * TILE] * SCALE + bias[t, n * GT + j]
                 pieces.append(part)
                 peak = part if peak is None else jnp.maximum(peak, part)
-        s = lax.dot_general(qt, words[0], contract, preferred_element_type=jnp.float32) * SCALE
+        words = jnp.concatenate([t0[0], t1[0]], axis=0)
+        s = lax.dot_general(qt, words, contract, preferred_element_type=jnp.float32) * SCALE
         for j in range(TEXT // TILE):
             part = s[:, j * TILE : (j + 1) * TILE]
             pieces.append(part)
@@ -143,7 +144,7 @@
                 values = sources[n][1][low * TILE : high * TILE, :]
             else:
                 count = TEXT // TILE
-                values = words[1]
+                values = jnp.concatenate([t0[1], t1[1]], axis=0)
             weights = []
             for j in range(count):
                 e = jnp.exp2(pieces[at + j] - top)
@@ -159,7 +160,7 @@
 
 def attend(bias, q, k0, v0, beside, near, far, text, first, count):
     wide = pl.BlockSpec((ROWS, HD), lambda i: (0, first + i))
-    words = pl.BlockSpec((2, TEXT, HD), lambda i: (0, 0, first + i))
+    words = pl.BlockSpec((2, TEXT // 2, HD), lambda i: (0, 0, first + i))
     pack = pl.BlockSpec((2, ROWS, HD), lambda i: (0, 0, i))
     whole = pl.BlockSpec((2, ROWS, HD), lambda i: (0, 0, first + i))
     units = 48 * count
@@ -171,7 +172,7 @@
         + [wide] * 3
         + [whole]
         + [pack] * 4
-        + [words],
+        + [words] * 2,
         out_specs=pl.BlockSpec((ROWS, HD), lambda i: (0, i)),
         compiler_params=pltpu.CompilerParams(vmem_limit_bytes=14 * 1024 * 1024),
         cost_estimate=pl.CostEstimate(
@@ -180,7 +181,7 @@
             transcendentals=units * TILE * TILE,
         ),
         name="attend",
-    )(bias, q, k0, v0, beside, *near, *far, text)
+    )(bias, q, k0, v0, beside, *near, *far, *text)
 
 
 def project_kernel(*refs):
@@ -208,7 +209,7 @@
 
 
 def project(parts, order, weights, bias, gate, residual):
-    step = 512
+    step = 768
     panel = pl.BlockSpec((step, QUARTER), lambda i: (i, 0))
     return pl.pallas_call(
         project_kernel,
@@ -226,7 +227,7 @@
         scratch_shapes=[
             pltpu.VMEM((ROWS, HID), jnp.bfloat16),
         ],
-        compiler_params=pltpu.CompilerParams(vmem_limit_bytes=14 * 1024 * 1024),
+        compiler_params=pltpu.CompilerParams(vmem_limit_bytes=24 * 1024 * 1024),
         cost_estimate=pl.CostEstimate(
             flops=2 * ROWS * HID * D,
             bytes_accessed=2 * D * HID + 4 * ROWS * D,
@@ -338,11 +339,12 @@
     wx = across(wy)
 
     def first_stage(near0, text):
-        far0 = forward(near0)
-        text = join(text, swap(text, 1))
-        return far0, shift(near0, dc=1), shift(far0, dc=1), text
-
-    far0, near0_other, far0_other, text = stage(ready, first_stage, near0, text)
+        near0_other = shift(near0, dc=1)
+        far0, text = lax.optimization_barrier((forward(near0), swap(text, 1)))
+        return far0, near0_other, shift(far0, dc=1), text
+
+    far0, near0_other, far0_other, text_other = stage(ready, first_stage, near0, text)
+    text = (text, text_other)
 
     def second_stage(near1, near0, near0_other, far0, far0_other, text):
         part0 = attend_group(0, near0, near0_other, far0, text, far0_other)
@@ -356,15 +358,15 @@
         ready, second_stage, near1, near0, near0_other, far0, far0_other, text
     )
 
-    def third_stage(near2, near1, near1_other, far1, far1_other, text, wy):
+    def third_stage(near2, near1, near1_other, far1, far1_other, text, wy, wx):
         part1 = attend_group(1, near1, near1_other, far1, text, far1_other)
-        near2_other, wb = shift(near2, dc=1), shift(wy, dc=1)
+        near2_other, wb, wd = shift(near2, dc=1), shift(wy, dc=1), shift(wx, dc=1)
         far2, part1 = lax.optimization_barrier((forward(near2), part1))
-        return part1, near2_other, far2, shift(far2, dc=1), wb
-
-    pack3, near2, part0 = lax.optimization_barrier((packs[3], near2, part0))
+        return part1, near2_other, far2, shift(far2, dc=1), wb, wd
+
+    pack3, near2, part0, wx = lax.optimization_barrier((packs[3], near2, part0, wx))
     near3 = shift(pack3, dz=4)
-    part1, near2_other, far2, far2_other, wb = stage(
+    part1, near2_other, far2, far2_other, wb, wd = stage(
         ready,
         third_stage,
         near2,
@@ -374,9 +376,9 @@
         far1_other,
         text,
         wy,
-    )
-    near3, near2_other, wx = lax.optimization_barrier((near3, near2_other, wx))
-    wd = shift(wx, dc=1)
+        wx,
+    )
+    near3, near2_other = lax.optimization_barrier((near3, near2_other))
     part2 = attend_group(2, near2, near2_other, far2, text, far2_other)
     far3, far3_other, near3_other, part2 = lax.optimization_barrier(
         (forward(near3), forward(near3, flip=1), shift(near3, dc=1), part2)

time: 186 us -> 182 us (0.978)
  local copies, waits for them, and re-layouts: 8.11 us -> 6.04 us
    pallas_call x4 -> x3, Pallas kernels: 4.31 us -> 1.03 us  [join(): pl.pallas_call(join_kernel, out_shape=jax.ShapeDtypeStruct((2, rows, HID)...]
    ppermute x20, waiting for transfers between devices: 32.7 us -> 35.7 us  [shift(): return lax.ppermute(value, AXES, pairs)]
    ppermute x5, waiting for transfers between devices: 42.5 us -> 40.3 us  [forward(): return lax.ppermute(value, 'seq', pairs)]
    ppermute x4, waiting for transfers between devices: 14.1 us -> 12.1 us  [swap(): return lax.ppermute(value, 'seq', [(s, s ^ bit) for s in range(16)])]
    unnamed x57 -> x55, local copies, waits for them, and re-layouts: 7.06 us -> 5.08 us
    ppermute x20, starting transfers between devices: 24 us -> 25.9 us  [shift(): return lax.ppermute(value, AXES, pairs)]
  transfers between devices with their start and end apart: 30 -> 30, of which waited for: 14 -> 15; matrix products, arithmetic and copies ran while one was open for 1% -> 1% of each run, Pallas kernels for 22% -> 20%
where the time goes in v3:
time: 182 us; the launch traced here: 181 us
  waiting for transfers between devices  88.1 us (48%)
  Pallas kernels  48.1 us (26%)
  starting transfers between devices  36.7 us (20%)
  local copies, waits for them, and re-layouts  6.04 us (3%)
    ppermute x5, waiting for transfers between devices, forward(): return lax.ppermute(value, 'seq', pairs)  40.3 us
    ppermute x20, waiting for transfers between devices, shift(): return lax.ppermute(value, AXES, pairs)  35.7 us
    pallas_call x4, Pallas kernels, attend(): pl.pallas_call(attend_kernel, grid=(count,), out_shape=jax.ShapeDtypeStru...  28.1 us
    ppermute x20, starting transfers between devices, shift(): return lax.ppermute(value, AXES, pairs)  25.9 us
    ppermute x4, waiting for transfers between devices, swap(): return lax.ppermute(value, 'seq', [(s, s ^ bit) for s in range(16)])  12.1 us
    pallas_call x1, Pallas kernels, project(): pl.pallas_call(project_kernel, grid=(D // step,), out_shape=jax.ShapeDtyp...  8.22 us
    pallas_call x6, Pallas kernels, pair(): pl.pallas_call(pair_kernel, grid=(count,), out_shape=jax.ShapeDtypeStruct...  7.39 us
    ppermute x4, starting transfers between devices, swap(): return lax.ppermute(value, 'seq', [(s, s ^ bit) for s in range(16)])  6.06 us
  transfers between devices with their start and end apart: 30, of which 15 were waited for; matrix products, arithmetic and copies ran while one was open for 1% of the time, Pallas kernels for 20%

profile of v3, /device:TPU:72, one launch (start us, length us, event | category | flops | bytes accessed | tf_op | source)
XLA Modules:
  0.0 181.2 jit_solution(4476254793145108590)
XLA Ops:
  1.1 4.6 %collective-permute-start.19 = (bf16[192,384]{1,0:T(8,128)(2,1)S(1)}, bf16[192,384]{1,0:T(8,128)(2,1)S(1)}, u32[]{:S(2)}, u32[]{:S(2)}) collective-permute-start(bf16[192,384]{1,0:T(8,128)(2,1)S(1)} %dynamic-slice_bitcast_fusion), channel_id=1, source_target_pairs={{0,2},{16,18},{1,3},{17,19},{2,32},{18,48},{3,33},{19,49},{32,34},... | collective-permute-start | bytes 442376 | tf_op jit(solution)/shard_map/ppermute | solution.py:38
  10.8 4.4 %pair.9 = bf16[2,384,768]{2,1,0:T(8,128)(2,1)} custom-call(bf16[384,1536]{1,0:T(8,128)(2,1)} %bitcast.31, bf16[384,1536]{1,0:T(8,128)(2,1)} %bitcast.40), custom_call_target="tpu_custom_call" | custom-call | bytes 2359296 | tf_op jit(solution)/shard_map/pair/pallas_call | solution.py:82
  15.2 4.8 %collective-permute-done.20 = bf16[2,16,1536]{2,1,0:T(8,128)(2,1)S(1)} collective-permute-done((bf16[2,16,1536]{2,1,0:T(8,128)(2,1)S(1)}, bf16[2,16,1536]{2,1,0:T(8,128)(2,1)S(1)}, u32[]{:S(2)}, u32[]{:S(2)}) %collective-permute-start.20) | collective-permute-done | bytes 98336 | tf_op jit(solution)/shard_map/ppermute | solution.py:47
  21.4 5.8 %collective-permute-start.23 = (bf16[2,384,768]{2,1,0:T(8,128)(2,1)}, bf16[2,384,768]{2,1,0:T(8,128)(2,1)}, u32[]{:S(2)}, u32[]{:S(2)}) collective-permute-start(bf16[2,384,768]{2,1,0:T(8,128)(2,1)} %pair.9), channel_id=1, source_target_pairs={{0,32},{16,48},{1,33},{17,49},{2,34},{18,50},{3,35},{19,51},{32,0}... | collective-permute-start | bytes 3538952 | tf_op jit(solution)/shard_map/ppermute | solution.py:38
  32.3 34.5 %conditional.4 = (bf16[3072,384]{1,0:T(8,128)(2,1)}, bf16[2,128,1536]{2,1,0:T(8,128)(2,1)S(1)}) conditional(s32[]{:T(128)} %bitcast.12, () %tuple.57, (s32[]{:T(128)}, s32[]{:T(128)}, (), bf16[192,384]{1,0:T(8,128)(2,1)}, bf16[192,384]{1,0:T(8,128)(2,1)}, /*index=5*/bf16[192,384]{1,0:T(8,128)(2,1)}, bf16[192,384]{1,0:T(8,128)(2,1)}, ...), branch_computations={%region_1.2_spmd, %region_2.3_spmd} | conditional | flops 115 | bytes 18088396 | solution.py:242
  40.2 10.3 %collective-permute-done.12.refs_1_ = bf16[4,192,384]{2,1,0:T(8,128)(2,1)S(1)} collective-permute-done((bf16[4,192,384]{2,1,0:T(8,128)(2,1)S(1)}, bf16[4,192,384]{2,1,0:T(8,128)(2,1)S(1)}, u32[]{:S(2)}, u32[]{:S(2)}) %collective-permute-start.12) | collective-permute-done | bytes 589856 | tf_op jit(solution)/shard_map/cond/branch_1_fun/ppermute | solution.py:38
  52.0 4.2 %collective-permute-done.15.refs_1_ = bf16[2,32,1536]{2,1,0:T(8,128)(2,1)S(1)} collective-permute-done((bf16[2,32,1536]{2,1,0:T(8,128)(2,1)S(1)}, bf16[2,32,1536]{2,1,0:T(8,128)(2,1)S(1)}, u32[]{:S(2)}, u32[]{:S(2)}) %collective-permute-start.15) | collective-permute-done | bytes 196640 | tf_op jit(solution)/shard_map/cond/branch_1_fun/ppermute | solution.py:47
  56.2 3.1 %collective-permute-start.16 = (bf16[2,64,1536]{2,1,0:T(8,128)(2,1)S(1)}, bf16[2,64,1536]{2,1,0:T(8,128)(2,1)S(1)}, u32[]{:S(2)}, u32[]{:S(2)}) collective-permute-start(bf16[2,64,1536]{2,1,0:T(8,128)(2,1)S(1)} %join.4.refs_0_), channel_id=1, source_target_pairs={{0,128},{16,144},{32,160},{48,176},{64,192},{80,208},{96,224},{112... | collective-permute-start | bytes 1179656 | tf_op jit(solution)/shard_map/cond/branch_1_fun/ppermute | solution.py:47
  59.3 5.2 %collective-permute-done.13.refs_2_ = bf16[4,192,384]{2,1,0:T(8,128)(2,1)S(1)} collective-permute-done((bf16[4,192,384]{2,1,0:T(8,128)(2,1)S(1)}, bf16[4,192,384]{2,1,0:T(8,128)(2,1)S(1)}, u32[]{:S(2)}, u32[]{:S(2)}) %collective-permute-start.13) | collective-permute-done | bytes 589856 | tf_op jit(solution)/shard_map/cond/branch_1_fun/ppermute | solution.py:38
  66.8 12.6 %collective-permute-done.23 = bf16[2,384,768]{2,1,0:T(8,128)(2,1)} collective-permute-done((bf16[2,384,768]{2,1,0:T(8,128)(2,1)}, bf16[2,384,768]{2,1,0:T(8,128)(2,1)}, u32[]{:S(2)}, u32[]{:S(2)}) %collective-permute-start.23) | collective-permute-done | bytes 1179680 | tf_op jit(solution)/shard_map/ppermute | solution.py:38
  84.5 31.6 %conditional.5 = (bf16[2,384,768]{2,1,0:T(8,128)(2,1)}, bf16[2,384,768]{2,1,0:T(8,128)(2,1)}, bf16[2,384,768]{2,1,0:T(8,128)(2,1)}, bf16[2,128,1536]{2,1,0:T(8,128)(2,1)}) conditional(s32[]{:T(128)} %bitcast.12, () %tuple.60, (bf16[2,384,768]{2,1,0:T(8,128)(2,1)}, bf16[2,128,1536]{2,1,0:T(8,128)(2,1)S(1)}) %tuple.62), branch_computations={%region_3.4_spmd, %region_4.5_spmd} | conditional | bytes 17301696 | solution.py:242
  86.5 3.0 %collective-permute-done.1 = bf16[2,128,1536]{2,1,0:T(8,128)(2,1)} collective-permute-done((bf16[2,128,1536]{2,1,0:T(8,128)(2,1)S(1)}, bf16[2,128,1536]{2,1,0:T(8,128)(2,1)}, u32[]{:S(2)}, u32[]{:S(2)}) %collective-permute-start.1) | collective-permute-done | bytes 786464 | tf_op jit(solution)/shard_map/cond/branch_1_fun/ppermute | solution.py:47
  89.5 23.4 %collective-permute-done = bf16[2,384,768]{2,1,0:T(8,128)(2,1)} collective-permute-done((bf16[2,384,768]{2,1,0:T(8,128)(2,1)}, bf16[2,384,768]{2,1,0:T(8,128)(2,1)}, u32[]{:S(2)}, u32[]{:S(2)}) %collective-permute-start) | collective-permute-done | bytes 1179680 | tf_op jit(solution)/shard_map/cond/branch_1_fun/ppermute | solution.py:43
  112.9 3.2 %collective-permute-done.3 = bf16[2,384,768]{2,1,0:T(8,128)(2,1)} collective-permute-done((bf16[2,384,768]{2,1,0:T(8,128)(2,1)}, bf16[2,384,768]{2,1,0:T(8,128)(2,1)}, u32[]{:S(2)}, u32[]{:S(2)}) %collective-permute-start.3) | collective-permute-done | bytes 1179680 | tf_op jit(solution)/shard_map/cond/branch_1_fun/ppermute | solution.py:38
  118.6 19.6 %conditional.6 = (bf16[384,768]{1,0:T(8,128)(2,1)S(1)}, bf16[2,384,384]{2,1,0:T(8,128)(2,1)}, bf16[2,384,384]{2,1,0:T(8,128)(2,1)}, bf16[2,384,384]{2,1,0:T(8,128)(2,1)}) conditional(s32[]{:T(128)} %bitcast.12, () %tuple.64, (bf16[2,384,384]{2,1,0:T(8,128)(2,1)}, f32[3,18]{1,0:T(4,128)S(1)}, bf16[384,1536]{1,0:T(8,128)(2,1)}, ...), branch_computations={%region_5.6_spmd, %region_6.7_spmd} | conditional | flops 9663676416 | bytes 16122008 | solution.py:242
  118.7 12.9 %attend.4 = bf16[384,768]{1,0:T(8,128)(2,1)S(1)} custom-call(f32[3,18]{1,0:T(4,128)S(1)} %get-tuple-element.138.bias, bf16[384,1536]{1,0:T(8,128)(2,1)} %get-tuple-element.139.q, bf16[384,1536]{1,0:T(8,128)(2,1)S(1)} %get-tuple-element.140.k0, bf16[384,1536]{1,0:T(8,128)(2,1)} %get-tuple-element.141.v0, bf16[2,384,1536]{2,1,0:T(8,128)(2,1)} %get-tuple-element.142.a1, ...), custom_call_target="tpu_custom_call" | custom-call | flops 9663676416 | bytes 9043968 | tf_op jit(solution)/shard_map/cond/branch_1_fun/attend/pallas_call | solution.py:167
  131.6 4.3 %collective-permute-done.4 = bf16[2,384,384]{2,1,0:T(8,128)(2,1)} collective-permute-done((bf16[2,384,384]{2,1,0:T(8,128)(2,1)}, bf16[2,384,384]{2,1,0:T(8,128)(2,1)}, u32[]{:S(2)}, u32[]{:S(2)}) %collective-permute-start.4) | collective-permute-done | bytes 589856 | tf_op jit(solution)/shard_map/cond/branch_1_fun/ppermute | solution.py:43
  141.5 15.7 %conditional.7 = (bf16[384,384]{1,0:T(8,128)(2,1)S(1)}, bf16[2,384,256]{2,1,0:T(8,128)(2,1)}, bf16[2,384,256]{2,1,0:T(8,128)(2,1)}, bf16[2,384,256]{2,1,0:T(8,12...) conditional(s32[]{:T(128)} %bitcast.12, () %tuple.67, (bf16[2,384,256]{2,1,0:T(8,128)(2,1)}, ...), branch_computations={%region_7.8_spmd, %region_8.9_spmd} | conditional | flops 4831838208 | bytes 28115192 | solution.py:242
  142.4 7.1 %attend.5 = bf16[384,384]{1,0:T(8,128)(2,1)S(1)} custom-call(f32[3,18]{1,0:T(4,128)S(1)} %get-tuple-element.152.bias, bf16[384,1536]{1,0:T(8,128)(2,1)} %get-tuple-element.153.q, bf16[384,1536]{1,0:T(8,128)(2,1)S(1)} %get-tuple-element.154.k0, bf16[384,1536]{1,0:T(8,128)(2,1)} %get-tuple-element.155.v0, bf16[2,384,1536]{2,1,0:T(8,128)(2,1)} %get-tuple-element.156.a1, ...), custom_call_target="tpu_custom_call" | custom-call | flops 4831838208 | bytes 4521984 | tf_op jit(solution)/shard_map/cond/branch_1_fun/attend/pallas_call | solution.py:167
  149.5 5.6 %collective-permute-done.7 = bf16[2,384,256]{2,1,0:T(8,128)(2,1)} collective-permute-done((bf16[2,384,256]{2,1,0:T(8,128)(2,1)}, bf16[2,384,256]{2,1,0:T(8,128)(2,1)}, u32[]{:S(2)}, u32[]{:S(2)}) %collective-permute-start.7) | collective-permute-done | bytes 393248 | tf_op jit(solution)/shard_map/cond/branch_1_fun/ppermute | solution.py:43
  157.7 5.3 %attend.6.refs_2_ = bf16[384,256]{1,0:T(8,128)(2,1)S(1)} custom-call(f32[3,18]{1,0:T(4,128)S(1)} %and_select_fusion.2.bias, bf16[384,1536]{1,0:T(8,128)(2,1)} %bitcast.51, bf16[384,1536]{1,0:T(8,128)(2,1)S(1)} %bitcast.38, bf16[384,1536]{1,0:T(8,128)(2,1)} %bitcast.44, bf16[2,384,1536]{2,1,0:T(8,128)(2,1)} %collective-permute-done.21.a1, ...), custom_call_target="tpu_custom_call" | custom-call | flops 3221225472 | bytes 3014656 | tf_op jit(solution)/shard_map/attend/pallas_call | solution.py:167
  165.4 4.7 %collective-permute-done.27.c0 = bf16[2,384,128]{2,1,0:T(8,128)(2,1)S(1)} collective-permute-done((bf16[2,384,128]{2,1,0:T(8,128)(2,1)S(1)}, bf16[2,384,128]{2,1,0:T(8,128)(2,1)S(1)}, u32[]{:S(2)}, u32[]{:S(2)}) %collective-permute-start.27) | collective-permute-done | bytes 196640 | tf_op jit(solution)/shard_map/ppermute | solution.py:43
  170.1 2.9 %attend.7.refs_3_ = bf16[384,128]{1,0:T(8,128)(2,1)S(1)} custom-call(f32[3,18]{1,0:T(4,128)S(1)} %and_select_fusion.2.bias, bf16[384,1536]{1,0:T(8,128)(2,1)S(1)} %bitcast.52, bf16[384,1536]{1,0:T(8,128)(2,1)S(1)} %bitcast.39, bf16[384,1536]{1,0:T(8,128)(2,1)S(1)} %bitcast.48, bf16[2,384,1536]{2,1,0:T(8,128)(2,1)} %collective-permute-done.21.a1, ...), custom_call_target="tpu_custom_call" | custom-call | flops 1610612736 | bytes 1507328 | tf_op jit(solution)/shard_map/attend/pallas_call | solution.py:167
  173.0 8.2 %project.1 = bf16[384,3072]{1,0:T(8,128)(2,1)} custom-call(bf16[384,768]{1,0:T(8,128)(2,1)S(1)} %copy-done.17, bf16[384,384]{1,0:T(8,128)(2,1)S(1)} %get-tuple-element.250.refs_1_, bf16[384,256]{1,0:T(8,128)(2,1)S(1)} %attend.6.refs_2_, bf16[384,128]{1,0:T(8,128)(2,1)S(1)} %attend.7.refs_3_, s32[4]{0:T(128)S(1)} %pad_add_fusion.refs_4_, ...), custom_call_target="tpu_custom_call" | custom-call | flops 3623878656 | bytes 14155776 | tf_op jit(solution)/shard_map/project/pallas_call | solution.py:214
  (125 shorter events, 44.7 us)
Async XLA Ops:
  1.1 18.9 %collective-permute-start.19 = (bf16[192,384]{1,0:T(8,128)(2,1)S(1)}, bf16[192,384]{1,0:T(8,128)(2,1)S(1)}, u32[]{:S(2)}, u32[]{:S(2)}) collective-permute-start(bf16[192,384]{1,0:T(8,128)(2,1)S(1)} %dynamic-slice_bitcast_fusion), channel_id=1, source_target_pairs={{0,2},{16,18},{1,3},{17,19},{2,32},{18,48},{3,33},{19,49},{32,34},... | collective-permute-start | bytes 442376 | tf_op jit(solution)/shard_map/ppermute | solution.py:38
  5.7 14.3 %collective-permute-start.18 = (bf16[192,384]{1,0:T(8,128)(2,1)S(1)}, bf16[192,384]{1,0:T(8,128)(2,1)S(1)}, u32[]{:S(2)}, u32[]{:S(2)}) collective-permute-start(bf16[192,384]{1,0:T(8,128)(2,1)S(1)} %dynamic-slice_bitcast_fusion), channel_id=1, source_target_pairs={{0,35},{16,51},{1,0},{17,16},{2,1},{18,17},{3,2},{19,18},{32,3},{4... | collective-permute-start | bytes 442376 | tf_op jit(solution)/shard_map/ppermute | solution.py:38
  5.7 14.3 %collective-permute-start.17 = (bf16[192,384]{1,0:T(8,128)(2,1)S(1)}, bf16[192,384]{1,0:T(8,128)(2,1)S(1)}, u32[]{:S(2)}, u32[]{:S(2)}) collective-permute-start(bf16[192,384]{1,0:T(8,128)(2,1)S(1)} %dynamic-slice_bitcast_fusion), channel_id=1, source_target_pairs={{0,1},{16,17},{1,2},{17,18},{2,3},{18,19},{3,32},{19,48},{32,33},{... | collective-permute-start | bytes 442376 | tf_op jit(solution)/shard_map/ppermute | solution.py:38
  9.3 10.6 %collective-permute-start.20 = (bf16[2,16,1536]{2,1,0:T(8,128)(2,1)S(1)}, bf16[2,16,1536]{2,1,0:T(8,128)(2,1)S(1)}, u32[]{:S(2)}, u32[]{:S(2)}) collective-permute-start(bf16[2,16,1536]{2,1,0:T(8,128)(2,1)S(1)} %pair.10), channel_id=1, source_target_pairs={{0,32},{16,48},{32,0},{48,16},{64,96},{80,112},{96,64},{112,80},{1... | collective-permute-start | bytes 294920 | tf_op jit(solution)/shard_map/ppermute | solution.py:47
  21.3 11.0 %collective-permute-start.21 = (bf16[2,384,1536]{2,1,0:T(8,128)(2,1)S(1)}, bf16[2,384,1536]{2,1,0:T(8,128)(2,1)}, u32[]{:S(2)}, u32[]{:S(2)}) collective-permute-start(bf16[2,384,1536]{2,1,0:T(8,128)(2,1)S(1)} %pair.11), channel_id=1, source_target_pairs={{0,16},{16,0},{1,17},{17,1},{2,18},{18,2},{3,19},{19,3},{32,48},{4... | collective-permute-start | bytes 7077896 | tf_op jit(solution)/shard_map/ppermute | solution.py:38
  21.4 58.1 %collective-permute-start.23 = (bf16[2,384,768]{2,1,0:T(8,128)(2,1)}, bf16[2,384,768]{2,1,0:T(8,128)(2,1)}, u32[]{:S(2)}, u32[]{:S(2)}) collective-permute-start(bf16[2,384,768]{2,1,0:T(8,128)(2,1)} %pair.9), channel_id=1, source_target_pairs={{0,32},{16,48},{1,33},{17,49},{2,34},{18,50},{3,35},{19,51},{32,0}... | collective-permute-start | bytes 3538952 | tf_op jit(solution)/shard_map/ppermute | solution.py:38
  34.2 16.2 %collective-permute-start.12 = (bf16[4,192,384]{2,1,0:T(8,128)(2,1)S(1)}, bf16[4,192,384]{2,1,0:T(8,128)(2,1)S(1)}, u32[]{:S(2)}, u32[]{:S(2)}) collective-permute-start(bf16[4,192,384]{2,1,0:T(8,128)(2,1)S(1)} %place.2.refs_0_), channel_id=1, source_target_pairs={{0,4},{16,20},{1,5},{17,21},{2,6},{18,22},{3,7},{19,23},{32,36},{4... | collective-permute-start | bytes 1769480 | tf_op jit(solution)/shard_map/cond/branch_1_fun/ppermute | solution.py:38
  35.9 23.4 %collective-permute-start.14 = (bf16[4,192,384]{2,1,0:T(8,128)(2,1)S(1)}, bf16[4,192,384]{2,1,0:T(8,128)(2,1)S(1)}, u32[]{:S(2)}, u32[]{:S(2)}) collective-permute-start(bf16[4,192,384]{2,1,0:T(8,128)(2,1)S(1)} %place.2.refs_0_), channel_id=1, source_target_pairs={{0,8},{16,24},{1,9},{17,25},{2,10},{18,26},{3,11},{19,27},{32,40},... | collective-permute-start | bytes 1769480 | tf_op jit(solution)/shard_map/cond/branch_1_fun/ppermute | solution.py:38
  36.8 27.6 %collective-permute-start.13 = (bf16[4,192,384]{2,1,0:T(8,128)(2,1)S(1)}, bf16[4,192,384]{2,1,0:T(8,128)(2,1)S(1)}, u32[]{:S(2)}, u32[]{:S(2)}) collective-permute-start(bf16[4,192,384]{2,1,0:T(8,128)(2,1)S(1)} %place.2.refs_0_), channel_id=1, source_target_pairs={{0,12},{16,28},{1,13},{17,29},{2,14},{18,30},{3,15},{19,31},{32,44... | collective-permute-start | bytes 1769480 | tf_op jit(solution)/shard_map/cond/branch_1_fun/ppermute | solution.py:38
  56.2 10.6 %collective-permute-start.16 = (bf16[2,64,1536]{2,1,0:T(8,128)(2,1)S(1)}, bf16[2,64,1536]{2,1,0:T(8,128)(2,1)S(1)}, u32[]{:S(2)}, u32[]{:S(2)}) collective-permute-start(bf16[2,64,1536]{2,1,0:T(8,128)(2,1)S(1)} %join.4.refs_0_), channel_id=1, source_target_pairs={{0,128},{16,144},{32,160},{48,176},{64,192},{80,208},{96,224},{112... | collective-permute-start | bytes 1179656 | tf_op jit(solution)/shard_map/cond/branch_1_fun/ppermute | solution.py:47
  79.5 58.7 %collective-permute-start.25 = (bf16[3072,384]{1,0:T(8,128)(2,1)}, bf16[3072,384]{1,0:T(8,128)(2,1)}, u32[]{:S(2)}, u32[]{:S(2)}) collective-permute-start(bf16[3072,384]{1,0:T(8,128)(2,1)} %get-tuple-element.243.refs_5_), channel_id=1, source_target_pairs={{0,192},{16,208},{32,96},{48,112},{64,0},{80,16},{96,160},{112,176... | collective-permute-start | bytes 7077896 | tf_op jit(solution)/shard_map/ppermute | solution.py:52
  82.2 33.9 %collective-permute-start.22 = (bf16[2,384,384]{2,1,0:T(8,128)(2,1)S(1)}, bf16[2,384,384]{2,1,0:T(8,128)(2,1)}, u32[]{:S(2)}, u32[]{:S(2)}) collective-permute-start(bf16[2,384,384]{2,1,0:T(8,128)(2,1)S(1)} %pair.6), channel_id=1, source_target_pairs={{0,32},{16,48},{1,33},{17,49},{2,34},{18,50},{3,35},{19,51},{32,0}... | collective-permute-start | bytes 1769480 | tf_op jit(solution)/shard_map/ppermute | solution.py:38
  84.5 28.4 %collective-permute-start = (bf16[2,384,768]{2,1,0:T(8,128)(2,1)}, bf16[2,384,768]{2,1,0:T(8,128)(2,1)}, u32[]{:S(2)}, u32[]{:S(2)}) collective-permute-start(bf16[2,384,768]{2,1,0:T(8,128)(2,1)} %get-tuple-element.133), channel_id=1, source_target_pairs={{0,64},{16,80},{32,224},{48,240},{64,128},{80,144},{96,32},{112,48... | collective-permute-start | bytes 3538952 | tf_op jit(solution)/shard_map/cond/branch_1_fun/ppermute | solution.py:43
  86.0 26.9 %collective-permute-start.2 = (bf16[2,384,768]{2,1,0:T(8,128)(2,1)}, bf16[2,384,768]{2,1,0:T(8,128)(2,1)}, u32[]{:S(2)}, u32[]{:S(2)}) collective-permute-start(bf16[2,384,768]{2,1,0:T(8,128)(2,1)} %get-tuple-element.133), channel_id=1, source_target_pairs={{0,16},{16,0},{1,17},{17,1},{2,18},{18,2},{3,19},{19,3},{32,48},{4... | collective-permute-start | bytes 3538952 | tf_op jit(solution)/shard_map/cond/branch_1_fun/ppermute | solution.py:38
  116.1 22.1 %collective-permute-start.24 = (bf16[2,384,256]{2,1,0:T(8,128)(2,1)S(1)}, bf16[2,384,256]{2,1,0:T(8,128)(2,1)S(1)}, u32[]{:S(2)}, u32[]{:S(2)}) collective-permute-start(bf16[2,384,256]{2,1,0:T(8,128)(2,1)S(1)} %copy-done.3), channel_id=1, source_target_pairs={{0,32},{16,48},{1,33},{17,49},{2,34},{18,50},{3,35},{19,51},{32,0}... | collective-permute-start | bytes 1179656 | tf_op jit(solution)/shard_map/ppermute | solution.py:38
  118.6 17.3 %collective-permute-start.5 = (bf16[2,384,384]{2,1,0:T(8,128)(2,1)}, bf16[2,384,384]{2,1,0:T(8,128)(2,1)}, u32[]{:S(2)}, u32[]{:S(2)}) collective-permute-start(bf16[2,384,384]{2,1,0:T(8,128)(2,1)} %get-tuple-element.137), channel_id=1, source_target_pairs={{0,16},{16,0},{1,17},{17,1},{2,18},{18,2},{3,19},{19,3},{32,48},{4... | collective-permute-start | bytes 1769480 | tf_op jit(solution)/shard_map/cond/branch_1_fun/ppermute | solution.py:38
  118.6 17.3 %collective-permute-start.4 = (bf16[2,384,384]{2,1,0:T(8,128)(2,1)}, bf16[2,384,384]{2,1,0:T(8,128)(2,1)}, u32[]{:S(2)}, u32[]{:S(2)}) collective-permute-start(bf16[2,384,384]{2,1,0:T(8,128)(2,1)} %get-tuple-element.137), channel_id=1, source_target_pairs={{0,64},{16,80},{32,224},{48,240},{64,128},{80,144},{96,32},{112,48... | collective-permute-start | bytes 1769480 | tf_op jit(solution)/shard_map/cond/branch_1_fun/ppermute | solution.py:43
  139.2 18.0 %collective-permute-start.26 = (bf16[2,384,128]{2,1,0:T(8,128)(2,1)S(1)}, bf16[2,384,128]{2,1,0:T(8,128)(2,1)S(1)}, u32[]{:S(2)}, u32[]{:S(2)}) collective-permute-start(bf16[2,384,128]{2,1,0:T(8,128)(2,1)S(1)} %copy-done.5), channel_id=1, source_target_pairs={{0,32},{16,48},{1,33},{17,49},{2,34},{18,50},{3,35},{19,51},{32,0}... | collective-permute-start | bytes 589832 | tf_op jit(solution)/shard_map/ppermute | solution.py:38
  141.5 15.7 %collective-permute-start.10 = (bf16[3072,384]{1,0:T(8,128)(2,1)}, bf16[3072,384]{1,0:T(8,128)(2,1)}, u32[]{:S(2)}, u32[]{:S(2)}) collective-permute-start(bf16[3072,384]{1,0:T(8,128)(2,1)} %get-tuple-element.165), channel_id=1, source_target_pairs={{0,16},{16,0},{1,17},{17,1},{2,18},{18,2},{3,19},{19,3},{32,48},{4... | collective-permute-start | bytes 7077896 | tf_op jit(solution)/shard_map/cond/branch_1_fun/ppermute | solution.py:38
  141.5 15.6 %collective-permute-start.11 = (bf16[3072,384]{1,0:T(8,128)(2,1)}, bf16[3072,384]{1,0:T(8,128)(2,1)}, u32[]{:S(2)}, u32[]{:S(2)}) collective-permute-start(bf16[3072,384]{1,0:T(8,128)(2,1)} %get-tuple-element.166), channel_id=1, source_target_pairs={{0,16},{16,0},{1,17},{17,1},{2,18},{18,2},{3,19},{19,3},{32,48},{4... | collective-permute-start | bytes 7077896 | tf_op jit(solution)/shard_map/cond/branch_1_fun/ppermute | solution.py:38
  142.0 13.1 %collective-permute-start.8 = (bf16[2,384,256]{2,1,0:T(8,128)(2,1)}, bf16[2,384,256]{2,1,0:T(8,128)(2,1)}, u32[]{:S(2)}, u32[]{:S(2)}) collective-permute-start(bf16[2,384,256]{2,1,0:T(8,128)(2,1)} %get-tuple-element.151), channel_id=1, source_target_pairs={{0,16},{16,0},{1,17},{17,1},{2,18},{18,2},{3,19},{19,3},{32,48},{4... | collective-permute-start | bytes 1179656 | tf_op jit(solution)/shard_map/cond/branch_1_fun/ppermute | solution.py:38
  142.1 13.0 %collective-permute-start.7 = (bf16[2,384,256]{2,1,0:T(8,128)(2,1)}, bf16[2,384,256]{2,1,0:T(8,128)(2,1)}, u32[]{:S(2)}, u32[]{:S(2)}) collective-permute-start(bf16[2,384,256]{2,1,0:T(8,128)(2,1)} %get-tuple-element.151), channel_id=1, source_target_pairs={{0,64},{16,80},{32,224},{48,240},{64,128},{80,144},{96,32},{112,48... | collective-permute-start | bytes 1179656 | tf_op jit(solution)/shard_map/cond/branch_1_fun/ppermute | solution.py:43
  157.4 7.9 %collective-permute-start.28 = (bf16[2,384,128]{2,1,0:T(8,128)(2,1)S(1)}, bf16[2,384,128]{2,1,0:T(8,128)(2,1)S(1)}, u32[]{:S(2)}, u32[]{:S(2)}) collective-permute-start(bf16[2,384,128]{2,1,0:T(8,128)(2,1)S(1)} %collective-permute-done.26.b0), channel_id=1, source_target_pairs={{0,80},{16,64},{32,240},{48,224},{64,144},{80,128},{96,48},{112,32... | collective-permute-start | bytes 589832 | tf_op jit(solution)/shard_map/ppermute | solution.py:43
  157.4 12.6 %collective-permute-start.27 = (bf16[2,384,128]{2,1,0:T(8,128)(2,1)S(1)}, bf16[2,384,128]{2,1,0:T(8,128)(2,1)S(1)}, u32[]{:S(2)}, u32[]{:S(2)}) collective-permute-start(bf16[2,384,128]{2,1,0:T(8,128)(2,1)S(1)} %collective-permute-done.26.b0), channel_id=1, source_target_pairs={{0,64},{16,80},{32,224},{48,240},{64,128},{80,144},{96,32},{112,48... | collective-permute-start | bytes 589832 | tf_op jit(solution)/shard_map/ppermute | solution.py:43
  (33 other events, 290.0 us)

commit v4 on v3

--- a/solution.py
+++ b/solution.py
@@ -17,7 +17,7 @@
 PANEL = 192
 D = 3072
 TEXT = 256
-GROUPS = (6, 3, 2, 1)
+GROUPS = (5, 3, 3, 1)
 NEG = -1e30
 SCALE = HD**-0.5 * 1.4426950408889634
 AXES = ("seq", "fsdp")
@@ -335,28 +335,29 @@
     wy, text = stage(ready, weight_stage, piece, wz1, wz2, wz3, text, text_z)
     pack1, wy = lax.optimization_barrier((packs[1], wy))
     near1 = shift(pack1, dz=4)
-    near0, wy = lax.optimization_barrier((near0, wy))
+    near0, wy, pack2 = lax.optimization_barrier((near0, wy, packs[2]))
+    near2 = shift(pack2, dz=4)
     wx = across(wy)
 
-    def first_stage(near0, text):
-        near0_other = shift(near0, dc=1)
-        far0, text = lax.optimization_barrier((forward(near0), swap(text, 1)))
-        return far0, near0_other, shift(far0, dc=1), text
-
-    far0, near0_other, far0_other, text_other = stage(ready, first_stage, near0, text)
-    text = (text, text_other)
+    def first_stage(near0):
+        far0 = forward(near0)
+        return far0, shift(near0, dc=1), shift(far0, dc=1)
+
+    far0, near0_other, far0_other = stage(ready, first_stage, near0)
 
     def second_stage(near1, near0, near0_other, far0, far0_other, text):
-        part0 = attend_group(0, near0, near0_other, far0, text, far0_other)
+        text_other = swap(text, 1)
+        part0 = attend_group(0, near0, near0_other, far0, (text, text_other), far0_other)
         near1_other = shift(near1, dc=1)
         far1, part0 = lax.optimization_barrier((forward(near1), part0))
-        return part0, far1, near1_other, shift(far1, dc=1)
-
-    pack2, near1, far0_other = lax.optimization_barrier((packs[2], near1, far0_other))
-    near2 = shift(pack2, dz=4)
-    part0, far1, near1_other, far1_other = stage(
+        return part0, far1, near1_other, shift(far1, dc=1), text_other
+
+    near1, far0_other = lax.optimization_barrier((near1, far0_other))
+    part0, far1, near1_other, far1_other, text_other = stage(
         ready, second_stage, near1, near0, near0_other, far0, far0_other, text
     )
+
+    text = (text, text_other)
 
     def third_stage(near2, near1, near1_other, far1, far1_other, text, wy, wx):
         part1 = attend_group(1, near1, near1_other, far1, text, far1_other)

time: 182 us -> 189 us (1.038)
  the two profiles are of different devices: /device:TPU:72 before, /device:TPU:16 now
where the time goes in v4:
time: 189 us; the launch traced here: 188 us
  waiting for transfers between devices  91.3 us (48%)
  Pallas kernels  48.5 us (26%)
  starting transfers between devices  40.5 us (21%)
  local copies, waits for them, and re-layouts  6.04 us (3%)
    ppermute x20, waiting for transfers between devices, shift(): return lax.ppermute(value, AXES, pairs)  43.8 us
    ppermute x5, waiting for transfers between devices, forward(): return lax.ppermute(value, 'seq', pairs)  33.3 us
    pallas_call x4, Pallas kernels, attend(): pl.pallas_call(attend_kernel, grid=(count,), out_shape=jax.ShapeDtypeStru...  28.1 us
    ppermute x20, starting transfers between devices, shift(): return lax.ppermute(value, AXES, pairs)  21.3 us
    ppermute x4, waiting for transfers between devices, swap(): return lax.ppermute(value, 'seq', [(s, s ^ bit) for s in range(16)])  14.1 us
    ppermute x4, starting transfers between devices, swap(): return lax.ppermute(value, 'seq', [(s, s ^ bit) for s in range(16)])  9.63 us
    pallas_call x1, Pallas kernels, project(): pl.pallas_call(project_kernel, grid=(D // step,), out_shape=jax.ShapeDtyp...  8.23 us
    pallas_call x6, Pallas kernels, pair(): pl.pallas_call(pair_kernel, grid=(count,), out_shape=jax.ShapeDtypeStruct...  6.91 us
  transfers between devices with their start and end apart: 30, of which 13 were waited for; matrix products, arithmetic and copies ran while one was open for 1% of the time, Pallas kernels for 19%

profile of v4, /device:TPU:16, one launch (start us, length us, event | category | flops | bytes accessed | tf_op | source)
XLA Modules:
  0.0 188.5 jit_solution(4414400619643093182)
XLA Ops:
  1.1 3.3 %collective-permute-start.19 = (bf16[192,384]{1,0:T(8,128)(2,1)S(1)}, bf16[192,384]{1,0:T(8,128)(2,1)S(1)}, u32[]{:S(2)}, u32[]{:S(2)}) collective-permute-start(bf16[192,384]{1,0:T(8,128)(2,1)S(1)} %dynamic-slice_bitcast_fusion), channel_id=1, source_target_pairs={{0,2},{16,18},{1,3},{17,19},{2,32},{18,48},{3,33},{19,49},{32,34},... | collective-permute-start | bytes 442376 | tf_op jit(solution)/shard_map/ppermute | solution.py:38
  8.7 5.0 %collective-permute-start.20 = (bf16[2,16,1536]{2,1,0:T(8,128)(2,1)S(1)}, bf16[2,16,1536]{2,1,0:T(8,128)(2,1)S(1)}, u32[]{:S(2)}, u32[]{:S(2)}) collective-permute-start(bf16[2,16,1536]{2,1,0:T(8,128)(2,1)S(1)} %pair.10), channel_id=1, source_target_pairs={{0,32},{16,48},{32,0},{48,16},{64,96},{80,112},{96,64},{112,80},{1... | collective-permute-start | bytes 294920 | tf_op jit(solution)/shard_map/ppermute | solution.py:47
  13.8 3.8 %pair.9 = bf16[2,384,640]{2,1,0:T(8,128)(2,1)} custom-call(bf16[384,1536]{1,0:T(8,128)(2,1)} %bitcast.31, bf16[384,1536]{1,0:T(8,128)(2,1)} %bitcast.40), custom_call_target="tpu_custom_call" | custom-call | bytes 1966080 | tf_op jit(solution)/shard_map/pair/pallas_call | solution.py:82
  17.6 4.3 %collective-permute-done.20 = bf16[2,16,1536]{2,1,0:T(8,128)(2,1)S(1)} collective-permute-done((bf16[2,16,1536]{2,1,0:T(8,128)(2,1)S(1)}, bf16[2,16,1536]{2,1,0:T(8,128)(2,1)S(1)}, u32[]{:S(2)}, u32[]{:S(2)}) %collective-permute-start.20) | collective-permute-done | bytes 98336 | tf_op jit(solution)/shard_map/ppermute | solution.py:47
  31.1 46.7 %conditional.4 = (bf16[3072,384]{1,0:T(8,128)(2,1)}, bf16[2,128,1536]{2,1,0:T(8,128)(2,1)}) conditional(s32[]{:T(128)} %bitcast.12, () %tuple.56, (s32[]{:T(128)}, s32[]{:T(128)}, (), bf16[192,384]{1,0:T(8,128)(2,1)}, bf16[192,384]{1,0:T(8,128)(2,1)}, /*index=5*/bf16[192,384]{1,0:T(8,128)(2,1)}, bf16[192,384]{1,0:T(8,128)(2,1)}, ...), branch_computations={%region_1.2_spmd, %region_2.3_spmd} | conditional | flops 115 | bytes 18088396 | solution.py:242
  37.0 24.1 %collective-permute-done.12.refs_1_ = bf16[4,192,384]{2,1,0:T(8,128)(2,1)S(1)} collective-permute-done((bf16[4,192,384]{2,1,0:T(8,128)(2,1)S(1)}, bf16[4,192,384]{2,1,0:T(8,128)(2,1)S(1)}, u32[]{:S(2)}, u32[]{:S(2)}) %collective-permute-start.12) | collective-permute-done | bytes 589856 | tf_op jit(solution)/shard_map/cond/branch_1_fun/ppermute | solution.py:38
  62.6 4.2 %collective-permute-done.15.refs_1_ = bf16[2,32,1536]{2,1,0:T(8,128)(2,1)S(1)} collective-permute-done((bf16[2,32,1536]{2,1,0:T(8,128)(2,1)S(1)}, bf16[2,32,1536]{2,1,0:T(8,128)(2,1)S(1)}, u32[]{:S(2)}, u32[]{:S(2)}) %collective-permute-start.15) | collective-permute-done | bytes 196640 | tf_op jit(solution)/shard_map/cond/branch_1_fun/ppermute | solution.py:47
  66.8 3.1 %collective-permute-start.16 = (bf16[2,64,1536]{2,1,0:T(8,128)(2,1)S(1)}, bf16[2,64,1536]{2,1,0:T(8,128)(2,1)S(1)}, u32[]{:S(2)}, u32[]{:S(2)}) collective-permute-start(bf16[2,64,1536]{2,1,0:T(8,128)(2,1)S(1)} %join.4.refs_0_), channel_id=1, source_target_pairs={{0,128},{16,144},{32,160},{48,176},{64,192},{80,208},{96,224},{112... | collective-permute-start | bytes 1179656 | tf_op jit(solution)/shard_map/cond/branch_1_fun/ppermute | solution.py:47
  72.1 4.7 %collective-permute-done.16.refs_1_ = bf16[2,64,1536]{2,1,0:T(8,128)(2,1)S(1)} collective-permute-done((bf16[2,64,1536]{2,1,0:T(8,128)(2,1)S(1)}, bf16[2,64,1536]{2,1,0:T(8,128)(2,1)S(1)}, u32[]{:S(2)}, u32[]{:S(2)}) %collective-permute-start.16) | collective-permute-done | bytes 393248 | tf_op jit(solution)/shard_map/cond/branch_1_fun/ppermute | solution.py:47
  77.8 6.4 %collective-permute-start.25 = (bf16[3072,384]{1,0:T(8,128)(2,1)}, bf16[3072,384]{1,0:T(8,128)(2,1)}, u32[]{:S(2)}, u32[]{:S(2)}) collective-permute-start(bf16[3072,384]{1,0:T(8,128)(2,1)} %get-tuple-element.232.refs_5_), channel_id=1, source_target_pairs={{0,192},{16,208},{32,96},{48,112},{64,0},{80,16},{96,160},{112,176... | collective-permute-start | bytes 7077896 | tf_op jit(solution)/shard_map/ppermute | solution.py:52
  85.2 4.9 %collective-permute-start.23 = (bf16[2,384,384]{2,1,0:T(8,128)(2,1)S(1)}, bf16[2,384,384]{2,1,0:T(8,128)(2,1)}, u32[]{:S(2)}, u32[]{:S(2)}) collective-permute-start(bf16[2,384,384]{2,1,0:T(8,128)(2,1)S(1)} %pair.7), channel_id=1, source_target_pairs={{0,32},{16,48},{1,33},{17,49},{2,34},{18,50},{3,35},{19,51},{32,0}... | collective-permute-start | bytes 1769480 | tf_op jit(solution)/shard_map/ppermute | solution.py:38
  90.1 18.5 %conditional.5 = (bf16[2,384,640]{2,1,0:T(8,128)(2,1)}, bf16[2,384,640]{2,1,0:T(8,128)(2,1)}, bf16[2,384,640]{2,1,0:T(8,128)(2,1)}) conditional(s32[]{:T(128)} %bitcast.12, () %tuple.61, bf16[2,384,640]{2,1,0:T(8,128)(2,1)} %collective-permute-done.22), branch_computations={%region_3.4_spmd, %region_4.5_spmd} | conditional | bytes 11796624 | solution.py:242
  90.1 15.6 %collective-permute-done = bf16[2,384,640]{2,1,0:T(8,128)(2,1)} collective-permute-done((bf16[2,384,640]{2,1,0:T(8,128)(2,1)}, bf16[2,384,640]{2,1,0:T(8,128)(2,1)}, u32[]{:S(2)}, u32[]{:S(2)}) %collective-permute-start) | collective-permute-done | bytes 983072 | tf_op jit(solution)/shard_map/cond/branch_1_fun/ppermute | solution.py:43
  105.8 2.9 %collective-permute-done.2 = bf16[2,384,640]{2,1,0:T(8,128)(2,1)} collective-permute-done((bf16[2,384,640]{2,1,0:T(8,128)(2,1)}, bf16[2,384,640]{2,1,0:T(8,128)(2,1)}, u32[]{:S(2)}, u32[]{:S(2)}) %collective-permute-start.2) | collective-permute-done | bytes 983072 | tf_op jit(solution)/shard_map/cond/branch_1_fun/ppermute | solution.py:38
  108.7 12.1 %collective-permute-done.24 = bf16[2,384,384]{2,1,0:T(8,128)(2,1)S(1)} collective-permute-done((bf16[2,384,384]{2,1,0:T(8,128)(2,1)S(1)}, bf16[2,384,384]{2,1,0:T(8,128)(2,1)S(1)}, u32[]{:S(2)}, u32[]{:S(2)}) %collective-permute-start.24) | collective-permute-done | bytes 589856 | tf_op jit(solution)/shard_map/ppermute | solution.py:38
  121.6 19.7 %conditional.6 = (bf16[384,640]{1,0:T(8,128)(2,1)S(1)}, bf16[2,384,384]{2,1,0:T(8,128)(2,1)}, bf16[2,384,384]{2,1,0:T(8,128)(2,1)}, bf16[2,384,384]{2,1,0:T(8,128)(2,1)}, bf16[2,128,1536]{2,1,0:T(8,128)(2,1)}) conditional(s32[]{:T(128)} %bitcast.12, () %tuple.60, (bf16[2,384,384]{2,1,0:T(8,128)(2,1)}, bf16[2,128,1536]{2,1,0:T(8,128)(2,1)}, ...), branch_computations={%region_5.6_spmd, %region_6.7_spmd} | conditional | flops 8053063680 | bytes 17760456 | solution.py:242
  124.2 10.9 %attend.4 = bf16[384,640]{1,0:T(8,128)(2,1)S(1)} custom-call(f32[3,18]{1,0:T(4,128)S(1)} %get-tuple-element.129.bias, bf16[384,1536]{1,0:T(8,128)(2,1)} %get-tuple-element.130.q, bf16[384,1536]{1,0:T(8,128)(2,1)S(1)} %get-tuple-element.131.k0, bf16[384,1536]{1,0:T(8,128)(2,1)} %get-tuple-element.132.v0, bf16[2,384,1536]{2,1,0:T(8,128)(2,1)} %get-tuple-element.133.a1, ...), custom_call_target="tpu_custom_call" | custom-call | flops 8053063680 | bytes 7536640 | tf_op jit(solution)/shard_map/cond/branch_1_fun/attend/pallas_call | solution.py:167
  135.1 3.8 %collective-permute-done.3 = bf16[2,384,384]{2,1,0:T(8,128)(2,1)} collective-permute-done((bf16[2,384,384]{2,1,0:T(8,128)(2,1)}, bf16[2,384,384]{2,1,0:T(8,128)(2,1)}, u32[]{:S(2)}, u32[]{:S(2)}) %collective-permute-start.3) | collective-permute-done | bytes 589856 | tf_op jit(solution)/shard_map/cond/branch_1_fun/ppermute | solution.py:43
  144.0 20.5 %conditional.7 = (bf16[384,384]{1,0:T(8,128)(2,1)S(1)}, bf16[2,384,384]{2,1,0:T(8,128)(2,1)}, bf16[2,384,384]{2,1,0:T(8,128)(2,1)}, bf16[2,384,384]{2,1,0:T(8,12...) conditional(s32[]{:T(128)} %bitcast.12, () %tuple.65, (bf16[2,384,384]{2,1,0:T(8,128)(2,1)}, ...), branch_computations={%region_7.8_spmd, %region_8.9_spmd} | conditional | flops 4831838208 | bytes 30474488 | solution.py:242
  145.7 7.1 %attend.5 = bf16[384,384]{1,0:T(8,128)(2,1)S(1)} custom-call(f32[3,18]{1,0:T(4,128)S(1)} %get-tuple-element.142.bias, bf16[384,1536]{1,0:T(8,128)(2,1)} %get-tuple-element.143.q, bf16[384,1536]{1,0:T(8,128)(2,1)S(1)} %get-tuple-element.144.k0, bf16[384,1536]{1,0:T(8,128)(2,1)} %get-tuple-element.145.v0, bf16[2,384,1536]{2,1,0:T(8,128)(2,1)} %get-tuple-element.146.a1, ...), custom_call_target="tpu_custom_call" | custom-call | flops 4831838208 | bytes 4521984 | tf_op jit(solution)/shard_map/cond/branch_1_fun/attend/pallas_call | solution.py:167
  152.9 9.3 %collective-permute-done.7 = bf16[2,384,384]{2,1,0:T(8,128)(2,1)} collective-permute-done((bf16[2,384,384]{2,1,0:T(8,128)(2,1)}, bf16[2,384,384]{2,1,0:T(8,128)(2,1)}, u32[]{:S(2)}, u32[]{:S(2)}) %collective-permute-start.7) | collective-permute-done | bytes 589856 | tf_op jit(solution)/shard_map/cond/branch_1_fun/ppermute | solution.py:43
  165.4 7.2 %attend.6.refs_2_ = bf16[384,384]{1,0:T(8,128)(2,1)S(1)} custom-call(f32[3,18]{1,0:T(4,128)S(1)} %and_select_fusion.2.bias, bf16[384,1536]{1,0:T(8,128)(2,1)} %bitcast.51, bf16[384,1536]{1,0:T(8,128)(2,1)S(1)} %bitcast.38, bf16[384,1536]{1,0:T(8,128)(2,1)} %bitcast.44, bf16[2,384,1536]{2,1,0:T(8,128)(2,1)} %collective-permute-done.21.a1, ...), custom_call_target="tpu_custom_call" | custom-call | flops 4831838208 | bytes 4521984 | tf_op jit(solution)/shard_map/attend/pallas_call | solution.py:167
  172.7 4.6 %collective-permute-done.27.c0 = bf16[2,384,128]{2,1,0:T(8,128)(2,1)S(1)} collective-permute-done((bf16[2,384,128]{2,1,0:T(8,128)(2,1)S(1)}, bf16[2,384,128]{2,1,0:T(8,128)(2,1)S(1)}, u32[]{:S(2)}, u32[]{:S(2)}) %collective-permute-start.27) | collective-permute-done | bytes 196640 | tf_op jit(solution)/shard_map/ppermute | solution.py:43
  180.3 8.2 %project.1 = bf16[384,3072]{1,0:T(8,128)(2,1)} custom-call(bf16[384,640]{1,0:T(8,128)(2,1)S(1)} %get-tuple-element.233.refs_0_, bf16[384,384]{1,0:T(8,128)(2,1)S(1)} %get-tuple-element.240.refs_1_, bf16[384,384]{1,0:T(8,128)(2,1)S(1)} %attend.6.refs_2_, bf16[384,128]{1,0:T(8,128)(2,1)S(1)} %attend.7.refs_3_, s32[4]{0:T(128)S(1)} %pad_add_fusion.refs_4_, ...), custom_call_target="tpu_custom_call" | custom-call | flops 3623878656 | bytes 14155776 | tf_op jit(solution)/shard_map/project/pallas_call | solution.py:214
  (121 shorter events, 41.8 us)
Async XLA Ops:
  1.1 20.8 %collective-permute-start.19 = (bf16[192,384]{1,0:T(8,128)(2,1)S(1)}, bf16[192,384]{1,0:T(8,128)(2,1)S(1)}, u32[]{:S(2)}, u32[]{:S(2)}) collective-permute-start(bf16[192,384]{1,0:T(8,128)(2,1)S(1)} %dynamic-slice_bitcast_fusion), channel_id=1, source_target_pairs={{0,2},{16,18},{1,3},{17,19},{2,32},{18,48},{3,33},{19,49},{32,34},... | collective-permute-start | bytes 442376 | tf_op jit(solution)/shard_map/ppermute | solution.py:38
  4.4 17.5 %collective-permute-start.18 = (bf16[192,384]{1,0:T(8,128)(2,1)S(1)}, bf16[192,384]{1,0:T(8,128)(2,1)S(1)}, u32[]{:S(2)}, u32[]{:S(2)}) collective-permute-start(bf16[192,384]{1,0:T(8,128)(2,1)S(1)} %dynamic-slice_bitcast_fusion), channel_id=1, source_target_pairs={{0,35},{16,51},{1,0},{17,16},{2,1},{18,17},{3,2},{19,18},{32,3},{4... | collective-permute-start | bytes 442376 | tf_op jit(solution)/shard_map/ppermute | solution.py:38
  7.1 14.8 %collective-permute-start.17 = (bf16[192,384]{1,0:T(8,128)(2,1)S(1)}, bf16[192,384]{1,0:T(8,128)(2,1)S(1)}, u32[]{:S(2)}, u32[]{:S(2)}) collective-permute-start(bf16[192,384]{1,0:T(8,128)(2,1)S(1)} %dynamic-slice_bitcast_fusion), channel_id=1, source_target_pairs={{0,1},{16,17},{1,2},{17,18},{2,3},{18,19},{3,32},{19,48},{32,33},{... | collective-permute-start | bytes 442376 | tf_op jit(solution)/shard_map/ppermute | solution.py:38
  8.7 13.2 %collective-permute-start.20 = (bf16[2,16,1536]{2,1,0:T(8,128)(2,1)S(1)}, bf16[2,16,1536]{2,1,0:T(8,128)(2,1)S(1)}, u32[]{:S(2)}, u32[]{:S(2)}) collective-permute-start(bf16[2,16,1536]{2,1,0:T(8,128)(2,1)S(1)} %pair.10), channel_id=1, source_target_pairs={{0,32},{16,48},{32,0},{48,16},{64,96},{80,112},{96,64},{112,80},{1... | collective-permute-start | bytes 294920 | tf_op jit(solution)/shard_map/ppermute | solution.py:47
  23.4 54.4 %collective-permute-start.22 = (bf16[2,384,640]{2,1,0:T(8,128)(2,1)}, bf16[2,384,640]{2,1,0:T(8,128)(2,1)}, u32[]{:S(2)}, u32[]{:S(2)}) collective-permute-start(bf16[2,384,640]{2,1,0:T(8,128)(2,1)} %pair.9), channel_id=1, source_target_pairs={{0,32},{16,48},{1,33},{17,49},{2,34},{18,50},{3,35},{19,51},{32,0}... | collective-permute-start | bytes 2949128 | tf_op jit(solution)/shard_map/ppermute | solution.py:38
  33.0 28.1 %collective-permute-start.12 = (bf16[4,192,384]{2,1,0:T(8,128)(2,1)S(1)}, bf16[4,192,384]{2,1,0:T(8,128)(2,1)S(1)}, u32[]{:S(2)}, u32[]{:S(2)}) collective-permute-start(bf16[4,192,384]{2,1,0:T(8,128)(2,1)S(1)} %place.2.refs_0_), channel_id=1, source_target_pairs={{0,4},{16,20},{1,5},{17,21},{2,6},{18,22},{3,7},{19,23},{32,36},{4... | collective-permute-start | bytes 1769480 | tf_op jit(solution)/shard_map/cond/branch_1_fun/ppermute | solution.py:38
  34.4 35.6 %collective-permute-start.14 = (bf16[4,192,384]{2,1,0:T(8,128)(2,1)S(1)}, bf16[4,192,384]{2,1,0:T(8,128)(2,1)S(1)}, u32[]{:S(2)}, u32[]{:S(2)}) collective-permute-start(bf16[4,192,384]{2,1,0:T(8,128)(2,1)S(1)} %place.2.refs_0_), channel_id=1, source_target_pairs={{0,8},{16,24},{1,9},{17,25},{2,10},{18,26},{3,11},{19,27},{32,40},... | collective-permute-start | bytes 1769480 | tf_op jit(solution)/shard_map/cond/branch_1_fun/ppermute | solution.py:38
  35.0 34.9 %collective-permute-start.13 = (bf16[4,192,384]{2,1,0:T(8,128)(2,1)S(1)}, bf16[4,192,384]{2,1,0:T(8,128)(2,1)S(1)}, u32[]{:S(2)}, u32[]{:S(2)}) collective-permute-start(bf16[4,192,384]{2,1,0:T(8,128)(2,1)S(1)} %place.2.refs_0_), channel_id=1, source_target_pairs={{0,12},{16,28},{1,13},{17,29},{2,14},{18,30},{3,15},{19,31},{32,44... | collective-permute-start | bytes 1769480 | tf_op jit(solution)/shard_map/cond/branch_1_fun/ppermute | solution.py:38
  66.8 10.0 %collective-permute-start.16 = (bf16[2,64,1536]{2,1,0:T(8,128)(2,1)S(1)}, bf16[2,64,1536]{2,1,0:T(8,128)(2,1)S(1)}, u32[]{:S(2)}, u32[]{:S(2)}) collective-permute-start(bf16[2,64,1536]{2,1,0:T(8,128)(2,1)S(1)} %join.4.refs_0_), channel_id=1, source_target_pairs={{0,128},{16,144},{32,160},{48,176},{64,192},{80,208},{96,224},{112... | collective-permute-start | bytes 1179656 | tf_op jit(solution)/shard_map/cond/branch_1_fun/ppermute | solution.py:47
  77.8 63.5 %collective-permute-start.25 = (bf16[3072,384]{1,0:T(8,128)(2,1)}, bf16[3072,384]{1,0:T(8,128)(2,1)}, u32[]{:S(2)}, u32[]{:S(2)}) collective-permute-start(bf16[3072,384]{1,0:T(8,128)(2,1)} %get-tuple-element.232.refs_5_), channel_id=1, source_target_pairs={{0,192},{16,208},{32,96},{48,112},{64,0},{80,16},{96,160},{112,176... | collective-permute-start | bytes 7077896 | tf_op jit(solution)/shard_map/ppermute | solution.py:52
  84.2 36.6 %collective-permute-start.24 = (bf16[2,384,384]{2,1,0:T(8,128)(2,1)S(1)}, bf16[2,384,384]{2,1,0:T(8,128)(2,1)S(1)}, u32[]{:S(2)}, u32[]{:S(2)}) collective-permute-start(bf16[2,384,384]{2,1,0:T(8,128)(2,1)S(1)} %copy-done.3), channel_id=1, source_target_pairs={{0,32},{16,48},{1,33},{17,49},{2,34},{18,50},{3,35},{19,51},{32,0}... | collective-permute-start | bytes 1769480 | tf_op jit(solution)/shard_map/ppermute | solution.py:38
  85.2 56.0 %collective-permute-start.23 = (bf16[2,384,384]{2,1,0:T(8,128)(2,1)S(1)}, bf16[2,384,384]{2,1,0:T(8,128)(2,1)}, u32[]{:S(2)}, u32[]{:S(2)}) collective-permute-start(bf16[2,384,384]{2,1,0:T(8,128)(2,1)S(1)} %pair.7), channel_id=1, source_target_pairs={{0,32},{16,48},{1,33},{17,49},{2,34},{18,50},{3,35},{19,51},{32,0}... | collective-permute-start | bytes 1769480 | tf_op jit(solution)/shard_map/ppermute | solution.py:38
  90.1 15.6 %collective-permute-start = (bf16[2,384,640]{2,1,0:T(8,128)(2,1)}, bf16[2,384,640]{2,1,0:T(8,128)(2,1)}, u32[]{:S(2)}, u32[]{:S(2)}) collective-permute-start(bf16[2,384,640]{2,1,0:T(8,128)(2,1)} %param.3), channel_id=1, source_target_pairs={{0,64},{16,80},{32,224},{48,240},{64,128},{80,144},{96,32},{112,48... | collective-permute-start | bytes 2949128 | tf_op jit(solution)/shard_map/cond/branch_1_fun/ppermute | solution.py:43
  90.1 15.6 %collective-permute-start.1 = (bf16[2,384,640]{2,1,0:T(8,128)(2,1)}, bf16[2,384,640]{2,1,0:T(8,128)(2,1)}, u32[]{:S(2)}, u32[]{:S(2)}) collective-permute-start(bf16[2,384,640]{2,1,0:T(8,128)(2,1)} %param.3), channel_id=1, source_target_pairs={{0,16},{16,0},{1,17},{17,1},{2,18},{18,2},{3,19},{19,3},{32,48},{4... | collective-permute-start | bytes 2949128 | tf_op jit(solution)/shard_map/cond/branch_1_fun/ppermute | solution.py:38
  121.6 17.4 %collective-permute-start.5 = (bf16[2,384,384]{2,1,0:T(8,128)(2,1)}, bf16[2,384,384]{2,1,0:T(8,128)(2,1)}, u32[]{:S(2)}, u32[]{:S(2)}) collective-permute-start(bf16[2,384,384]{2,1,0:T(8,128)(2,1)} %get-tuple-element.128), channel_id=1, source_target_pairs={{0,16},{16,0},{1,17},{17,1},{2,18},{18,2},{3,19},{19,3},{32,48},{4... | collective-permute-start | bytes 1769480 | tf_op jit(solution)/shard_map/cond/branch_1_fun/ppermute | solution.py:38
  122.1 16.9 %collective-permute-start.3 = (bf16[2,384,384]{2,1,0:T(8,128)(2,1)}, bf16[2,384,384]{2,1,0:T(8,128)(2,1)}, u32[]{:S(2)}, u32[]{:S(2)}) collective-permute-start(bf16[2,384,384]{2,1,0:T(8,128)(2,1)} %get-tuple-element.128), channel_id=1, source_target_pairs={{0,64},{16,80},{32,224},{48,240},{64,128},{80,144},{96,32},{112,48... | collective-permute-start | bytes 1769480 | tf_op jit(solution)/shard_map/cond/branch_1_fun/ppermute | solution.py:43
  141.3 23.2 %collective-permute-start.26 = (bf16[2,384,128]{2,1,0:T(8,128)(2,1)S(1)}, bf16[2,384,128]{2,1,0:T(8,128)(2,1)S(1)}, u32[]{:S(2)}, u32[]{:S(2)}) collective-permute-start(bf16[2,384,128]{2,1,0:T(8,128)(2,1)S(1)} %copy-done.5), channel_id=1, source_target_pairs={{0,32},{16,48},{1,33},{17,49},{2,34},{18,50},{3,35},{19,51},{32,0}... | collective-permute-start | bytes 589832 | tf_op jit(solution)/shard_map/ppermute | solution.py:38
  144.0 20.5 %collective-permute-start.10 = (bf16[3072,384]{1,0:T(8,128)(2,1)}, bf16[3072,384]{1,0:T(8,128)(2,1)}, u32[]{:S(2)}, u32[]{:S(2)}) collective-permute-start(bf16[3072,384]{1,0:T(8,128)(2,1)} %get-tuple-element.155), channel_id=1, source_target_pairs={{0,16},{16,0},{1,17},{17,1},{2,18},{18,2},{3,19},{19,3},{32,48},{4... | collective-permute-start | bytes 7077896 | tf_op jit(solution)/shard_map/cond/branch_1_fun/ppermute | solution.py:38
  144.0 20.4 %collective-permute-start.11 = (bf16[3072,384]{1,0:T(8,128)(2,1)}, bf16[3072,384]{1,0:T(8,128)(2,1)}, u32[]{:S(2)}, u32[]{:S(2)}) collective-permute-start(bf16[3072,384]{1,0:T(8,128)(2,1)} %get-tuple-element.156), channel_id=1, source_target_pairs={{0,16},{16,0},{1,17},{17,1},{2,18},{18,2},{3,19},{19,3},{32,48},{4... | collective-permute-start | bytes 7077896 | tf_op jit(solution)/shard_map/cond/branch_1_fun/ppermute | solution.py:38
  144.5 17.6 %collective-permute-start.7 = (bf16[2,384,384]{2,1,0:T(8,128)(2,1)}, bf16[2,384,384]{2,1,0:T(8,128)(2,1)}, u32[]{:S(2)}, u32[]{:S(2)}) collective-permute-start(bf16[2,384,384]{2,1,0:T(8,128)(2,1)} %get-tuple-element.141), channel_id=1, source_target_pairs={{0,64},{16,80},{32,224},{48,240},{64,128},{80,144},{96,32},{112,48... | collective-permute-start | bytes 1769480 | tf_op jit(solution)/shard_map/cond/branch_1_fun/ppermute | solution.py:43
  145.7 16.4 %collective-permute-start.8 = (bf16[2,384,384]{2,1,0:T(8,128)(2,1)}, bf16[2,384,384]{2,1,0:T(8,128)(2,1)}, u32[]{:S(2)}, u32[]{:S(2)}) collective-permute-start(bf16[2,384,384]{2,1,0:T(8,128)(2,1)} %get-tuple-element.141), channel_id=1, source_target_pairs={{0,16},{16,0},{1,17},{17,1},{2,18},{18,2},{3,19},{19,3},{32,48},{4... | collective-permute-start | bytes 1769480 | tf_op jit(solution)/shard_map/cond/branch_1_fun/ppermute | solution.py:38
  164.5 8.2 %collective-permute-start.29 = (bf16[2,384,128]{2,1,0:T(8,128)(2,1)S(1)}, bf16[2,384,128]{2,1,0:T(8,128)(2,1)S(1)}, u32[]{:S(2)}, u32[]{:S(2)}) collective-permute-start(bf16[2,384,128]{2,1,0:T(8,128)(2,1)S(1)} %collective-permute-done.26.b0), channel_id=1, source_target_pairs={{0,16},{16,0},{1,17},{17,1},{2,18},{18,2},{3,19},{19,3},{32,48},{4... | collective-permute-start | bytes 589832 | tf_op jit(solution)/shard_map/ppermute | solution.py:38
  164.7 8.0 %collective-permute-start.28 = (bf16[2,384,128]{2,1,0:T(8,128)(2,1)S(1)}, bf16[2,384,128]{2,1,0:T(8,128)(2,1)S(1)}, u32[]{:S(2)}, u32[]{:S(2)}) collective-permute-start(bf16[2,384,128]{2,1,0:T(8,128)(2,1)S(1)} %collective-permute-done.26.b0), channel_id=1, source_target_pairs={{0,80},{16,64},{32,240},{48,224},{64,144},{80,128},{96,48},{112,32... | collective-permute-start | bytes 589832 | tf_op jit(solution)/shard_map/ppermute | solution.py:43
  164.7 12.6 %collective-permute-start.27 = (bf16[2,384,128]{2,1,0:T(8,128)(2,1)S(1)}, bf16[2,384,128]{2,1,0:T(8,128)(2,1)S(1)}, u32[]{:S(2)}, u32[]{:S(2)}) collective-permute-start(bf16[2,384,128]{2,1,0:T(8,128)(2,1)S(1)} %collective-permute-done.26.b0), channel_id=1, source_target_pairs={{0,64},{16,80},{32,224},{48,240},{64,128},{80,144},{96,32},{112,48... | collective-permute-start | bytes 589832 | tf_op jit(solution)/shard_map/ppermute | solution.py:43
  (31 other events, 273.1 us)

commit v5 on v3

--- a/solution.py
+++ b/solution.py
@@ -299,11 +299,11 @@
         out_weight.T, (0, (x % 2 * 2 + c) * QUARTER), (PANEL, QUARTER)
     )
     text_z = swap(text, 2)
-    pack0, keys, values, wz1, wz2, wz3, text_z = lax.optimization_barrier(
+    own = pair(k0, v0, 0, HEADS)
+    pack0, own, wz1, wz2, wz3, text_z = lax.optimization_barrier(
         (
             packs[0],
-            k0,
-            v0,
+            own,
             shift(piece, dz=1),
             shift(piece, dz=-1),
             shift(piece, dz=2),
@@ -314,7 +314,7 @@
         (
             packs[1:],
             bias,
-            shift(pair(keys, values, 0, HEADS), dc=1),
+            shift(own, dc=1),
             wz1,
             wz2,
             wz3,

time: 182 us -> 180 us (0.989)
  waiting for transfers between devices: 88.1 us -> 85.8 us
  transfers between devices with their start and end apart: 30 -> 30, of which waited for: 15 -> 15; matrix products, arithmetic and copies ran while one was open for 1% -> 1% of each run, Pallas kernels for 20% -> 21%
where the time goes in v5:
time: 180 us; the launch traced here: 179 us
  waiting for transfers between devices  85.8 us (48%)
  Pallas kernels  48.1 us (27%)
  starting transfers between devices  36.5 us (20%)
  local copies, waits for them, and re-layouts  6.71 us (4%)
    ppermute x5, waiting for transfers between devices, forward(): return lax.ppermute(value, 'seq', pairs)  39.7 us
    ppermute x20, waiting for transfers between devices, shift(): return lax.ppermute(value, AXES, pairs)  34.6 us
    pallas_call x4, Pallas kernels, attend(): pl.pallas_call(attend_kernel, grid=(count,), out_shape=jax.ShapeDtypeStru...  28.1 us
    ppermute x20, starting transfers between devices, shift(): return lax.ppermute(value, AXES, pairs)  25.6 us
    ppermute x4, waiting for transfers between devices, swap(): return lax.ppermute(value, 'seq', [(s, s ^ bit) for s in range(16)])  11.5 us
    pallas_call x1, Pallas kernels, project(): pl.pallas_call(project_kernel, grid=(D // step,), out_shape=jax.ShapeDtyp...  8.22 us
    pallas_call x6, Pallas kernels, pair(): pl.pallas_call(pair_kernel, grid=(count,), out_shape=jax.ShapeDtypeStruct...  7.39 us
    ppermute x4, starting transfers between devices, swap(): return lax.ppermute(value, 'seq', [(s, s ^ bit) for s in range(16)])  6.07 us
  transfers between devices with their start and end apart: 30, of which 15 were waited for; matrix products, arithmetic and copies ran while one was open for 1% of the time, Pallas kernels for 21%

profile of v5, /device:TPU:72, one launch (start us, length us, event | category | flops | bytes accessed | tf_op | source)
XLA Modules:
  0.0 179.3 jit_solution(11240299117583174663)
XLA Ops:
  1.1 4.6 %collective-permute-start.19 = (bf16[192,384]{1,0:T(8,128)(2,1)S(1)}, bf16[192,384]{1,0:T(8,128)(2,1)S(1)}, u32[]{:S(2)}, u32[]{:S(2)}) collective-permute-start(bf16[192,384]{1,0:T(8,128)(2,1)S(1)} %dynamic-slice_bitcast_fusion), channel_id=1, source_target_pairs={{0,2},{16,18},{1,3},{17,19},{2,32},{18,48},{3,33},{19,49},{32,34},... | collective-permute-start | bytes 442376 | tf_op jit(solution)/shard_map/ppermute | solution.py:38
  10.8 4.4 %pair.9 = bf16[2,384,768]{2,1,0:T(8,128)(2,1)} custom-call(bf16[384,1536]{1,0:T(8,128)(2,1)} %bitcast.31, bf16[384,1536]{1,0:T(8,128)(2,1)} %bitcast.40), custom_call_target="tpu_custom_call" | custom-call | bytes 2359296 | tf_op jit(solution)/shard_map/pair/pallas_call | solution.py:82
  16.4 3.5 %collective-permute-done.20 = bf16[2,16,1536]{2,1,0:T(8,128)(2,1)S(1)} collective-permute-done((bf16[2,16,1536]{2,1,0:T(8,128)(2,1)S(1)}, bf16[2,16,1536]{2,1,0:T(8,128)(2,1)S(1)}, u32[]{:S(2)}, u32[]{:S(2)}) %collective-permute-start.20) | collective-permute-done | bytes 98336 | tf_op jit(solution)/shard_map/ppermute | solution.py:47
  20.8 5.7 %collective-permute-start.23 = (bf16[2,384,768]{2,1,0:T(8,128)(2,1)}, bf16[2,384,768]{2,1,0:T(8,128)(2,1)}, u32[]{:S(2)}, u32[]{:S(2)}) collective-permute-start(bf16[2,384,768]{2,1,0:T(8,128)(2,1)} %pair.9), channel_id=1, source_target_pairs={{0,32},{16,48},{1,33},{17,49},{2,34},{18,50},{3,35},{19,51},{32,0}... | collective-permute-start | bytes 3538952 | tf_op jit(solution)/shard_map/ppermute | solution.py:38
  31.6 34.6 %conditional.4 = (bf16[3072,384]{1,0:T(8,128)(2,1)}, bf16[2,128,1536]{2,1,0:T(8,128)(2,1)S(1)}) conditional(s32[]{:T(128)} %bitcast.12, () %tuple.57, (s32[]{:T(128)}, s32[]{:T(128)}, (), bf16[192,384]{1,0:T(8,128)(2,1)}, bf16[192,384]{1,0:T(8,128)(2,1)}, /*index=5*/bf16[192,384]{1,0:T(8,128)(2,1)}, bf16[192,384]{1,0:T(8,128)(2,1)}, ...), branch_computations={%region_1.2_spmd, %region_2.3_spmd} | conditional | flops 115 | bytes 18088396 | solution.py:242
  39.5 10.4 %collective-permute-done.12.refs_1_ = bf16[4,192,384]{2,1,0:T(8,128)(2,1)S(1)} collective-permute-done((bf16[4,192,384]{2,1,0:T(8,128)(2,1)S(1)}, bf16[4,192,384]{2,1,0:T(8,128)(2,1)S(1)}, u32[]{:S(2)}, u32[]{:S(2)}) %collective-permute-start.12) | collective-permute-done | bytes 589856 | tf_op jit(solution)/shard_map/cond/branch_1_fun/ppermute | solution.py:38
  51.3 4.2 %collective-permute-done.15.refs_1_ = bf16[2,32,1536]{2,1,0:T(8,128)(2,1)S(1)} collective-permute-done((bf16[2,32,1536]{2,1,0:T(8,128)(2,1)S(1)}, bf16[2,32,1536]{2,1,0:T(8,128)(2,1)S(1)}, u32[]{:S(2)}, u32[]{:S(2)}) %collective-permute-start.15) | collective-permute-done | bytes 196640 | tf_op jit(solution)/shard_map/cond/branch_1_fun/ppermute | solution.py:47
  55.5 3.1 %collective-permute-start.16 = (bf16[2,64,1536]{2,1,0:T(8,128)(2,1)S(1)}, bf16[2,64,1536]{2,1,0:T(8,128)(2,1)S(1)}, u32[]{:S(2)}, u32[]{:S(2)}) collective-permute-start(bf16[2,64,1536]{2,1,0:T(8,128)(2,1)S(1)} %join.4.refs_0_), channel_id=1, source_target_pairs={{0,128},{16,144},{32,160},{48,176},{64,192},{80,208},{96,224},{112... | collective-permute-start | bytes 1179656 | tf_op jit(solution)/shard_map/cond/branch_1_fun/ppermute | solution.py:47
  58.7 4.6 %collective-permute-done.13.refs_2_ = bf16[4,192,384]{2,1,0:T(8,128)(2,1)S(1)} collective-permute-done((bf16[4,192,384]{2,1,0:T(8,128)(2,1)S(1)}, bf16[4,192,384]{2,1,0:T(8,128)(2,1)S(1)}, u32[]{:S(2)}, u32[]{:S(2)}) %collective-permute-start.13) | collective-permute-done | bytes 589856 | tf_op jit(solution)/shard_map/cond/branch_1_fun/ppermute | solution.py:38
  66.2 12.1 %collective-permute-done.23 = bf16[2,384,768]{2,1,0:T(8,128)(2,1)} collective-permute-done((bf16[2,384,768]{2,1,0:T(8,128)(2,1)}, bf16[2,384,768]{2,1,0:T(8,128)(2,1)}, u32[]{:S(2)}, u32[]{:S(2)}) %collective-permute-start.23) | collective-permute-done | bytes 1179680 | tf_op jit(solution)/shard_map/ppermute | solution.py:38
  83.1 31.1 %conditional.5 = (bf16[2,384,768]{2,1,0:T(8,128)(2,1)}, bf16[2,384,768]{2,1,0:T(8,128)(2,1)}, bf16[2,384,768]{2,1,0:T(8,128)(2,1)}, bf16[2,128,1536]{2,1,0:T(8,128)(2,1)}) conditional(s32[]{:T(128)} %bitcast.12, () %tuple.60, (bf16[2,384,768]{2,1,0:T(8,128)(2,1)}, bf16[2,128,1536]{2,1,0:T(8,128)(2,1)S(1)}) %tuple.62), branch_computations={%region_3.4_spmd, %region_4.5_spmd} | conditional | bytes 17301696 | solution.py:242
  85.1 3.0 %collective-permute-done.1 = bf16[2,128,1536]{2,1,0:T(8,128)(2,1)} collective-permute-done((bf16[2,128,1536]{2,1,0:T(8,128)(2,1)S(1)}, bf16[2,128,1536]{2,1,0:T(8,128)(2,1)}, u32[]{:S(2)}, u32[]{:S(2)}) %collective-permute-start.1) | collective-permute-done | bytes 786464 | tf_op jit(solution)/shard_map/cond/branch_1_fun/ppermute | solution.py:47
  88.1 22.9 %collective-permute-done = bf16[2,384,768]{2,1,0:T(8,128)(2,1)} collective-permute-done((bf16[2,384,768]{2,1,0:T(8,128)(2,1)}, bf16[2,384,768]{2,1,0:T(8,128)(2,1)}, u32[]{:S(2)}, u32[]{:S(2)}) %collective-permute-start) | collective-permute-done | bytes 1179680 | tf_op jit(solution)/shard_map/cond/branch_1_fun/ppermute | solution.py:43
  111.0 3.2 %collective-permute-done.3 = bf16[2,384,768]{2,1,0:T(8,128)(2,1)} collective-permute-done((bf16[2,384,768]{2,1,0:T(8,128)(2,1)}, bf16[2,384,768]{2,1,0:T(8,128)(2,1)}, u32[]{:S(2)}, u32[]{:S(2)}) %collective-permute-start.3) | collective-permute-done | bytes 1179680 | tf_op jit(solution)/shard_map/cond/branch_1_fun/ppermute | solution.py:38
  116.9 19.6 %conditional.6 = (bf16[384,768]{1,0:T(8,128)(2,1)S(1)}, bf16[2,384,384]{2,1,0:T(8,128)(2,1)}, bf16[2,384,384]{2,1,0:T(8,128)(2,1)}, bf16[2,384,384]{2,1,0:T(8,128)(2,1)}) conditional(s32[]{:T(128)} %bitcast.12, () %tuple.64, (bf16[2,384,384]{2,1,0:T(8,128)(2,1)}, f32[3,18]{1,0:T(4,128)S(1)}, bf16[384,1536]{1,0:T(8,128)(2,1)}, ...), branch_computations={%region_5.6_spmd, %region_6.7_spmd} | conditional | flops 9663676416 | bytes 16122008 | solution.py:242
  117.0 12.9 %attend.4 = bf16[384,768]{1,0:T(8,128)(2,1)S(1)} custom-call(f32[3,18]{1,0:T(4,128)S(1)} %get-tuple-element.138.bias, bf16[384,1536]{1,0:T(8,128)(2,1)} %get-tuple-element.139.q, bf16[384,1536]{1,0:T(8,128)(2,1)S(1)} %get-tuple-element.140.k0, bf16[384,1536]{1,0:T(8,128)(2,1)} %get-tuple-element.141.v0, bf16[2,384,1536]{2,1,0:T(8,128)(2,1)} %get-tuple-element.142.a1, ...), custom_call_target="tpu_custom_call" | custom-call | flops 9663676416 | bytes 9043968 | tf_op jit(solution)/shard_map/cond/branch_1_fun/attend/pallas_call | solution.py:167
  129.9 4.3 %collective-permute-done.4 = bf16[2,384,384]{2,1,0:T(8,128)(2,1)} collective-permute-done((bf16[2,384,384]{2,1,0:T(8,128)(2,1)}, bf16[2,384,384]{2,1,0:T(8,128)(2,1)}, u32[]{:S(2)}, u32[]{:S(2)}) %collective-permute-start.4) | collective-permute-done | bytes 589856 | tf_op jit(solution)/shard_map/cond/branch_1_fun/ppermute | solution.py:43
  139.6 15.7 %conditional.7 = (bf16[384,384]{1,0:T(8,128)(2,1)S(1)}, bf16[2,384,256]{2,1,0:T(8,128)(2,1)}, bf16[2,384,256]{2,1,0:T(8,128)(2,1)}, bf16[2,384,256]{2,1,0:T(8,12...) conditional(s32[]{:T(128)} %bitcast.12, () %tuple.67, (bf16[2,384,256]{2,1,0:T(8,128)(2,1)}, ...), branch_computations={%region_7.8_spmd, %region_8.9_spmd} | conditional | flops 4831838208 | bytes 28115192 | solution.py:242
  140.5 7.1 %attend.5 = bf16[384,384]{1,0:T(8,128)(2,1)S(1)} custom-call(f32[3,18]{1,0:T(4,128)S(1)} %get-tuple-element.152.bias, bf16[384,1536]{1,0:T(8,128)(2,1)} %get-tuple-element.153.q, bf16[384,1536]{1,0:T(8,128)(2,1)S(1)} %get-tuple-element.154.k0, bf16[384,1536]{1,0:T(8,128)(2,1)} %get-tuple-element.155.v0, bf16[2,384,1536]{2,1,0:T(8,128)(2,1)} %get-tuple-element.156.a1, ...), custom_call_target="tpu_custom_call" | custom-call | flops 4831838208 | bytes 4521984 | tf_op jit(solution)/shard_map/cond/branch_1_fun/attend/pallas_call | solution.py:167
  147.6 5.6 %collective-permute-done.7 = bf16[2,384,256]{2,1,0:T(8,128)(2,1)} collective-permute-done((bf16[2,384,256]{2,1,0:T(8,128)(2,1)}, bf16[2,384,256]{2,1,0:T(8,128)(2,1)}, u32[]{:S(2)}, u32[]{:S(2)}) %collective-permute-start.7) | collective-permute-done | bytes 393248 | tf_op jit(solution)/shard_map/cond/branch_1_fun/ppermute | solution.py:43
  155.8 5.3 %attend.6.refs_2_ = bf16[384,256]{1,0:T(8,128)(2,1)S(1)} custom-call(f32[3,18]{1,0:T(4,128)S(1)} %and_select_fusion.2.bias, bf16[384,1536]{1,0:T(8,128)(2,1)} %bitcast.51, bf16[384,1536]{1,0:T(8,128)(2,1)S(1)} %bitcast.38, bf16[384,1536]{1,0:T(8,128)(2,1)} %bitcast.44, bf16[2,384,1536]{2,1,0:T(8,128)(2,1)} %collective-permute-done.21.a1, ...), custom_call_target="tpu_custom_call" | custom-call | flops 3221225472 | bytes 3014656 | tf_op jit(solution)/shard_map/attend/pallas_call | solution.py:167
  163.5 4.7 %collective-permute-done.27.c0 = bf16[2,384,128]{2,1,0:T(8,128)(2,1)S(1)} collective-permute-done((bf16[2,384,128]{2,1,0:T(8,128)(2,1)S(1)}, bf16[2,384,128]{2,1,0:T(8,128)(2,1)S(1)}, u32[]{:S(2)}, u32[]{:S(2)}) %collective-permute-start.27) | collective-permute-done | bytes 196640 | tf_op jit(solution)/shard_map/ppermute | solution.py:43
  168.2 2.9 %attend.7.refs_3_ = bf16[384,128]{1,0:T(8,128)(2,1)S(1)} custom-call(f32[3,18]{1,0:T(4,128)S(1)} %and_select_fusion.2.bias, bf16[384,1536]{1,0:T(8,128)(2,1)S(1)} %bitcast.52, bf16[384,1536]{1,0:T(8,128)(2,1)S(1)} %bitcast.39, bf16[384,1536]{1,0:T(8,128)(2,1)S(1)} %bitcast.48, bf16[2,384,1536]{2,1,0:T(8,128)(2,1)} %collective-permute-done.21.a1, ...), custom_call_target="tpu_custom_call" | custom-call | flops 1610612736 | bytes 1507328 | tf_op jit(solution)/shard_map/attend/pallas_call | solution.py:167
  171.1 8.2 %project.1 = bf16[384,3072]{1,0:T(8,128)(2,1)} custom-call(bf16[384,768]{1,0:T(8,128)(2,1)S(1)} %copy-done.17, bf16[384,384]{1,0:T(8,128)(2,1)S(1)} %get-tuple-element.248.refs_1_, bf16[384,256]{1,0:T(8,128)(2,1)S(1)} %attend.6.refs_2_, bf16[384,128]{1,0:T(8,128)(2,1)S(1)} %attend.7.refs_3_, s32[4]{0:T(128)S(1)} %pad_add_fusion.refs_4_, ...), custom_call_target="tpu_custom_call" | custom-call | flops 3623878656 | bytes 14155776 | tf_op jit(solution)/shard_map/project/pallas_call | solution.py:214
  (125 shorter events, 45.8 us)
Async XLA Ops:
  1.1 18.9 %collective-permute-start.19 = (bf16[192,384]{1,0:T(8,128)(2,1)S(1)}, bf16[192,384]{1,0:T(8,128)(2,1)S(1)}, u32[]{:S(2)}, u32[]{:S(2)}) collective-permute-start(bf16[192,384]{1,0:T(8,128)(2,1)S(1)} %dynamic-slice_bitcast_fusion), channel_id=1, source_target_pairs={{0,2},{16,18},{1,3},{17,19},{2,32},{18,48},{3,33},{19,49},{32,34},... | collective-permute-start | bytes 442376 | tf_op jit(solution)/shard_map/ppermute | solution.py:38
  5.7 14.3 %collective-permute-start.18 = (bf16[192,384]{1,0:T(8,128)(2,1)S(1)}, bf16[192,384]{1,0:T(8,128)(2,1)S(1)}, u32[]{:S(2)}, u32[]{:S(2)}) collective-permute-start(bf16[192,384]{1,0:T(8,128)(2,1)S(1)} %dynamic-slice_bitcast_fusion), channel_id=1, source_target_pairs={{0,35},{16,51},{1,0},{17,16},{2,1},{18,17},{3,2},{19,18},{32,3},{4... | collective-permute-start | bytes 442376 | tf_op jit(solution)/shard_map/ppermute | solution.py:38
  5.7 14.3 %collective-permute-start.17 = (bf16[192,384]{1,0:T(8,128)(2,1)S(1)}, bf16[192,384]{1,0:T(8,128)(2,1)S(1)}, u32[]{:S(2)}, u32[]{:S(2)}) collective-permute-start(bf16[192,384]{1,0:T(8,128)(2,1)S(1)} %dynamic-slice_bitcast_fusion), channel_id=1, source_target_pairs={{0,1},{16,17},{1,2},{17,18},{2,3},{18,19},{3,32},{19,48},{32,33},{... | collective-permute-start | bytes 442376 | tf_op jit(solution)/shard_map/ppermute | solution.py:38
  9.3 10.6 %collective-permute-start.20 = (bf16[2,16,1536]{2,1,0:T(8,128)(2,1)S(1)}, bf16[2,16,1536]{2,1,0:T(8,128)(2,1)S(1)}, u32[]{:S(2)}, u32[]{:S(2)}) collective-permute-start(bf16[2,16,1536]{2,1,0:T(8,128)(2,1)S(1)} %pair.11), channel_id=1, source_target_pairs={{0,32},{16,48},{32,0},{48,16},{64,96},{80,112},{96,64},{112,80},{1... | collective-permute-start | bytes 294920 | tf_op jit(solution)/shard_map/ppermute | solution.py:47
  20.0 11.6 %collective-permute-start.21 = (bf16[2,384,1536]{2,1,0:T(8,128)(2,1)S(1)}, bf16[2,384,1536]{2,1,0:T(8,128)(2,1)}, u32[]{:S(2)}, u32[]{:S(2)}) collective-permute-start(bf16[2,384,1536]{2,1,0:T(8,128)(2,1)S(1)} %pair.10), channel_id=1, source_target_pairs={{0,16},{16,0},{1,17},{17,1},{2,18},{18,2},{3,19},{19,3},{32,48},{4... | collective-permute-start | bytes 7077896 | tf_op jit(solution)/shard_map/ppermute | solution.py:38
  20.8 57.5 %collective-permute-start.23 = (bf16[2,384,768]{2,1,0:T(8,128)(2,1)}, bf16[2,384,768]{2,1,0:T(8,128)(2,1)}, u32[]{:S(2)}, u32[]{:S(2)}) collective-permute-start(bf16[2,384,768]{2,1,0:T(8,128)(2,1)} %pair.9), channel_id=1, source_target_pairs={{0,32},{16,48},{1,33},{17,49},{2,34},{18,50},{3,35},{19,51},{32,0}... | collective-permute-start | bytes 3538952 | tf_op jit(solution)/shard_map/ppermute | solution.py:38
  33.5 16.3 %collective-permute-start.12 = (bf16[4,192,384]{2,1,0:T(8,128)(2,1)S(1)}, bf16[4,192,384]{2,1,0:T(8,128)(2,1)S(1)}, u32[]{:S(2)}, u32[]{:S(2)}) collective-permute-start(bf16[4,192,384]{2,1,0:T(8,128)(2,1)S(1)} %place.2.refs_0_), channel_id=1, source_target_pairs={{0,4},{16,20},{1,5},{17,21},{2,6},{18,22},{3,7},{19,23},{32,36},{4... | collective-permute-start | bytes 1769480 | tf_op jit(solution)/shard_map/cond/branch_1_fun/ppermute | solution.py:38
  35.2 23.5 %collective-permute-start.14 = (bf16[4,192,384]{2,1,0:T(8,128)(2,1)S(1)}, bf16[4,192,384]{2,1,0:T(8,128)(2,1)S(1)}, u32[]{:S(2)}, u32[]{:S(2)}) collective-permute-start(bf16[4,192,384]{2,1,0:T(8,128)(2,1)S(1)} %place.2.refs_0_), channel_id=1, source_target_pairs={{0,8},{16,24},{1,9},{17,25},{2,10},{18,26},{3,11},{19,27},{32,40},... | collective-permute-start | bytes 1769480 | tf_op jit(solution)/shard_map/cond/branch_1_fun/ppermute | solution.py:38
  36.1 27.1 %collective-permute-start.13 = (bf16[4,192,384]{2,1,0:T(8,128)(2,1)S(1)}, bf16[4,192,384]{2,1,0:T(8,128)(2,1)S(1)}, u32[]{:S(2)}, u32[]{:S(2)}) collective-permute-start(bf16[4,192,384]{2,1,0:T(8,128)(2,1)S(1)} %place.2.refs_0_), channel_id=1, source_target_pairs={{0,12},{16,28},{1,13},{17,29},{2,14},{18,30},{3,15},{19,31},{32,44... | collective-permute-start | bytes 1769480 | tf_op jit(solution)/shard_map/cond/branch_1_fun/ppermute | solution.py:38
  55.5 10.6 %collective-permute-start.16 = (bf16[2,64,1536]{2,1,0:T(8,128)(2,1)S(1)}, bf16[2,64,1536]{2,1,0:T(8,128)(2,1)S(1)}, u32[]{:S(2)}, u32[]{:S(2)}) collective-permute-start(bf16[2,64,1536]{2,1,0:T(8,128)(2,1)S(1)} %join.4.refs_0_), channel_id=1, source_target_pairs={{0,128},{16,144},{32,160},{48,176},{64,192},{80,208},{96,224},{112... | collective-permute-start | bytes 1179656 | tf_op jit(solution)/shard_map/cond/branch_1_fun/ppermute | solution.py:47
  78.3 58.2 %collective-permute-start.25 = (bf16[3072,384]{1,0:T(8,128)(2,1)}, bf16[3072,384]{1,0:T(8,128)(2,1)}, u32[]{:S(2)}, u32[]{:S(2)}) collective-permute-start(bf16[3072,384]{1,0:T(8,128)(2,1)} %get-tuple-element.241.refs_5_), channel_id=1, source_target_pairs={{0,192},{16,208},{32,96},{48,112},{64,0},{80,16},{96,160},{112,176... | collective-permute-start | bytes 7077896 | tf_op jit(solution)/shard_map/ppermute | solution.py:52
  81.0 33.2 %collective-permute-start.22 = (bf16[2,384,384]{2,1,0:T(8,128)(2,1)S(1)}, bf16[2,384,384]{2,1,0:T(8,128)(2,1)}, u32[]{:S(2)}, u32[]{:S(2)}) collective-permute-start(bf16[2,384,384]{2,1,0:T(8,128)(2,1)S(1)} %pair.6), channel_id=1, source_target_pairs={{0,32},{16,48},{1,33},{17,49},{2,34},{18,50},{3,35},{19,51},{32,0}... | collective-permute-start | bytes 1769480 | tf_op jit(solution)/shard_map/ppermute | solution.py:38
  83.1 27.9 %collective-permute-start = (bf16[2,384,768]{2,1,0:T(8,128)(2,1)}, bf16[2,384,768]{2,1,0:T(8,128)(2,1)}, u32[]{:S(2)}, u32[]{:S(2)}) collective-permute-start(bf16[2,384,768]{2,1,0:T(8,128)(2,1)} %get-tuple-element.133), channel_id=1, source_target_pairs={{0,64},{16,80},{32,224},{48,240},{64,128},{80,144},{96,32},{112,48... | collective-permute-start | bytes 3538952 | tf_op jit(solution)/shard_map/cond/branch_1_fun/ppermute | solution.py:43
  84.6 26.4 %collective-permute-start.2 = (bf16[2,384,768]{2,1,0:T(8,128)(2,1)}, bf16[2,384,768]{2,1,0:T(8,128)(2,1)}, u32[]{:S(2)}, u32[]{:S(2)}) collective-permute-start(bf16[2,384,768]{2,1,0:T(8,128)(2,1)} %get-tuple-element.133), channel_id=1, source_target_pairs={{0,16},{16,0},{1,17},{17,1},{2,18},{18,2},{3,19},{19,3},{32,48},{4... | collective-permute-start | bytes 3538952 | tf_op jit(solution)/shard_map/cond/branch_1_fun/ppermute | solution.py:38
  114.2 22.3 %collective-permute-start.24 = (bf16[2,384,256]{2,1,0:T(8,128)(2,1)S(1)}, bf16[2,384,256]{2,1,0:T(8,128)(2,1)S(1)}, u32[]{:S(2)}, u32[]{:S(2)}) collective-permute-start(bf16[2,384,256]{2,1,0:T(8,128)(2,1)S(1)} %copy-done.3), channel_id=1, source_target_pairs={{0,32},{16,48},{1,33},{17,49},{2,34},{18,50},{3,35},{19,51},{32,0}... | collective-permute-start | bytes 1179656 | tf_op jit(solution)/shard_map/ppermute | solution.py:38
  116.9 17.3 %collective-permute-start.5 = (bf16[2,384,384]{2,1,0:T(8,128)(2,1)}, bf16[2,384,384]{2,1,0:T(8,128)(2,1)}, u32[]{:S(2)}, u32[]{:S(2)}) collective-permute-start(bf16[2,384,384]{2,1,0:T(8,128)(2,1)} %get-tuple-element.137), channel_id=1, source_target_pairs={{0,16},{16,0},{1,17},{17,1},{2,18},{18,2},{3,19},{19,3},{32,48},{4... | collective-permute-start | bytes 1769480 | tf_op jit(solution)/shard_map/cond/branch_1_fun/ppermute | solution.py:38
  116.9 17.3 %collective-permute-start.4 = (bf16[2,384,384]{2,1,0:T(8,128)(2,1)}, bf16[2,384,384]{2,1,0:T(8,128)(2,1)}, u32[]{:S(2)}, u32[]{:S(2)}) collective-permute-start(bf16[2,384,384]{2,1,0:T(8,128)(2,1)} %get-tuple-element.137), channel_id=1, source_target_pairs={{0,64},{16,80},{32,224},{48,240},{64,128},{80,144},{96,32},{112,48... | collective-permute-start | bytes 1769480 | tf_op jit(solution)/shard_map/cond/branch_1_fun/ppermute | solution.py:43
  137.4 17.9 %collective-permute-start.26 = (bf16[2,384,128]{2,1,0:T(8,128)(2,1)S(1)}, bf16[2,384,128]{2,1,0:T(8,128)(2,1)S(1)}, u32[]{:S(2)}, u32[]{:S(2)}) collective-permute-start(bf16[2,384,128]{2,1,0:T(8,128)(2,1)S(1)} %copy-done.5), channel_id=1, source_target_pairs={{0,32},{16,48},{1,33},{17,49},{2,34},{18,50},{3,35},{19,51},{32,0}... | collective-permute-start | bytes 589832 | tf_op jit(solution)/shard_map/ppermute | solution.py:38
  139.6 15.7 %collective-permute-start.10 = (bf16[3072,384]{1,0:T(8,128)(2,1)}, bf16[3072,384]{1,0:T(8,128)(2,1)}, u32[]{:S(2)}, u32[]{:S(2)}) collective-permute-start(bf16[3072,384]{1,0:T(8,128)(2,1)} %get-tuple-element.165), channel_id=1, source_target_pairs={{0,16},{16,0},{1,17},{17,1},{2,18},{18,2},{3,19},{19,3},{32,48},{4... | collective-permute-start | bytes 7077896 | tf_op jit(solution)/shard_map/cond/branch_1_fun/ppermute | solution.py:38
  139.7 15.6 %collective-permute-start.11 = (bf16[3072,384]{1,0:T(8,128)(2,1)}, bf16[3072,384]{1,0:T(8,128)(2,1)}, u32[]{:S(2)}, u32[]{:S(2)}) collective-permute-start(bf16[3072,384]{1,0:T(8,128)(2,1)} %get-tuple-element.166), channel_id=1, source_target_pairs={{0,16},{16,0},{1,17},{17,1},{2,18},{18,2},{3,19},{19,3},{32,48},{4... | collective-permute-start | bytes 7077896 | tf_op jit(solution)/shard_map/cond/branch_1_fun/ppermute | solution.py:38
  140.2 13.1 %collective-permute-start.8 = (bf16[2,384,256]{2,1,0:T(8,128)(2,1)}, bf16[2,384,256]{2,1,0:T(8,128)(2,1)}, u32[]{:S(2)}, u32[]{:S(2)}) collective-permute-start(bf16[2,384,256]{2,1,0:T(8,128)(2,1)} %get-tuple-element.151), channel_id=1, source_target_pairs={{0,16},{16,0},{1,17},{17,1},{2,18},{18,2},{3,19},{19,3},{32,48},{4... | collective-permute-start | bytes 1179656 | tf_op jit(solution)/shard_map/cond/branch_1_fun/ppermute | solution.py:38
  140.3 13.0 %collective-permute-start.7 = (bf16[2,384,256]{2,1,0:T(8,128)(2,1)}, bf16[2,384,256]{2,1,0:T(8,128)(2,1)}, u32[]{:S(2)}, u32[]{:S(2)}) collective-permute-start(bf16[2,384,256]{2,1,0:T(8,128)(2,1)} %get-tuple-element.151), channel_id=1, source_target_pairs={{0,64},{16,80},{32,224},{48,240},{64,128},{80,144},{96,32},{112,48... | collective-permute-start | bytes 1179656 | tf_op jit(solution)/shard_map/cond/branch_1_fun/ppermute | solution.py:43
  155.5 7.9 %collective-permute-start.28 = (bf16[2,384,128]{2,1,0:T(8,128)(2,1)S(1)}, bf16[2,384,128]{2,1,0:T(8,128)(2,1)S(1)}, u32[]{:S(2)}, u32[]{:S(2)}) collective-permute-start(bf16[2,384,128]{2,1,0:T(8,128)(2,1)S(1)} %collective-permute-done.26.b0), channel_id=1, source_target_pairs={{0,80},{16,64},{32,240},{48,224},{64,144},{80,128},{96,48},{112,32... | collective-permute-start | bytes 589832 | tf_op jit(solution)/shard_map/ppermute | solution.py:43
  155.5 12.6 %collective-permute-start.27 = (bf16[2,384,128]{2,1,0:T(8,128)(2,1)S(1)}, bf16[2,384,128]{2,1,0:T(8,128)(2,1)S(1)}, u32[]{:S(2)}, u32[]{:S(2)}) collective-permute-start(bf16[2,384,128]{2,1,0:T(8,128)(2,1)S(1)} %collective-permute-done.26.b0), channel_id=1, source_target_pairs={{0,64},{16,80},{32,224},{48,240},{64,128},{80,144},{96,32},{112,48... | collective-permute-start | bytes 589832 | tf_op jit(solution)/shard_map/ppermute | solution.py:43
  (33 other events, 268.9 us)
